TPU v7x, 32 devices: a whole 2x2x4 slice. The times are simulated.
32 devices in a mesh: grp: 2 (over x), probe: 8 (over z, y), beam: 2 (over core).
Axes of the slice: x: 2, y: 2, z: 4, core: 2. Of those that a mesh axis runs over, the one named last changes fastest.
Arguments:
- smatrix: bfloat16 [8192, 8, 512], P(('grp', 'beam'), 'probe'), parts along dimension 0, may hold values from -0.09375 to 0.09375
- aperture: float32 [4096], P('beam'), may hold values from 0.5 to 1.5
- aberration: float32 [4096], P('beam'), may hold values from -3.140625 to 3.140625
- beam_k: int32 [2, 4096], P(None, 'beam'), may hold values from -32 to 31, as said below
- probe_pos: int32 [2, 2048], P(None, 'probe'), may hold values from 0 to 1023
- patches: bfloat16 [128, 512], P(('grp', 'probe')), parts along dimension 0, may hold values from -6 to 6
- patch_col: int32 [128], P('grp'), parts along dimension 0, may hold values from 0 to 7, never falling along the last dimension, each value on 1 to 32 neighbouring positions
Outputs:
- ionization: float32 [16, 2048], P('grp', ('probe', 'beam')), parts along dimension 0
There are 2 independent parts, one for each index of `grp`. A program takes and returns all parts, laid end to end along the dimension named above; an argument that names none is the same for every part. Nothing has to cross between parts.
Inputs may be any that keep to these rules, and one draw needn't show every extreme that they name: `patch_col`: patches are ordered by atom column; each of the 8 columns has 1 to 32 patches, and some column has exactly 32. `beam_k`: no two beams have the same pair of indices.
All inputs are finite; a program needn't handle non-finite values.
Results may differ from a plain program's by a relative error of at most 0.005.
Values may be sent and summed in bfloat16 or wider, within the bound.
No kernel may reach another device: no remote copies, remote signals or barrier semaphores. Data moves between devices by JAX's collectives and lax.ppermute only.
A program may use at most 128 MiB of HBM per device.

v0:
```python
import math

import jax
import jax.numpy as jnp
from jax import lax
from jax.sharding import PartitionSpec as P

PSIDE = 16
GRID = 1024


def coefficients(beam_k, aperture, aberration, positions):
    turn_count = jnp.mod(
        positions[0][:, None] * beam_k[0][None, :] + positions[1][:, None] * beam_k[1][None, :],
        GRID,
    )
    phase_angle = aberration[None, :] + 2.0 * math.pi / GRID * turn_count.astype(jnp.float32)
    real_coef = (aperture[None, :] * jnp.cos(phase_angle)).astype(jnp.bfloat16)
    imag_coef = (-(aperture[None, :] * jnp.sin(phase_angle))).astype(jnp.bfloat16)
    return (real_coef, imag_coef)


def detector(edge_count):
    half_side = edge_count // 2
    pixel_index = jnp.arange(edge_count * edge_count, dtype=jnp.int32)
    mode_index = jnp.arange(edge_count * half_side, dtype=jnp.int32)
    row_off = pixel_index // edge_count
    col_off = pixel_index % edge_count
    freq_first = mode_index // half_side - half_side
    freq_second = mode_index % half_side - edge_count // 4
    turn_count = jnp.mod(
        row_off[:, None] * freq_first[None, :] + col_off[:, None] * freq_second[None, :], edge_count
    )
    angle_value = 2.0 * math.pi / edge_count * turn_count.astype(jnp.float32)
    real_part = jnp.cos(angle_value)
    imag_part = -jnp.sin(angle_value)
    upper_rows = jnp.concatenate([real_part, imag_part], axis=1)
    lower_rows = jnp.concatenate([-imag_part, real_part], axis=1)
    return jnp.concatenate([upper_rows, lower_rows], axis=0).astype(jnp.bfloat16)


def patch_energy(picked, pot_rows, det_table):
    half_width = pot_rows.shape[-1] // 2
    psi_re = picked[..., :half_width].astype(jnp.float32)
    psi_im = picked[..., half_width:].astype(jnp.float32)
    pot_re = pot_rows[:, :half_width].astype(jnp.float32)
    pot_im = pot_rows[:, half_width:].astype(jnp.float32)
    wave_out = jnp.concatenate(
        [psi_re * pot_re - psi_im * pot_im, psi_re * pot_im + psi_im * pot_re], axis=-1
    ).astype(jnp.bfloat16)
    projected = jnp.einsum("rjx,xq->rjq", wave_out, det_table, preferred_element_type=jnp.float32)
    return jnp.sum(projected * projected, axis=-1) / float(half_width * (det_table.shape[1] // 2))


def combine(beam_terms):
    half_width = beam_terms.shape[-1] // 2
    return jnp.concatenate(
        [
            beam_terms[0, ..., :half_width] - beam_terms[1, ..., half_width:],
            beam_terms[0, ..., half_width:] + beam_terms[1, ..., :half_width],
        ],
        axis=-1,
    )


def spread_patches(psi, all_patches, patch_col, det_table):
    patch_total = all_patches.shape[0]
    group_size = math.gcd(patch_total, 16)
    column_count = psi.shape[1]
    col_groups = patch_col.reshape(patch_total // group_size, group_size)
    pot_groups = all_patches.reshape(patch_total // group_size, group_size, all_patches.shape[1])
    col_range = jnp.arange(column_count, dtype=jnp.int32)

    def add_block(running, blk_pair):
        col_ids, pot_rows = blk_pair
        picked = jnp.take(psi, col_ids, axis=1)
        energy = patch_energy(picked, pot_rows, det_table)
        onehot = (col_ids[:, None] == col_range[None, :]).astype(jnp.float32)
        return (
            running + jnp.einsum("rj,jc->cr", energy, onehot, precision=lax.Precision.HIGHEST),
            None,
        )

    running, _ = lax.scan(
        add_block, jnp.zeros((column_count, psi.shape[0]), jnp.float32), (col_groups, pot_groups)
    )
    return running


def apply_patches(psi_own, all_patches, patch_col, det_table):
    traded = lax.all_to_all(psi_own, "probe", split_axis=0, concat_axis=2, tiled=True)
    return spread_patches(traded[0], all_patches, patch_col, det_table)


def shards(smatrix, aperture, aberration, beam_k, probe_pos, patches, patch_col):
    probe_count = lax.axis_size("probe")
    beam_count = lax.axis_size("beam")
    all_patches = lax.all_gather(patches, "probe", axis=0, tiled=True)
    det_table = detector(PSIDE)
    col_dev = smatrix.shape[1]
    width_two = smatrix.shape[2]
    full_matrix, full_aperture, full_aberration, full_k = (
        lax.all_gather(smatrix, "beam", axis=0, tiled=True),
        lax.all_gather(aperture.astype(jnp.bfloat16), "beam", axis=0, tiled=True).astype(
            aperture.dtype
        ),
        lax.all_gather(aberration.astype(jnp.bfloat16), "beam", axis=0, tiled=True).astype(
            aberration.dtype
        ),
        lax.all_gather(beam_k, "beam", axis=1, tiled=True),
    )
    all_pos = lax.all_gather(probe_pos, "probe", axis=1, tiled=True)
    probe_total = all_pos.shape[1]
    half_probes = probe_total // (beam_count * probe_count)
    split_pos = all_pos.reshape(2, probe_count, beam_count, half_probes)
    mine = lax.dynamic_slice_in_dim(split_pos, lax.axis_index("beam"), 1, 2).reshape(
        2, probe_count * half_probes
    )
    row_total = probe_count * half_probes
    block_rows = math.gcd(row_total, 512)
    pos_blocks = mine.reshape(2, row_total // block_rows, block_rows).transpose(1, 0, 2)

    def whole_block(positions):
        real_coef, imag_coef = coefficients(full_k, full_aperture, full_aberration, positions)
        beam_terms = jnp.einsum(
            "kpb,bcx->kpcx",
            jnp.stack([real_coef, imag_coef]),
            full_matrix,
            preferred_element_type=jnp.float32,
        )
        return combine(beam_terms).astype(jnp.bfloat16)

    psi_own = lax.map(whole_block, pos_blocks).reshape(probe_count, half_probes, col_dev, width_two)
    return apply_patches(psi_own, all_patches, patch_col, det_table)


def solution(mesh):
    placed = (
        P(("grp", "beam"), "probe", None),
        P("beam"),
        P("beam"),
        P(None, "beam"),
        P(None, "probe"),
        P(("grp", "probe"), None),
        P("grp"),
    )
    return jax.shard_map(
        shards, mesh=mesh, in_specs=placed, out_specs=P("grp", ("probe", "beam")), check_vma=False
    )
```

profile of v0, /device:TPU:0, one launch (start us, length us, event | category | flops | bytes accessed | tf_op | source)
XLA Modules:
  0.0 199.6 jit_solution(7711247507291517825)
XLA Ops:
  6.5 0.0 all-gather.2.cloned.1.call-start
  6.6 4.0 %copy.15 = bf16[2048,1,512]{0,2,1:T(8,128)(2,1)} copy(bf16[2048,1,512]{2,0,1:T(8,128)(2,1)} %param.11) | data formatting | bytes 4194304 | tf_op args[0]
  10.6 0.0 all-gather.2.cloned.1.call-update
  10.6 1.9 all_gather.18
  12.6 1.8 all_gather.19
  14.4 27.6 %all_gather.20 = s32[2,2048]{1,0:T(2,128)S(1)} all-gather(s32[2,256]{1,0:T(2,128)S(1)} %copy-done.5), channel_id=1, replica_groups=mesh['grp'=2,'probe'=8,'beam'=2] {'probe'}, dimensions={1}, use_global_device_ids=true | all-gather | bytes 18432 | tf_op jit(solution)/shard_map/all_gather | solution.py:112
  42.1 1.8 all_gather.21
  43.9 0.0 copy-start.6
  44.0 82.0 %while.23 = (s32[]{:T(128)}, bf16[2,512,1,512]{3,1,0,2:T(8,128)(2,1)}, f32[4096]{0:T(1024)S(1)}, f32[4096]{0:T(1024)S(1)}, s32[2,2,512]{2,0,1:T(2,128)S(1)}, /*i...) while((s32[]{:T(128)}, bf16[2,512,1,512]{3,1,0,2:T(8,128)(2,1)}, ...), condition=%wide.region_1.2_spmd, body=%wide.region_0.1_spmd.sunk | while | flops 4346871808 | bytes 45756576 | solution.py:133
  44.0 35.1 %multiply_convert_fusion.2 = (bf16[1,512,4096]{2,1,0:T(8,128)(2,1)S(1)}, bf16[1,512,4096]{2,1,0:T(8,128)(2,1)S(1)}) fusion(s32[4096]{0:T(1024)S(1)} %bitcast.69, s32[512]{0:T(512)S(1)} %bitcast.72, s32[4096]{0:T(1024)S(1)} %bitcast.68, s32[512]{0:T(512)S(1)} %bitcast.71, f32[4096]{0:T(1024)S(1)} %get-tuple-element.349, f32[4096]{0:T(1024)S(1)} %get-tuple-element.348), kind=kLoop, calls=%fused_computation.14.clone.1 | loop fusion | flops 46137344 | bytes 8458240 | tf_op jit(solution)/shard_map/while/body/eval_jaxpr/convert_element_type | solution.py:18
  79.2 4.5 %fusion.66 = f32[2,512,1,512]{1,3,0,2:T(8,128)S(1)} fusion(bf16[4096,1,512]{0,2,1:T(8,128)(2,1)S(1)} %copy-done.7, bf16[1,512,4096]{2,1,0:T(8,128)(2,1)S(1)} %get-tuple-element.310, bf16[1,512,4096]{2,1,0:T(8,128)(2,1)S(1)} %get-tuple-element.311), kind=kOutput, calls=%fused_computation.16.clone.1 | convolution fusion | flops 4299161600 | bytes 14680064 | tf_op jit(solution)/shard_map/while/body/eval_jaxpr/kpb,bcx->kpcx/dot_general | solution.py:125
  83.7 0.2 fusion.67
  83.9 0.2 copy.30
  84.1 0.8 constant_dynamic-update-slice_fusion.2
  85.0 35.1 %multiply_convert_fusion.2 = (bf16[1,512,4096]{2,1,0:T(8,128)(2,1)S(1)}, bf16[1,512,4096]{2,1,0:T(8,128)(2,1)S(1)}) fusion(s32[4096]{0:T(1024)S(1)} %bitcast.69, s32[512]{0:T(512)S(1)} %bitcast.72, s32[4096]{0:T(1024)S(1)} %bitcast.68, s32[512]{0:T(512)S(1)} %bitcast.71, f32[4096]{0:T(1024)S(1)} %get-tuple-element.349, f32[4096]{0:T(1024)S(1)} %get-tuple-element.348), kind=kLoop, calls=%fused_computation.14.clone.1 | loop fusion | flops 46137344 | bytes 8458240 | tf_op jit(solution)/shard_map/while/body/eval_jaxpr/convert_element_type | solution.py:18
  120.2 4.5 %fusion.66 = f32[2,512,1,512]{1,3,0,2:T(8,128)S(1)} fusion(bf16[4096,1,512]{0,2,1:T(8,128)(2,1)S(1)} %copy-done.7, bf16[1,512,4096]{2,1,0:T(8,128)(2,1)S(1)} %get-tuple-element.310, bf16[1,512,4096]{2,1,0:T(8,128)(2,1)S(1)} %get-tuple-element.311), kind=kOutput, calls=%fused_computation.16.clone.1 | convolution fusion | flops 4299161600 | bytes 14680064 | tf_op jit(solution)/shard_map/while/body/eval_jaxpr/kpb,bcx->kpcx/dot_general | solution.py:125
  124.7 0.2 fusion.67
  124.9 0.2 copy.30
  125.2 0.8 constant_dynamic-update-slice_fusion.2
  126.0 4.0 %all-to-all-start = ((bf16[8,128,1,512]{3,1,2,0:T(8,128)(2,1)}), bf16[8,128,1,512]{3,1,2,0:T(8,128)(2,1)S(1)}, u32[]{:S(2)}, u32[]{:S(2)}) async-start(bf16[8,128,1,512]{3,1,2,0:T(8,128)(2,1)} %bitcast.9), calls=%async_computation | async-start | bytes 2097152 | tf_op jit(solution)/shard_map/all_to_all | solution.py:91
  130.0 0.1 reshape.547
  130.1 46.0 %all_gather.23 = bf16[64,512]{1,0:T(8,128)(2,1)S(1)} all-gather(bf16[8,512]{1,0:T(8,128)(2,1)S(1)} %copy-done.2), channel_id=1, replica_groups=mesh['grp'=2,'probe'=8,'beam'=2] {'probe'}, dimensions={0}, use_global_device_ids=true | all-gather | bytes 73728 | tf_op jit(solution)/shard_map/all_gather | solution.py:98
  176.1 0.6 negate_convert_fusion.1
  176.8 15.3 %while.24 = (s32[]{:T(128)}, f32[8,128]{1,0:T(8,128)S(1)}, s32[4,16]{1,0:T(4,128)S(1)}, bf16[128,8,512]{2,0,1:T(8,128)(2,1)S(1)}, bf16[4,16,512]{2,1,0:T(8,128)(...) while((s32[]{:T(128)}, f32[8,128]{1,0:T(8,128)S(1)}, s32[4,16]{1,0:T(4,128)S(1)}, ...), condition=%wide.region_4.5_spmd.clone, body=%wide.region_2.4_spmd.clone.sunk | while | flops 548613504 | bytes 15086163 | solution.py:84
  176.9 0.7 gather_fusion
  177.6 1.3 fusion.73
  178.9 0.7 fusion.74
  179.6 0.8 multiply_reduce_fusion.2
  180.4 0.2 convolution_add_fusion.2
  180.6 0.1 slice_convert_fusion.3
  180.7 0.7 gather_fusion
  181.4 1.3 fusion.73
  182.7 0.7 fusion.74
  183.4 0.8 multiply_reduce_fusion.2
  184.2 0.2 convolution_add_fusion.2
  184.4 0.1 slice_convert_fusion.3
  184.5 0.7 gather_fusion
  185.2 1.3 fusion.73
  186.5 0.7 fusion.74
  187.2 0.8 multiply_reduce_fusion.2
  188.0 0.2 convolution_add_fusion.2
  188.3 0.1 slice_convert_fusion.3
  188.4 0.7 gather_fusion
  189.1 1.3 fusion.73
  190.4 0.7 fusion.74
  191.1 0.8 multiply_reduce_fusion.2
  191.9 0.2 convolution_add_fusion.2
  192.1 0.7 copy-done
  (53 shorter events, 0.4 us)
Async XLA Ops:
  6.5 4.1 %copy-start.3 = (f32[2048]{0:T(1024)S(1)}, f32[2048]{0:T(1024)}, u32[]{:S(2)}) copy-start(f32[2048]{0:T(1024)} %param.12) | copy-start | bytes 24580
  6.5 6.1 %copy-start.4 = (f32[2048]{0:T(1024)S(1)}, f32[2048]{0:T(1024)}, u32[]{:S(2)}) copy-start(f32[2048]{0:T(1024)} %param.13) | copy-start | bytes 24580
  6.5 7.9 %copy-start.5 = (s32[2,256]{1,0:T(2,128)S(1)}, s32[2,256]{1,0:T(2,128)}, u32[]{:S(2)}) copy-start(s32[2,256]{1,0:T(2,128)} %param.15) | copy-start | bytes 6148
  6.5 35.6 %copy-start.1 = (s32[2,2048]{1,0:T(2,128)S(1)}, s32[2,2048]{1,0:T(2,128)}, u32[]{:S(2)}) copy-start(s32[2,2048]{1,0:T(2,128)} %param.14) | copy-start | bytes 49156
  6.5 37.4 %all-gather.2.cloned.1.call-start = ((), (), s32[]{:S(2)}) async-start(), calls=%async_computation.1 | async-start | bytes 6291456 | tf_op jit(solution)/shard_map/all_gather | solution.py:103
  43.9 86.1 %copy-start.6 = (s32[64]{0:T(128)S(1)}, s32[64]{0:T(128)}, u32[]{:S(2)}) copy-start(s32[64]{0:T(128)} %param.17) | copy-start | bytes 772
  44.0 86.1 %copy-start.2 = (bf16[8,512]{1,0:T(8,128)(2,1)S(1)}, bf16[8,512]{1,0:T(8,128)(2,1)}, u32[]{:S(2)}) copy-start(bf16[8,512]{1,0:T(8,128)(2,1)} %param.16) | copy-start | bytes 24580
  44.0 35.1 %copy-start.7 = (bf16[4096,1,512]{0,2,1:T(8,128)(2,1)S(1)}, bf16[4096,1,512]{0,2,1:T(8,128)(2,1)}, u32[]{:S(2)}) copy-start(bf16[4096,1,512]{0,2,1:T(8,128)(2,1)} %get-tuple-element.352) | copy-start | bytes 12582916 | tf_op jit(solution)/shard_map/while
  85.0 35.1 %copy-start.7 = (bf16[4096,1,512]{0,2,1:T(8,128)(2,1)S(1)}, bf16[4096,1,512]{0,2,1:T(8,128)(2,1)}, u32[]{:S(2)}) copy-start(bf16[4096,1,512]{0,2,1:T(8,128)(2,1)} %get-tuple-element.352) | copy-start | bytes 12582916 | tf_op jit(solution)/shard_map/while
  126.0 50.8 %all-to-all-start = ((bf16[8,128,1,512]{3,1,2,0:T(8,128)(2,1)}), bf16[8,128,1,512]{3,1,2,0:T(8,128)(2,1)S(1)}, u32[]{:S(2)}, u32[]{:S(2)}) async-start(bf16[8,128,1,512]{3,1,2,0:T(8,128)(2,1)} %bitcast.9), calls=%async_computation | async-start | bytes 2097152 | tf_op jit(solution)/shard_map/all_to_all | solution.py:91
  192.1 0.7 copy-start
Sparse Core Ops, SparseCore 0:
  10.7 16.3 all-gather.1
where the time goes:
time: 200 us
  other arithmetic  79.6 us (40%)
  blocking collectives  79.2 us (40%)
  between operations  13.5 us (7%)
  matrix products  13.1 us (7%)
  local copies, waits for them, and re-layouts  9.73 us (5%)
  starting transfers between devices  4.05 us (2%)
    convert_element_type x2, other arithmetic, coefficients(): real_coef = (aperture[None, :] * jnp.cos(phase_angle)).astype(jnp.bfloat16)  70.2 us
    all_gather x1, blocking collectives, shards(): all_patches = lax.all_gather(patches, 'probe', axis=0, tiled=True)  46 us
    all_gather x1, blocking collectives, shards(): all_pos = lax.all_gather(probe_pos, 'probe', axis=1, tiled=True)  27.6 us
    dot_general x2, matrix products, whole_block(): jnp.einsum('kpb,bcx->kpcx', jnp.stack([real_coef, imag_coef]), full_matri...  9.06 us
    select_n x8, other arithmetic, add_block(): picked = jnp.take(psi, col_ids, axis=1)  5.19 us
    unnamed x15, local copies, waits for them, and re-layouts  4.67 us
    all_to_all x1, starting transfers between devices, apply_patches(): lax.all_to_all(psi_own, 'probe', split_axis=0, concat_axis=2, tiled=True)  4.02 us
  transfers between devices with their start and end apart: 2, of which 0 were waited for; matrix products, arithmetic and copies ran while one was open for 0% of the time, Pallas kernels for 0%

commit v1 on v0

v1 whole, which is shorter than its diff:
```python
import functools
import math

import jax
import jax.numpy as jnp
import numpy as np
from jax import lax
from jax.experimental import pallas as pl
from jax.experimental.pallas import tpu as pltpu
from jax.sharding import PartitionSpec as P

PSIDE = 16
GRID = 1024
KMAX = 32
LANE = 128


def mode_overlap():
    pix = np.arange(LANE)
    row, col = pix // PSIDE, pix % PSIDE
    dist = col[:, None] - col[None, :]
    freq = np.arange(PSIDE // 2) - PSIDE // 4
    angle = (2.0 * math.pi / PSIDE) * ((freq[:, None, None] * dist[None]) % PSIDE)
    same = (row[:, None] == row[None, :]).astype(np.float64) * PSIDE / float(PSIDE**2 * (PSIDE**2 // 2))
    return np.stack([np.cos(angle).sum(0) * same, -np.sin(angle).sum(0) * same]).astype(np.float32)


def half_turns(count):
    folded = jnp.bitwise_and(count + GRID, 2 * GRID - 1) - GRID
    u = folded.astype(jnp.float32) * (1.0 / GRID)
    u2 = u * u
    terms = 9
    c = [(-1.0) ** k * math.pi ** (2 * k) / math.factorial(2 * k) for k in range(terms)]
    s = [(-1.0) ** k * math.pi ** (2 * k + 1) / math.factorial(2 * k + 1) for k in range(terms)]
    cos_v, sin_v = jnp.full_like(u, c[-1]), jnp.full_like(u, s[-1])
    for k in range(terms - 2, -1, -1):
        cos_v = cos_v * u2 + c[k]
        sin_v = sin_v * u2 + s[k]
    return cos_v, sin_v * u


def kernel(
    rows, blocks, s_own, s_rem, amp, abr, k_own, k_rem, shared, cols, overlap, out,
    s_all, x_even, x_odd, grid_rows, coef, basis, tab, phase, place_v, place_s, sem_s, sem_i,
):
    f32, bf16 = jnp.float32, jnp.bfloat16
    half = lax.axis_index("beam")
    column = lax.axis_index("probe")
    copies = [
        pltpu.make_async_copy(src, s_all.at[pl.ds(i * rows, rows)], sem_s.at[i])
        for i, src in enumerate((s_own, s_rem))
    ]
    for c in copies:
        c.start()
    for i, k_ref in enumerate((k_own, k_rem)):
        kx, ky = k_ref[0:1, :], k_ref[1:2, :]
        qx, qy = kx >= 0, ky >= 0
        mx, my = jnp.where(qx, kx, -1 - kx), jnp.where(qy, ky, -1 - ky)
        quad = 2 * qx.astype(jnp.int32) + qy.astype(jnp.int32)
        place_v[i : i + 1, :] = ((quad * KMAX + mx) * KMAX + my) * 4
    idx_copy = pltpu.make_async_copy(place_v, place_s, sem_i)
    idx_copy.start()
    phase[0] = amp[...] * jnp.cos(abr[...])
    phase[1] = amp[...] * jnp.sin(abr[...])

    def tables(j):
        px = shared[j, 8:9, pl.ds(pl.multiple_of(half * LANE, LANE), LANE)].astype(jnp.int32)
        py = shared[j, 8:9, pl.ds(pl.multiple_of(2 * LANE + half * LANE, LANE), LANE)].astype(jnp.int32)
        my = lax.broadcasted_iota(jnp.int32, (KMAX, LANE), 0)
        mx = lax.broadcasted_iota(jnp.int32, (8, LANE), 0)
        cy, sy = half_turns((2 * my + 1) * py)
        cx, sx = half_turns(jnp.where(mx < 4, 2 * mx + 1, 8) * px)
        reps = LANE // KMAX
        spread = lambda t: jnp.concatenate([jnp.broadcast_to(t[m : m + 1], (KMAX, LANE)) for m in range(reps)], 0)
        made = (
            jnp.concatenate([cy] * reps, 0), jnp.concatenate([sy] * reps, 0), spread(cx), spread(sx),
            jnp.broadcast_to(cx[4:5], (LANE, LANE)), jnp.broadcast_to(sx[4:5], (LANE, LANE)),
        )
        for n, t in enumerate(made):
            tab[n, pl.ds(pl.multiple_of(j * LANE, LANE), LANE), :] = t.T

    def coefficients(j, sub, step=32):
        here = pl.ds(pl.multiple_of(j * LANE + sub * step, step), step)
        cy, sy, cx, sx, c4, s4 = (tab[n, here, :] for n in range(6))
        for g in range(KMAX // 4):
            prods = (cx * cy, sx * sy, sx * cy, cx * sy)
            for n, v in enumerate(prods):
                coef[here, pl.ds((4 * g + n) * LANE, LANE)] = v.astype(bf16)
            cx, sx = cx * c4 - sx * s4, sx * c4 + cx * s4

    def turned(r, x_ref):
        here = pl.ds(pl.multiple_of(r * LANE, LANE), LANE)
        ph_c = jnp.broadcast_to(phase[0, pl.ds(r, 1), :], (LANE, LANE)).T
        ph_s = jnp.broadcast_to(phase[1, pl.ds(r, 1), :], (LANE, LANE)).T
        for h in range(2):
            re = s_all[here, pl.ds(h * LANE, LANE)].astype(f32)
            im = s_all[here, pl.ds((2 + h) * LANE, LANE)].astype(f32)
            x_ref[pl.ds(h, LANE, stride=4), :] = ph_c * re + ph_s * im
            x_ref[pl.ds(2 + h, LANE, stride=4), :] = ph_c * im - ph_s * re

    def scatter(r, x_ref):
        per = rows // LANE
        which, base = r // per, (r % per) * LANE
        for u in range(LANE):
            to = place_s[which, base + u]
            grid_rows[pl.ds(pl.multiple_of(to, 4), 4), :] = x_ref[4 * u : 4 * u + 4, :]

    total = 2 * rows // LANE
    tables(0)
    for c in copies:
        c.wait()
    idx_copy.wait()
    turned(0, x_even)
    per_step = total // blocks

    @pl.loop(0, blocks)
    def _(j):
        for u in range(per_step):
            r = j * per_step + u
            now, later = (x_even, x_odd) if u % 2 == 0 else (x_odd, x_even)
            turned(jnp.minimum(r + 1, total - 1), later)
            scatter(r, now)
        for sub in range(4):
            coefficients(j, sub)
        tables(jnp.minimum(j + 1, blocks - 1))

    quarter = KMAX * KMAX * 4

    @pl.loop(0, KMAX * KMAX // LANE)
    def _(g):
        to = lambda n: pl.ds(pl.multiple_of((4 * g + n) * LANE, LANE), LANE)
        for h in range(2):
            vals = []
            for part in range(2):
                mm, mp, pm, pp = (
                    grid_rows[pl.ds(q * quarter + g * 4 * LANE + 2 * part + h, LANE, stride=4), :] for q in range(4)
                )
                a, b, c, d = pp + mm, pp - mm, pm + mp, pm - mp
                vals.append((a + c, c - a, b + d, b - d))
            re, im = vals
            at_re, at_im = pl.ds(2 * h * LANE, LANE), pl.ds((2 * h + 1) * LANE, LANE)
            for n in range(4):
                if n < 2:
                    basis[to(n), at_re], basis[to(n), at_im] = re[n].astype(bf16), im[n].astype(bf16)
                else:
                    basis[to(n), at_re], basis[to(n), at_im] = im[n].astype(bf16), (-re[n]).astype(bf16)

    pots = jnp.concatenate([shared[j, 0:8, :] for j in range(blocks)], 0)
    mine = (cols[...] == column).astype(f32)
    left = (pots.T * mine).astype(bf16)
    right = pots.astype(bf16)
    g_re, g_im = overlap[0], overlap[1]
    energy = []
    for h in range(2):
        lr, li = left[h * LANE : (h + 1) * LANE], left[(2 + h) * LANE : (3 + h) * LANE]
        rr, ri = right[:, h * LANE : (h + 1) * LANE], right[:, (2 + h) * LANE : (3 + h) * LANE]
        mul = lambda a, b: jnp.dot(a, b, preferred_element_type=f32)
        r_re, r_im = mul(lr, rr) + mul(li, ri), mul(li, rr) - mul(lr, ri)
        h_re, h_im = g_re * r_re - g_im * r_im, g_re * r_im + g_im * r_re
        form = jnp.concatenate(
            [jnp.concatenate([h_re, h_im], 1), jnp.concatenate([-h_im, h_re], 1)], 0
        ).astype(bf16)
        psi = jnp.dot(coef[...], basis[:, pl.ds(2 * h * LANE, 2 * LANE)], preferred_element_type=f32)
        e = psi * jnp.dot(psi.astype(bf16), form, preferred_element_type=f32)
        energy.append(e[:, :LANE] + e[:, LANE:])
    e = energy[0] + energy[1]
    for j in range(blocks):
        out[j : j + 1, :] = jnp.sum(e[j * LANE : (j + 1) * LANE].T, axis=0, keepdims=True)


def shards(smatrix, aperture, aberration, beam_k, probe_pos, patches, patch_col):
    blocks = lax.axis_size("probe")
    rows, width = smatrix.shape[0], smatrix.shape[2]
    swap = lambda v: lax.ppermute(v, "beam", [(0, 1), (1, 0)])
    s_own = smatrix.reshape(rows, width)
    s_rem = swap(s_own)
    k_rem = swap(beam_k)
    weights = jnp.stack([aperture, aberration])
    both = jnp.concatenate([weights, swap(weights)], 1).reshape(2, 2 * rows // LANE, LANE)
    small = jnp.concatenate([patches.astype(jnp.float32), probe_pos.astype(jnp.float32).reshape(1, width)], 0)
    shared = lax.all_to_all(jnp.broadcast_to(small[None], (blocks,) + small.shape), "probe", 0, 0)
    vmem, anyw = pl.BlockSpec(memory_space=pltpu.VMEM), pl.BlockSpec(memory_space=pl.ANY)
    probes = blocks * LANE
    grid = 4 * KMAX * KMAX
    energy = pl.pallas_call(
        functools.partial(kernel, rows, blocks),
        out_shape=jax.ShapeDtypeStruct((blocks, LANE), jnp.float32),
        in_specs=[anyw, anyw] + [vmem] * 7,
        out_specs=vmem,
        scratch_shapes=[
            pltpu.VMEM((2 * rows, width), jnp.bfloat16),
            pltpu.VMEM((4 * LANE, LANE), jnp.float32),
            pltpu.VMEM((4 * LANE, LANE), jnp.float32),
            pltpu.VMEM((4 * grid, LANE), jnp.float32),
            pltpu.VMEM((probes, grid), jnp.bfloat16),
            pltpu.VMEM((grid, width), jnp.bfloat16),
            pltpu.VMEM((6, probes, LANE), jnp.float32),
            pltpu.VMEM((2, 2 * rows // LANE, LANE), jnp.float32),
            pltpu.VMEM((2, rows), jnp.int32),
            pltpu.SMEM((2, rows), jnp.int32),
            pltpu.SemaphoreType.DMA((2,)),
            pltpu.SemaphoreType.DMA,
        ],
        compiler_params=pltpu.CompilerParams(vmem_limit_bytes=56 * 1024 * 1024),
    )(
        s_own, s_rem, both[0], both[1], beam_k, k_rem, shared, patch_col.reshape(1, -1),
        jnp.asarray(mode_overlap()),
    )
    return lax.all_to_all(energy, "probe", 0, 0, tiled=True)


def solution(mesh):
    placed = (
        P(("grp", "beam"), "probe", None),
        P("beam"),
        P("beam"),
        P(None, "beam"),
        P(None, "probe"),
        P(("grp", "probe"), None),
        P("grp"),
    )
    return jax.shard_map(
        shards, mesh=mesh, in_specs=placed, out_specs=P("grp", ("probe", "beam")), check_vma=False
    )
```

time: 200 us -> 60.3 us (0.30)
  other arithmetic: 79.6 us -> 2.86 us
  blocking collectives: 79.2 us -> 9.98 us
  Pallas kernels: 0 us -> 27.4 us
  between operations: 13.5 us -> 0.03 us
  matrix products: 13.1 us -> 0 us
  waiting for transfers between devices: 0.02 us -> 8.15 us
  local copies, waits for them, and re-layouts: 9.73 us -> 3.37 us
  starting transfers between devices: 4.05 us -> 7.93 us
    all_gather x5 -> x0, blocking collectives: 79.2 us -> none  [the longest x1 46 us: shards(): all_patches = lax.all_gather(patches, 'probe', axis=0, tiled=True)]
    convert_element_type x10 -> x1, other arithmetic: 70.4 us -> 0.7 us  [shards(): patches.astype(jnp.float32)]
    pallas_call x0 -> x1, Pallas kernels: none -> 27.4 us  [shards(): pl.pallas_call(functools.partial(kernel, rows, blocks), out_shape=jax.Sha...]
    dot_general x10 -> x0, matrix products: 13.1 us -> none  [the longest x2 9.06 us: whole_block(): jnp.einsum('kpb,bcx->kpcx', jnp.stack([real_coef, imag_coef]), full_matri...]
    all_to_all x0 -> x1, blocking collectives: none -> 9.98 us  [shards(): return lax.all_to_all(energy, 'probe', 0, 0, tiled=True)]
    all_to_all x1, waiting for transfers between devices: 0.01 us -> 8.14 us  [shards(): lax.all_to_all(jnp.broadcast_to(small[None], (blocks,) + small.shape), 'p...]
    select_n x9 -> x0, other arithmetic: 5.19 us -> none  [the longest x8 5.19 us: add_block(): picked = jnp.take(psi, col_ids, axis=1)]
    another operation x7 -> x1, other arithmetic: 3.76 us -> 0.73 us  [shards(): weights = jnp.stack([aperture, aberration])]
  transfers between devices with their start and end apart: 2 -> 4, of which waited for: 0 -> 1; matrix products, arithmetic and copies ran while one was open for 0% -> 7% of each run, Pallas kernels for 0% -> 0%
where the time goes in v1:
time: 60.3 us; the launch traced here: 59.7 us
  Pallas kernels  27.4 us (45%)
  blocking collectives  9.98 us (17%)
  waiting for transfers between devices  8.15 us (14%)
  starting transfers between devices  7.93 us (13%)
  local copies, waits for them, and re-layouts  3.37 us (6%)
  other arithmetic  2.86 us (5%)
    pallas_call x1, Pallas kernels, shards(): pl.pallas_call(functools.partial(kernel, rows, blocks), out_shape=jax.Sha...  27.4 us
    all_to_all x1, blocking collectives, shards(): return lax.all_to_all(energy, 'probe', 0, 0, tiled=True)  9.98 us
    all_to_all x1, waiting for transfers between devices, shards(): lax.all_to_all(jnp.broadcast_to(small[None], (blocks,) + small.shape), 'p...  8.14 us
    all_to_all x1, starting transfers between devices, shards(): lax.all_to_all(jnp.broadcast_to(small[None], (blocks,) + small.shape), 'p...  6.91 us
    unnamed x8, local copies, waits for them, and re-layouts  2.01 us
  transfers between devices with their start and end apart: 4, of which 1 were waited for; matrix products, arithmetic and copies ran while one was open for 7% of the time, Pallas kernels for 0%

profile of v1, /device:TPU:0, one launch (start us, length us, event | category | flops | bytes accessed | tf_op | source)
XLA Modules:
  0.0 59.7 jit_solution(18396459964117901288)
XLA Ops:
  0.0 0.5 collective-permute-start
  0.5 0.7 %pad_maximum_fusion.2 = f32[2,2048]{1,0:T(2,128)S(1)} fusion(f32[1,2048]{1,0:T(1,128)} %bitcast.18, f32[1,2048]{1,0:T(1,128)} %bitcast.20), kind=kLoop, calls=%fused_computation.2 | loop fusion | flops 4096 | bytes 32768 | tf_op jit(solution)/shard_map/stack | solution.py:178
  1.2 0.1 collective-permute-start.1
  1.3 0.5 collective-permute-start.2
  1.8 0.7 %convert_bitcast_fusion = f32[1,1,2,256]{3,2,1,0:T(2,128)S(1)} fusion(s32[2,256]{1,0:T(2,128)} %param.12), kind=kLoop, calls=%fused_computation.3 | loop fusion | flops 512 | bytes 4096
  2.5 0.7 %convert_element_type.6 = f32[8,512]{1,0:T(8,128)S(1)} convert(bf16[8,512]{1,0:T(8,128)(2,1)} %param.13) | non-fusion elementwise | flops 4096 | bytes 24576 | tf_op jit(solution)/shard_map/convert_element_type | solution.py:180
  3.2 0.7 %broadcast_in_dim.2 = f32[8,9,512]{2,1,0:T(8,128)} broadcast(f32[9,512]{1,0:T(8,128)S(1)} %pad_maximum_fusion.1), dimensions={1,2} | broadcast | bytes 165888 | tf_op jit(solution)/shard_map/broadcast_in_dim | solution.py:181
  3.9 6.9 %all-to-all-start = ((f32[8,9,512]{2,1,0:T(8,128)}), f32[8,9,512]{2,1,0:T(8,128)S(1)}, u32[]{:S(2)}, u32[]{:S(2)}) async-start(f32[8,9,512]{2,1,0:T(8,128)} %broadcast_in_dim.2), calls=%async_computation | async-start | bytes 524288 | tf_op jit(solution)/shard_map/all_to_all | solution.py:181
  10.8 0.0 collective-permute-done.1
  10.8 0.7 %pad_maximum_fusion = f32[2,4096]{1,0:T(2,128)S(1)} fusion(f32[2,2048]{1,0:T(2,128)S(1)} %collective-permute-done.1, f32[1,2048]{1,0:T(1,128)} %bitcast.19, f32[1,2048]{1,0:T(1,128)} %bitcast.21), kind=kLoop, calls=%fused_computation | loop fusion | flops 16384 | bytes 65536 | tf_op jit(solution)/shard_map/concatenate | solution.py:179
  11.5 0.6 %fusion = (f32[1,4096]{1,0:T(1,128)}, f32[1,4096]{1,0:T(1,128)}) fusion(f32[2,4096]{1,0:T(2,128)S(1)} %pad_maximum_fusion), kind=kLoop, calls=%fused_computation.4 | loop fusion | bytes 65536 | tf_op jit(solution)/shard_map/slice | solution.py:206
  12.2 0.0 collective-permute-done.2.k_rem
  12.2 0.0 copy-start.2
  12.2 8.1 %all-to-all-done.shared = f32[8,9,512]{2,1,0:T(8,128)S(1)} async-done(((f32[8,9,512]{2,1,0:T(8,128)}), f32[8,9,512]{2,1,0:T(8,128)S(1)}, u32[]{:S(2)}, u32[]{:S(2)}) %all-to-all-start) | async-done | bytes 147488 | tf_op jit(solution)/shard_map/all_to_all | solution.py:181
  20.3 0.0 copy-start.1
  20.3 0.0 collective-permute-done.s_rem
  20.3 0.0 copy-start
  20.3 0.0 copy-done.2
  20.3 0.7 %copy-done.1 = f32[8,9,512]{2,1,0:T(8,128)} copy-done((f32[8,9,512]{2,1,0:T(8,128)}, f32[8,9,512]{2,1,0:T(8,128)S(1)}, u32[]{:S(2)}) %copy-start.1) | copy-done | bytes 147480
  21.0 0.7 %copy-done = bf16[2048,512]{1,0:T(8,128)(2,1)} copy-done((bf16[2048,512]{1,0:T(8,128)(2,1)}, bf16[2048,512]{1,0:T(8,128)(2,1)S(1)}, u32[]{:S(2)}) %copy-start) | copy-done | bytes 2097176
  21.7 27.4 %shard_map.82 = f32[8,128]{1,0:T(8,128)} custom-call(bf16[2048,512]{1,0:T(8,128)(2,1)} %bitcast.15, bf16[2048,512]{1,0:T(8,128)(2,1)} %copy-done, f32[32,128]{1,0:T(8,128)} %bitcast.17, f32[32,128]{1,0:T(8,128)} %bitcast.16, s32[2,2048]{1,0:T(2,128)} %k_own.1, s32[2,2048]{1,0:T(2,128)} %copy-done.2, f32[8,9,512]{2,1,0:T(8,128)} %copy-done.1, ...), custom_call_target="tpu_custom_call" | custom-call | tf_op jit(solution)/shard_map/pallas_call | solution.py:185
  49.1 10.0 %all_to_all.17 = f32[8,1,128]{2,1,0:T(1,128)S(1)} all-to-all(f32[8,1,128]{2,1,0:T(1,128)} %bitcast.23), channel_id=1, replica_groups=mesh['grp'=2,'probe'=8,'beam'=2] {'probe'}, dimensions={0} | all-to-all | bytes 8192 | tf_op jit(solution)/shard_map/all_to_all | solution.py:209
  59.1 0.6 copy.12
  (2 shorter events, 0.0 us)
Async XLA Ops:
  0.0 20.3 %collective-permute-start = (bf16[2048,512]{1,0:T(8,128)(2,1)}, bf16[2048,512]{1,0:T(8,128)(2,1)S(1)}, u32[]{:S(2)}, u32[]{:S(2)}) collective-permute-start(bf16[2048,512]{1,0:T(8,128)(2,1)} %bitcast.14), channel_id=1, source_target_pairs={{0,1},{1,0},{2,3},{3,2},{4,5},{5,4},{6,7},{7,6},{8,9},{9,8},{10,11... | collective-permute-start | bytes 6291464 | tf_op jit(solution)/shard_map/ppermute | solution.py:174
  1.2 9.6 %collective-permute-start.1 = (f32[2,2048]{1,0:T(2,128)S(1)}, f32[2,2048]{1,0:T(2,128)S(1)}, u32[]{:S(2)}, u32[]{:S(2)}) collective-permute-start(f32[2,2048]{1,0:T(2,128)S(1)} %pad_maximum_fusion.2), channel_id=1, source_target_pairs={{0,1},{1,0},{2,3},{3,2},{4,5},{5,4},{6,7},{7,6},{8,9},{9,8},{10,11... | collective-permute-start | bytes 49160 | tf_op jit(solution)/shard_map/ppermute | solution.py:174
  1.3 10.9 %collective-permute-start.2 = (s32[2,2048]{1,0:T(2,128)}, s32[2,2048]{1,0:T(2,128)S(1)}, u32[]{:S(2)}, u32[]{:S(2)}) collective-permute-start(s32[2,2048]{1,0:T(2,128)} %k_own.1), channel_id=1, source_target_pairs={{0,1},{1,0},{2,3},{3,2},{4,5},{5,4},{6,7},{7,6},{8,9},{9,8},{10,11... | collective-permute-start | bytes 49160 | tf_op jit(solution)/shard_map/ppermute | solution.py:174
  3.9 16.4 %all-to-all-start = ((f32[8,9,512]{2,1,0:T(8,128)}), f32[8,9,512]{2,1,0:T(8,128)S(1)}, u32[]{:S(2)}, u32[]{:S(2)}) async-start(f32[8,9,512]{2,1,0:T(8,128)} %broadcast_in_dim.2), calls=%async_computation | async-start | bytes 524288 | tf_op jit(solution)/shard_map/all_to_all | solution.py:181
  12.2 8.1 %copy-start.2 = (s32[2,2048]{1,0:T(2,128)}, s32[2,2048]{1,0:T(2,128)S(1)}, u32[]{:S(2)}) copy-start(s32[2,2048]{1,0:T(2,128)S(1)} %collective-permute-done.2.k_rem) | copy-start | bytes 49156
  20.3 0.7 %copy-start.1 = (f32[8,9,512]{2,1,0:T(8,128)}, f32[8,9,512]{2,1,0:T(8,128)S(1)}, u32[]{:S(2)}) copy-start(f32[8,9,512]{2,1,0:T(8,128)S(1)} %all-to-all-done.shared) | copy-start | bytes 442372
  20.3 1.4 %copy-start = (bf16[2048,512]{1,0:T(8,128)(2,1)}, bf16[2048,512]{1,0:T(8,128)(2,1)S(1)}, u32[]{:S(2)}) copy-start(bf16[2048,512]{1,0:T(8,128)(2,1)S(1)} %collective-permute-done.s_rem) | copy-start | bytes 6291460

commit v2 on v1

v2 whole, which is shorter than its diff:
```python
import functools
import math

import jax
import jax.numpy as jnp
import numpy as np
from jax import lax
from jax.experimental import pallas as pl
from jax.experimental.pallas import tpu as pltpu
from jax.sharding import PartitionSpec as P

PSIDE = 16
GRID = 1024
KMAX = 32
LANE = 128


def mode_overlap():
    pix = np.arange(LANE)
    row, col = pix // PSIDE, pix % PSIDE
    dist = col[:, None] - col[None, :]
    freq = np.arange(PSIDE // 2) - PSIDE // 4
    angle = (2.0 * math.pi / PSIDE) * ((freq[:, None, None] * dist[None]) % PSIDE)
    same = (row[:, None] == row[None, :]).astype(np.float64) * PSIDE / float(PSIDE**2 * (PSIDE**2 // 2))
    return np.stack([np.cos(angle).sum(0) * same, -np.sin(angle).sum(0) * same]).astype(np.float32)


def half_turns(count):
    folded = jnp.bitwise_and(count + GRID, 2 * GRID - 1) - GRID
    u = folded.astype(jnp.float32) * (1.0 / GRID)
    u2 = u * u
    terms = 9
    c = [(-1.0) ** k * math.pi ** (2 * k) / math.factorial(2 * k) for k in range(terms)]
    s = [(-1.0) ** k * math.pi ** (2 * k + 1) / math.factorial(2 * k + 1) for k in range(terms)]
    cos_v, sin_v = jnp.full_like(u, c[-1]), jnp.full_like(u, s[-1])
    for k in range(terms - 2, -1, -1):
        cos_v = cos_v * u2 + c[k]
        sin_v = sin_v * u2 + s[k]
    return cos_v, sin_v * u


def place_rows(k_ref, place_v):
    kx, ky = k_ref[0:1, :], k_ref[1:2, :]
    qx, qy = kx >= 0, ky >= 0
    mx, my = jnp.where(qx, kx, -1 - kx), jnp.where(qy, ky, -1 - ky)
    quad = 2 * qx.astype(jnp.int32) + qy.astype(jnp.int32)
    place_v[...] = ((quad * KMAX + mx) * KMAX + my) * 4


def spread_rows(s_ref, amp, abr, k_ref, grid_rows, x_even, x_odd, phase, place_v, place_s, sem, ready=None):
    f32 = jnp.float32
    rows = s_ref.shape[0]
    place_rows(k_ref, place_v)
    idx_copy = pltpu.make_async_copy(place_v.at[0], place_s, sem)
    idx_copy.start()
    phase[0] = amp[...] * jnp.cos(abr[...])
    phase[1] = amp[...] * jnp.sin(abr[...])

    def turned(r, x_ref):
        here = pl.ds(pl.multiple_of(r * LANE, LANE), LANE)
        ph_c = jnp.broadcast_to(phase[0, pl.ds(r, 1), :], (LANE, LANE)).T
        ph_s = jnp.broadcast_to(phase[1, pl.ds(r, 1), :], (LANE, LANE)).T
        for h in range(2):
            re = s_ref[here, pl.ds(h * LANE, LANE)].astype(f32)
            im = s_ref[here, pl.ds((2 + h) * LANE, LANE)].astype(f32)
            x_ref[pl.ds(h, LANE, stride=4), :] = ph_c * re + ph_s * im
            x_ref[pl.ds(2 + h, LANE, stride=4), :] = ph_c * im - ph_s * re

    def scatter(r, x_ref):
        base = r * LANE
        for u in range(LANE):
            to = pl.multiple_of(place_s[base + u], 4)
            grid_rows[pl.ds(to, 4), :] = x_ref[4 * u : 4 * u + 4, :]

    if ready is not None:
        ready()
    turned(0, x_even)
    idx_copy.wait()
    total = rows // LANE

    @pl.loop(0, total // 2)
    def _(i):
        r = 2 * i
        turned(r + 1, x_odd)
        scatter(r, x_even)
        turned(jnp.minimum(r + 2, total - 1), x_even)
        scatter(r + 1, x_odd)


def own_kernel(s_own, amp, abr, k_ref, grid_rows, s_vmem, x_even, x_odd, phase, place_v, place_s, sem, sem_s):
    load = pltpu.make_async_copy(s_own, s_vmem, sem_s)
    load.start()
    spread_rows(s_vmem, amp, abr, k_ref, grid_rows, x_even, x_odd, phase, place_v, place_s, sem, load.wait)


def other_kernel(
    held, s_rem, amp, abr, k_ref, grid_rows, basis, x_even, x_odd, phase, place_v, place_s, sem
):
    bf16 = jnp.bfloat16
    spread_rows(s_rem, amp, abr, k_ref, grid_rows, x_even, x_odd, phase, place_v, place_s, sem)
    quarter = KMAX * KMAX * 4

    @pl.loop(0, KMAX * KMAX // LANE)
    def _(g):
        to = lambda n: pl.ds(pl.multiple_of((4 * g + n) * LANE, LANE), LANE)
        for h in range(2):
            vals = []
            for part in range(2):
                mm, mp, pm, pp = (
                    grid_rows[pl.ds(q * quarter + g * 4 * LANE + 2 * part + h, LANE, stride=4), :] for q in range(4)
                )
                a, b, c, d = pp + mm, pp - mm, pm + mp, pm - mp
                vals.append((a + c, c - a, b + d, b - d))
            re, im = vals
            at_re, at_im = pl.ds(2 * h * LANE, LANE), pl.ds((2 * h + 1) * LANE, LANE)
            for n in range(4):
                if n < 2:
                    basis[to(n), at_re], basis[to(n), at_im] = re[n].astype(bf16), im[n].astype(bf16)
                else:
                    basis[to(n), at_re], basis[to(n), at_im] = im[n].astype(bf16), (-re[n]).astype(bf16)


def probe_kernel(blocks, basis, near, far, cols, overlap, out, coef_even, coef_odd, tab, pots):
    f32, bf16 = jnp.float32, jnp.bfloat16
    half, column = lax.axis_index("beam"), lax.axis_index("probe")
    step = coef_even.shape[0]
    per = step // LANE

    def tables(j, source, i):
        hi = source[i, 8:9, :].astype(f32).astype(jnp.int32)
        lo = source[i, 9:10, :].astype(f32).astype(jnp.int32)
        pos = 32 * hi + lo
        width = pos.shape[1] // 4
        px = jnp.where(half == 0, pos[:, :width], pos[:, width : 2 * width])
        py = jnp.where(half == 0, pos[:, 2 * width : 3 * width], pos[:, 3 * width :])
        my = lax.broadcasted_iota(jnp.int32, (KMAX, LANE), 0)
        mx = lax.broadcasted_iota(jnp.int32, (8, LANE), 0)
        cy, sy = half_turns((2 * my + 1) * py)
        cx, sx = half_turns(jnp.where(mx < 4, 2 * mx + 1, 8) * px)
        reps = LANE // KMAX
        spread = lambda t: jnp.concatenate([jnp.broadcast_to(t[m : m + 1], (KMAX, LANE)) for m in range(reps)], 0)
        made = (
            jnp.concatenate([cy] * reps, 0), jnp.concatenate([sy] * reps, 0), spread(cx), spread(sx),
            jnp.broadcast_to(cx[4:5], (LANE, LANE)), jnp.broadcast_to(sx[4:5], (LANE, LANE)),
        )
        for n, t in enumerate(made):
            tab[n, j * LANE : (j + 1) * LANE, :] = t.T

    def coefficients(m, coef, sub=32):
        for row in range(0, step, sub):
            cy, sy, cx, sx, c4, s4 = (tab[n, m * step + row : m * step + row + sub, :] for n in range(6))
            for g in range(KMAX // 4):
                prods = (cx * cy, sx * sy, sx * cy, cx * sy)
                for n, v in enumerate(prods):
                    coef[row : row + sub, (4 * g + n) * LANE : (4 * g + n + 1) * LANE] = v.astype(bf16)
                cx, sx = cx * c4 - sx * s4, sx * c4 + cx * s4

    def prepare(m, coef):
        for j in range(m * per, (m + 1) * per):
            tables(j, near if j < blocks // 2 else far, j % (blocks // 2))
        coefficients(m, coef)

    for j in range(blocks):
        source = near if j < blocks // 2 else far
        owner = column ^ j
        pots[pl.ds(pl.multiple_of(owner * 8, 8), 8), :] = source[j % (blocks // 2), 0:8, :].astype(f32)
    mine = (cols[...] == column).astype(f32)
    left = (pots[...].T * mine).astype(bf16)
    right = pots[...].astype(bf16)
    g_re, g_im = overlap[0], overlap[1]
    mul = lambda a, b: jnp.dot(a, b, preferred_element_type=f32)
    forms = []
    for h in range(2):
        lr, li = left[h * LANE : (h + 1) * LANE], left[(2 + h) * LANE : (3 + h) * LANE]
        rr, ri = right[:, h * LANE : (h + 1) * LANE], right[:, (2 + h) * LANE : (3 + h) * LANE]
        r_re, r_im = mul(lr, rr) + mul(li, ri), mul(li, rr) - mul(lr, ri)
        h_re, h_im = g_re * r_re - g_im * r_im, g_re * r_im + g_im * r_re
        forms.append(
            jnp.concatenate([jnp.concatenate([h_re, h_im], 1), jnp.concatenate([-h_im, h_re], 1)], 0).astype(bf16)
        )

    prepare(0, coef_even)
    steps = blocks * LANE // step
    for m in range(steps):
        now, later = (coef_even, coef_odd) if m % 2 == 0 else (coef_odd, coef_even)
        psi = mul(now[...], basis[...])
        if m + 1 < steps:
            prepare(m + 1, later)
        e = 0.0
        for h in range(2):
            wave = psi[:, 2 * h * LANE : (2 * h + 2) * LANE]
            v = wave * mul(wave.astype(bf16), forms[h])
            e = e + v[:, :LANE] + v[:, LANE:]
        for i in range(per):
            j = m * per + i
            out[pl.ds(column ^ j, 1), :] = jnp.sum(e[i * LANE : (i + 1) * LANE].T, axis=0, keepdims=True)


def shards(smatrix, aperture, aberration, beam_k, probe_pos, patches, patch_col):
    f32, bf16 = jnp.float32, jnp.bfloat16
    blocks = lax.axis_size("probe")
    rows, width = smatrix.shape[0], smatrix.shape[2]
    swap = lambda v: lax.ppermute(v, "beam", [(0, 1), (1, 0)])
    s_own = smatrix.reshape(rows, width)
    s_rem = swap(s_own)
    amp_rem, abr_rem, k_rem = swap(aperture), swap(aberration), swap(beam_k)
    pos = probe_pos.reshape(1, width)
    small = jnp.concatenate(
        [patches, (pos // 32).astype(bf16), (pos % 32).astype(bf16), jnp.zeros((6, width), bf16)], 0
    )[None]
    reach = 1
    while reach < blocks:
        far = lax.ppermute(small, "probe", [(i, i ^ reach) for i in range(blocks)])
        near, reach = small, 2 * reach
        if reach < blocks:
            small = jnp.concatenate([near, far], 0)

    vmem, anyw = pl.BlockSpec(memory_space=pltpu.VMEM), pl.BlockSpec(memory_space=pl.ANY)
    params = pltpu.CompilerParams(vmem_limit_bytes=24 * 1024 * 1024)
    probes, grid = blocks * LANE, 4 * KMAX * KMAX
    turning = [
        pltpu.VMEM((4 * LANE, LANE), f32),
        pltpu.VMEM((4 * LANE, LANE), f32),
        pltpu.VMEM((2, rows // LANE, LANE), f32),
        pltpu.VMEM((1, rows), jnp.int32),
        pltpu.SMEM((rows,), jnp.int32),
        pltpu.SemaphoreType.DMA,
    ]
    tile = lambda v: v.reshape(rows // LANE, LANE)
    cost = lambda n: pl.CostEstimate(flops=n, bytes_accessed=4 * 2**20, transcendentals=0)
    held_shape = jax.ShapeDtypeStruct((4 * grid, LANE), f32)
    held = pl.pallas_call(
        own_kernel,
        out_shape=held_shape,
        in_specs=[anyw] + [vmem] * 3,
        out_specs=vmem,
        scratch_shapes=[pltpu.VMEM((rows, width), bf16)] + turning + [pltpu.SemaphoreType.DMA],
        compiler_params=params,
        cost_estimate=cost(3 * 10**9),
    )(s_own, tile(aperture), tile(aberration), beam_k)
    _, basis = pl.pallas_call(
        other_kernel,
        out_shape=(held_shape, jax.ShapeDtypeStruct((grid, width), bf16)),
        in_specs=[vmem] * 5,
        out_specs=(vmem, vmem),
        scratch_shapes=turning,
        input_output_aliases={0: 0},
        compiler_params=params,
        cost_estimate=cost(4 * 10**9),
    )(held, s_rem, tile(amp_rem), tile(abr_rem), k_rem)
    energy = pl.pallas_call(
        functools.partial(probe_kernel, blocks),
        out_shape=jax.ShapeDtypeStruct((blocks, LANE), f32),
        in_specs=[vmem] * 5,
        out_specs=vmem,
        scratch_shapes=[
            pltpu.VMEM((2 * LANE, grid), bf16),
            pltpu.VMEM((2 * LANE, grid), bf16),
            pltpu.VMEM((6, probes, LANE), f32),
            pltpu.VMEM((patch_col.shape[0], width), f32),
        ],
        compiler_params=params,
        cost_estimate=cost(6 * 10**9),
    )(basis, near, far, patch_col.reshape(1, -1), jnp.asarray(mode_overlap()))
    return lax.all_to_all(energy, "probe", 0, 0, tiled=True)


def solution(mesh):
    placed = (
        P(("grp", "beam"), "probe", None),
        P("beam"),
        P("beam"),
        P(None, "beam"),
        P(None, "probe"),
        P(("grp", "probe"), None),
        P("grp"),
    )
    return jax.shard_map(
        shards, mesh=mesh, in_specs=placed, out_specs=P("grp", ("probe", "beam")), check_vma=False
    )
```

time: 60.3 us -> 37.7 us (0.63)
  Pallas kernels: 27.4 us -> 11.9 us
  waiting for transfers between devices: 8.15 us -> 1 us
  other arithmetic: 2.86 us -> 0.81 us
  local copies, waits for them, and re-layouts: 3.37 us -> 5.07 us
    pallas_call x1 -> x3, Pallas kernels: 27.4 us -> 11.9 us  [the longest x1 5.69 us: shards(): pl.pallas_call(functools.partial(probe_kernel, blocks), out_shape=jax.Sha...]
    all_to_all x1 -> x0, waiting for transfers between devices: 8.14 us -> none  [shards(): lax.all_to_all(jnp.broadcast_to(small[None], (blocks,) + small.shape), 'p...]
    ppermute x0 -> x3, starting transfers between devices: none -> 7.25 us  [shards(): far = lax.ppermute(small, 'probe', [(i, i ^ reach) for i in range(blocks)])]
    all_to_all x1 -> x0, starting transfers between devices: 6.91 us -> none  [shards(): lax.all_to_all(jnp.broadcast_to(small[None], (blocks,) + small.shape), 'p...]
    unnamed x8 -> x14, local copies, waits for them, and re-layouts: 2.01 us -> 4.99 us
    ppermute x0 -> x3, waiting for transfers between devices: none -> 0.99 us  [shards(): far = lax.ppermute(small, 'probe', [(i, i ^ reach) for i in range(blocks)])]
    broadcast_in_dim x0 -> x1, other arithmetic: none -> 0.77 us  [shards(): jnp.concatenate([patches, (pos // 32).astype(bf16), (pos % 32).astype(bf1...]
    concatenate x2, other arithmetic: 0.75 us -> 0.02 us  [shards(): small = jnp.concatenate([near, far], 0)]
  transfers between devices with their start and end apart: 4 -> 7, of which waited for: 1 -> 1; matrix products, arithmetic and copies ran while one was open for 7% -> 4% of each run, Pallas kernels for 0% -> 17%
where the time goes in v2:
time: 37.7 us; the launch traced here: 37.2 us
  Pallas kernels  11.9 us (32%)
  blocking collectives  9.86 us (26%)
  starting transfers between devices  8.44 us (22%)
  local copies, waits for them, and re-layouts  5.07 us (13%)
  waiting for transfers between devices  1 us (3%)
  other arithmetic  0.81 us (2%)
    all_to_all x1, blocking collectives, shards(): return lax.all_to_all(energy, 'probe', 0, 0, tiled=True)  9.86 us
    ppermute x3, starting transfers between devices, shards(): far = lax.ppermute(small, 'probe', [(i, i ^ reach) for i in range(blocks)])  7.25 us
    pallas_call x1, Pallas kernels, shards(): pl.pallas_call(functools.partial(probe_kernel, blocks), out_shape=jax.Sha...  5.69 us
    unnamed x14, local copies, waits for them, and re-layouts  4.99 us
    pallas_call x1, Pallas kernels, shards(): pl.pallas_call(other_kernel, out_shape=(held_shape, jax.ShapeDtypeStruct(...  3.72 us
    pallas_call x1, Pallas kernels, shards(): pl.pallas_call(own_kernel, out_shape=held_shape, in_specs=[anyw] + [vmem]...  2.51 us
    ppermute x4, starting transfers between devices, shards(): swap = lambda v: lax.ppermute(v, 'beam', [(0, 1), (1, 0)])  1.19 us
    ppermute x3, waiting for transfers between devices, shards(): far = lax.ppermute(small, 'probe', [(i, i ^ reach) for i in range(blocks)])  0.99 us
  transfers between devices with their start and end apart: 7, of which 1 were waited for; matrix products, arithmetic and copies ran while one was open for 4% of the time, Pallas kernels for 17%

profile of v2, /device:TPU:0, one launch (start us, length us, event | category | flops | bytes accessed | tf_op | source)
XLA Modules:
  0.0 37.2 jit_solution(4828461767230891732)
XLA Ops:
  0.0 0.5 %collective-permute-start = (bf16[2048,512]{1,0:T(8,128)(2,1)}, bf16[2048,512]{1,0:T(8,128)(2,1)S(1)}, u32[]{:S(2)}, u32[]{:S(2)}) collective-permute-start(bf16[2048,512]{1,0:T(8,128)(2,1)} %bitcast.16), channel_id=1, source_target_pairs={{0,1},{1,0},{2,3},{3,2},{4,5},{5,4},{6,7},{7,6},{8,9},{9,8},{10,11... | collective-permute-start | bytes 6291464 | tf_op jit(solution)/shard_map/ppermute | solution.py:203
  0.5 0.7 %copy.11 = s32[1,1,2,256]{3,1,2,0:T(1,128)S(1)} copy(s32[1,1,2,256]{3,2,1,0:T(2,128)} %bitcast.25) | data formatting | bytes 4096
  1.1 0.1 pad.8.clone
  1.3 0.8 %maximum_bitcast_fusion = bf16[1,16,512]{2,1,0:T(8,128)(2,1)S(1)} fusion(bf16[1,512]{1,0:T(2,128)(2,1)S(1)} %fusion, bf16[1,512]{1,0:T(2,128)(2,1)S(1)} %get-tuple-element.7, bf16[8,512]{1,0:T(8,128)(2,1)} %param.13, bf16[16]{0:T(256)(128)(2,1)S(1)} %pad.8.clone), kind=kLoop, calls=%fused_computation.2 | loop fusion | flops 65536 | bytes 26656 | tf_op jit(solution)/shard_map/broadcast_in_dim | solution.py:208
  2.0 2.5 %collective-permute-start.4 = (bf16[1,16,512]{2,1,0:T(8,128)(2,1)S(1)}, bf16[1,16,512]{2,1,0:T(8,128)(2,1)S(1)}, u32[]{:S(2)}, u32[]{:S(2)}) collective-permute-start(bf16[1,16,512]{2,1,0:T(8,128)(2,1)S(1)} %maximum_bitcast_fusion), channel_id=1, source_target_pairs={{0,2},{2,0},{4,6},{6,4},{8,10},{10,8},{12,14},{14,12},{1,3},{3,1},... | collective-permute-start | bytes 49160 | tf_op jit(solution)/shard_map/ppermute | solution.py:213
  4.6 0.2 collective-permute-start.1
  4.8 0.3 collective-permute-start.2
  5.1 0.2 collective-permute-start.3
  5.3 1.0 %collective-permute-done.4 = bf16[1,16,512]{2,1,0:T(8,128)(2,1)S(1)} collective-permute-done((bf16[1,16,512]{2,1,0:T(8,128)(2,1)S(1)}, bf16[1,16,512]{2,1,0:T(8,128)(2,1)S(1)}, u32[]{:S(2)}, u32[]{:S(2)}) %collective-permute-start.4) | collective-permute-done | bytes 16416 | tf_op jit(solution)/shard_map/ppermute | solution.py:213
  6.3 2.1 %collective-permute-start.5 = (bf16[2,16,512]{2,1,0:T(8,128)(2,1)S(1)}, bf16[2,16,512]{2,1,0:T(8,128)(2,1)S(1)}, u32[]{:S(2)}, u32[]{:S(2)}) collective-permute-start(bf16[2,16,512]{2,1,0:T(8,128)(2,1)S(1)} %pad_maximum_fusion.1), channel_id=1, source_target_pairs={{0,4},{2,6},{4,0},{6,2},{8,12},{10,14},{12,8},{14,10},{1,5},{3,7},... | collective-permute-start | bytes 98312 | tf_op jit(solution)/shard_map/ppermute | solution.py:213
  8.4 0.0 copy-start
  8.4 1.6 %copy-done = bf16[2048,1,512]{2,0,1:T(8,128)(2,1)S(1)} copy-done((bf16[2048,1,512]{2,0,1:T(8,128)(2,1)S(1)}, bf16[2048,1,512]{2,0,1:T(8,128)(2,1)}, u32[]{:S(2)}) %copy-start) | copy-done | bytes 2097176
  9.9 0.0 copy-start.1
  9.9 0.7 %copy-done.1 = s32[2,2048]{1,0:T(2,128)S(1)} copy-done((s32[2,2048]{1,0:T(2,128)S(1)}, s32[2,2048]{1,0:T(2,128)}, u32[]{:S(2)}) %copy-start.1) | copy-done | bytes 16408
  10.7 0.0 copy-start.2
  10.7 0.7 %copy-done.2 = f32[2048]{0:T(1024)S(1)} copy-done((f32[2048]{0:T(1024)S(1)}, f32[2048]{0:T(1024)}, u32[]{:S(2)}) %copy-start.2) | copy-done | bytes 8216
  11.4 0.0 copy-start.3
  11.4 0.7 %copy-done.3 = f32[2048]{0:T(1024)S(1)} copy-done((f32[2048]{0:T(1024)S(1)}, f32[2048]{0:T(1024)}, u32[]{:S(2)}) %copy-start.3) | copy-done | bytes 8216
  12.1 2.5 %shard_map.82.held = f32[16384,128]{1,0:T(8,128)S(1)} custom-call(bf16[2048,512]{1,0:T(8,128)(2,1)S(1)} %bitcast.17, f32[16,128]{1,0:T(8,128)S(1)} %bitcast.18, f32[16,128]{1,0:T(8,128)S(1)} %bitcast.19, s32[2,2048]{1,0:T(2,128)S(1)} %copy-done.1), custom_call_target="tpu_custom_call" | custom-call | flops 3000000000 | bytes 4194304 | tf_op jit(solution)/shard_map/pallas_call | solution.py:232
  14.6 0.0 collective-permute-done.5
  14.6 2.7 %collective-permute-start.6 = (bf16[4,16,512]{2,1,0:T(8,128)(2,1)S(1)}, bf16[4,16,512]{2,1,0:T(8,128)(2,1)S(1)}, u32[]{:S(2)}, u32[]{:S(2)}) collective-permute-start(bf16[4,16,512]{2,1,0:T(8,128)(2,1)S(1)} %pad_maximum_fusion.near), channel_id=1, source_target_pairs={{0,8},{2,10},{4,12},{6,14},{8,0},{10,2},{12,4},{14,6},{1,9},{3,11}... | collective-permute-start | bytes 196616 | tf_op jit(solution)/shard_map/ppermute | solution.py:213
  17.3 0.0 collective-permute-done.1
  17.3 0.0 collective-permute-done.2
  17.3 0.0 collective-permute-done.3.k_ref
  17.3 0.0 collective-permute-done.s_rem
  17.3 0.0 copy-start.4
  17.3 0.0 copy-start.5
  17.3 3.7 %shard_map.83 = (f32[16384,128]{1,0:T(8,128)S(1)}, bf16[4096,512]{1,0:T(8,128)(2,1)S(1)}) custom-call(f32[16384,128]{1,0:T(8,128)S(1)} %shard_map.82.held, bf16[2048,512]{1,0:T(8,128)(2,1)S(1)} %collective-permute-done.s_rem, f32[16,128]{1,0:T(8,128)S(1)} %bitcast.20, f32[16,128]{1,0:T(8,128)S(1)} %bitcast.21, ...), custom_call_target="tpu_custom_call", output_to_operand_aliasing={{0}: (0, {})} | custom-call | flops 4000000000 | bytes 4194304 | tf_op jit(solution)/shard_map/pallas_call | solution.py:241
  21.0 0.0 collective-permute-done.6.far
  21.0 0.0 copy-done.4
  21.1 0.0 copy-done.5
  21.1 5.7 %shard_map.84 = f32[8,128]{1,0:T(8,128)S(1)} custom-call(bf16[4096,512]{1,0:T(8,128)(2,1)S(1)} %get-tuple-element.6.basis, bf16[4,16,512]{2,1,0:T(8,128)(2,1)S(1)} %pad_maximum_fusion.near, bf16[4,16,512]{2,1,0:T(8,128)(2,1)S(1)} %collective-permute-done.6.far, s32[1,64]{1,0:T(1,128)S(1)} %bitcast.22, f32[2,128,128]{2,1,0:T(8,128)S(1)} %copy-done.5), custom_call_target="tpu_custom_call" | custom-call | flops 6000000000 | bytes 4194304 | tf_op jit(solution)/shard_map/pallas_call | solution.py:251
  26.8 9.9 %all_to_all.12 = f32[8,1,128]{2,1,0:T(1,128)S(1)} all-to-all(f32[8,1,128]{2,1,0:T(1,128)S(1)} %bitcast.15), channel_id=1, replica_groups=mesh['grp'=2,'probe'=8,'beam'=2] {'probe'}, dimensions={0} | all-to-all | bytes 8192 | tf_op jit(solution)/shard_map/all_to_all | solution.py:265
  36.6 0.6 %copy.14 = f32[8,128]{1,0:T(8,128)} copy(f32[8,128]{1,0:T(8,128)S(1)} %bitcast.23) | data formatting | bytes 8192
  (5 shorter events, 0.0 us)
Async XLA Ops:
  0.0 17.3 %collective-permute-start = (bf16[2048,512]{1,0:T(8,128)(2,1)}, bf16[2048,512]{1,0:T(8,128)(2,1)S(1)}, u32[]{:S(2)}, u32[]{:S(2)}) collective-permute-start(bf16[2048,512]{1,0:T(8,128)(2,1)} %bitcast.16), channel_id=1, source_target_pairs={{0,1},{1,0},{2,3},{3,2},{4,5},{5,4},{6,7},{7,6},{8,9},{9,8},{10,11... | collective-permute-start | bytes 6291464 | tf_op jit(solution)/shard_map/ppermute | solution.py:203
  2.0 4.2 %collective-permute-start.4 = (bf16[1,16,512]{2,1,0:T(8,128)(2,1)S(1)}, bf16[1,16,512]{2,1,0:T(8,128)(2,1)S(1)}, u32[]{:S(2)}, u32[]{:S(2)}) collective-permute-start(bf16[1,16,512]{2,1,0:T(8,128)(2,1)S(1)} %maximum_bitcast_fusion), channel_id=1, source_target_pairs={{0,2},{2,0},{4,6},{6,4},{8,10},{10,8},{12,14},{14,12},{1,3},{3,1},... | collective-permute-start | bytes 49160 | tf_op jit(solution)/shard_map/ppermute | solution.py:213
  4.6 12.7 %collective-permute-start.1 = (f32[2048]{0:T(1024)}, f32[2048]{0:T(1024)S(1)}, u32[]{:S(2)}, u32[]{:S(2)}) collective-permute-start(f32[2048]{0:T(1024)} %param.9), channel_id=1, source_target_pairs={{0,1},{1,0},{2,3},{3,2},{4,5},{5,4},{6,7},{7,6},{8,9},{9,8},{10,11... | collective-permute-start | bytes 24584 | tf_op jit(solution)/shard_map/ppermute | solution.py:203
  4.8 12.5 %collective-permute-start.2 = (f32[2048]{0:T(1024)}, f32[2048]{0:T(1024)S(1)}, u32[]{:S(2)}, u32[]{:S(2)}) collective-permute-start(f32[2048]{0:T(1024)} %param.10), channel_id=1, source_target_pairs={{0,1},{1,0},{2,3},{3,2},{4,5},{5,4},{6,7},{7,6},{8,9},{9,8},{10,11... | collective-permute-start | bytes 24584 | tf_op jit(solution)/shard_map/ppermute | solution.py:203
  5.1 12.2 %collective-permute-start.3 = (s32[2,2048]{1,0:T(2,128)}, s32[2,2048]{1,0:T(2,128)S(1)}, u32[]{:S(2)}, u32[]{:S(2)}) collective-permute-start(s32[2,2048]{1,0:T(2,128)} %k_ref.1), channel_id=1, source_target_pairs={{0,1},{1,0},{2,3},{3,2},{4,5},{5,4},{6,7},{7,6},{8,9},{9,8},{10,11... | collective-permute-start | bytes 49160 | tf_op jit(solution)/shard_map/ppermute | solution.py:203
  6.3 8.3 %collective-permute-start.5 = (bf16[2,16,512]{2,1,0:T(8,128)(2,1)S(1)}, bf16[2,16,512]{2,1,0:T(8,128)(2,1)S(1)}, u32[]{:S(2)}, u32[]{:S(2)}) collective-permute-start(bf16[2,16,512]{2,1,0:T(8,128)(2,1)S(1)} %pad_maximum_fusion.1), channel_id=1, source_target_pairs={{0,4},{2,6},{4,0},{6,2},{8,12},{10,14},{12,8},{14,10},{1,5},{3,7},... | collective-permute-start | bytes 98312 | tf_op jit(solution)/shard_map/ppermute | solution.py:213
  8.4 1.6 %copy-start = (bf16[2048,1,512]{2,0,1:T(8,128)(2,1)S(1)}, bf16[2048,1,512]{2,0,1:T(8,128)(2,1)}, u32[]{:S(2)}) copy-start(bf16[2048,1,512]{2,0,1:T(8,128)(2,1)} %param.8) | copy-start | bytes 6291460
  9.9 0.7 %copy-start.1 = (s32[2,2048]{1,0:T(2,128)S(1)}, s32[2,2048]{1,0:T(2,128)}, u32[]{:S(2)}) copy-start(s32[2,2048]{1,0:T(2,128)} %k_ref.1) | copy-start | bytes 49156
  10.7 0.7 %copy-start.2 = (f32[2048]{0:T(1024)S(1)}, f32[2048]{0:T(1024)}, u32[]{:S(2)}) copy-start(f32[2048]{0:T(1024)} %param.9) | copy-start | bytes 24580
  11.4 0.7 %copy-start.3 = (f32[2048]{0:T(1024)S(1)}, f32[2048]{0:T(1024)}, u32[]{:S(2)}) copy-start(f32[2048]{0:T(1024)} %param.10) | copy-start | bytes 24580
  14.6 6.4 %collective-permute-start.6 = (bf16[4,16,512]{2,1,0:T(8,128)(2,1)S(1)}, bf16[4,16,512]{2,1,0:T(8,128)(2,1)S(1)}, u32[]{:S(2)}, u32[]{:S(2)}) collective-permute-start(bf16[4,16,512]{2,1,0:T(8,128)(2,1)S(1)} %pad_maximum_fusion.near), channel_id=1, source_target_pairs={{0,8},{2,10},{4,12},{6,14},{8,0},{10,2},{12,4},{14,6},{1,9},{3,11}... | collective-permute-start | bytes 196616 | tf_op jit(solution)/shard_map/ppermute | solution.py:213
  17.3 3.8 %copy-start.4 = (s32[64]{0:T(128)S(1)}, s32[64]{0:T(128)}, u32[]{:S(2)}) copy-start(s32[64]{0:T(128)} %param.14) | copy-start | bytes 772
  17.3 3.8 %copy-start.5 = (f32[2,128,128]{2,1,0:T(8,128)S(1)}, f32[2,128,128]{2,1,0:T(8,128)}, u32[]{:S(2)}) copy-start(f32[2,128,128]{2,1,0:T(8,128)} %constant.32.clone.overlap) | copy-start | bytes 393220

commit v3 on v2

--- a/solution.py
+++ b/solution.py
@@ -47,7 +47,7 @@
     place_v[...] = ((quad * KMAX + mx) * KMAX + my) * 4
 
 
-def spread_rows(s_ref, amp, abr, k_ref, grid_rows, x_even, x_odd, phase, place_v, place_s, sem, ready=None):
+def spread_rows(s_ref, amp, abr, k_ref, grid_rows, x_even, x_odd, phase, place_v, place_s, sem, ready=(None,)):
     f32 = jnp.float32
     rows = s_ref.shape[0]
     place_rows(k_ref, place_v)
@@ -72,25 +72,37 @@
             to = pl.multiple_of(place_s[base + u], 4)
             grid_rows[pl.ds(to, 4), :] = x_ref[4 * u : 4 * u + 4, :]
 
-    if ready is not None:
-        ready()
-    turned(0, x_even)
-    idx_copy.wait()
-    total = rows // LANE
-
-    @pl.loop(0, total // 2)
-    def _(i):
-        r = 2 * i
-        turned(r + 1, x_odd)
-        scatter(r, x_even)
-        turned(jnp.minimum(r + 2, total - 1), x_even)
-        scatter(r + 1, x_odd)
-
-
-def own_kernel(s_own, amp, abr, k_ref, grid_rows, s_vmem, x_even, x_odd, phase, place_v, place_s, sem, sem_s):
-    load = pltpu.make_async_copy(s_own, s_vmem, sem_s)
-    load.start()
-    spread_rows(s_vmem, amp, abr, k_ref, grid_rows, x_even, x_odd, phase, place_v, place_s, sem, load.wait)
+    part = rows // LANE // len(ready)
+    for n, wait in enumerate(ready):
+        first, last = n * part, (n + 1) * part - 1
+        if wait is not None:
+            wait()
+        turned(first, x_even)
+        if n == 0:
+            idx_copy.wait()
+
+        @pl.loop(first // 2, (last + 1) // 2)
+        def _(i):
+            r = 2 * i
+            turned(r + 1, x_odd)
+            scatter(r, x_even)
+            turned(jnp.minimum(r + 2, last), x_even)
+            scatter(r + 1, x_odd)
+
+
+def own_kernel(
+    s_own, amp, abr, k_ref, grid_rows, s_vmem, amp_v, abr_v, k_v, x_even, x_odd, phase, place_v, place_s, sem, sems
+):
+    rows = s_vmem.shape[0]
+    chunks = [pl.ds(n * (rows // 2), rows // 2) for n in range(2)]
+    pairs = [(k_ref, k_v), (amp, amp_v), (abr, abr_v)] + [(s_own.at[c], s_vmem.at[c]) for c in chunks]
+    copies = [pltpu.make_async_copy(src, dst, sems.at[n]) for n, (src, dst) in enumerate(pairs)]
+    for c in copies:
+        c.start()
+    for c in copies[:3]:
+        c.wait()
+    ready = [c.wait for c in copies[3:]]
+    spread_rows(s_vmem, amp_v, abr_v, k_v, grid_rows, x_even, x_odd, phase, place_v, place_s, sem, ready)
 
 
 def other_kernel(
@@ -120,19 +132,18 @@
                     basis[to(n), at_re], basis[to(n), at_im] = im[n].astype(bf16), (-re[n]).astype(bf16)
 
 
-def probe_kernel(blocks, basis, near, far, cols, overlap, out, coef_even, coef_odd, tab, pots):
+def waves(source, basis, coef_even, coef_odd, tab, emit):
     f32, bf16 = jnp.float32, jnp.bfloat16
-    half, column = lax.axis_index("beam"), lax.axis_index("probe")
-    step = coef_even.shape[0]
+    half = lax.axis_index("beam")
+    blocks, step = source.shape[0], coef_even.shape[0]
     per = step // LANE
 
-    def tables(j, source, i):
-        hi = source[i, 8:9, :].astype(f32).astype(jnp.int32)
-        lo = source[i, 9:10, :].astype(f32).astype(jnp.int32)
-        pos = 32 * hi + lo
-        width = pos.shape[1] // 4
-        px = jnp.where(half == 0, pos[:, :width], pos[:, width : 2 * width])
-        py = jnp.where(half == 0, pos[:, 2 * width : 3 * width], pos[:, 3 * width :])
+    def tables(j):
+        pos = source[j, 8:10, :].astype(f32).astype(jnp.int32)
+        width = pos.shape[1] // 2
+        pos = 32 * pos[:, :width] + pos[:, width:]
+        pos = jnp.where(half == 0, pos[:, :LANE], pos[:, LANE:])
+        px, py = pos[0:1], pos[1:2]
         my = lax.broadcasted_iota(jnp.int32, (KMAX, LANE), 0)
         mx = lax.broadcasted_iota(jnp.int32, (8, LANE), 0)
         cy, sy = half_turns((2 * my + 1) * py)
@@ -157,13 +168,37 @@
 
     def prepare(m, coef):
         for j in range(m * per, (m + 1) * per):
-            tables(j, near if j < blocks // 2 else far, j % (blocks // 2))
+            tables(j)
         coefficients(m, coef)
 
-    for j in range(blocks):
-        source = near if j < blocks // 2 else far
-        owner = column ^ j
-        pots[pl.ds(pl.multiple_of(owner * 8, 8), 8), :] = source[j % (blocks // 2), 0:8, :].astype(f32)
+    prepare(0, coef_even)
+    steps = blocks // per
+    for m in range(steps):
+        now, later = (coef_even, coef_odd) if m % 2 == 0 else (coef_odd, coef_even)
+        psi = jnp.dot(now[...], basis[...], preferred_element_type=f32)
+        if m + 1 < steps:
+            prepare(m + 1, later)
+        emit(m, psi)
+
+
+def near_kernel(basis, near, psi_near, coef_even, coef_odd, tab):
+    step = coef_even.shape[0]
+
+    def emit(m, psi):
+        psi_near[m * step : (m + 1) * step, :] = psi
+
+    waves(near, basis, coef_even, coef_odd, tab, emit)
+
+
+def far_kernel(basis, psi_near, near, far, cols, overlap, out, coef_even, coef_odd, tab, pots):
+    f32, bf16 = jnp.float32, jnp.bfloat16
+    column = lax.axis_index("probe")
+    step = coef_even.shape[0]
+    blocks = near.shape[0]
+    for n, source in enumerate((near, far)):
+        for j in range(blocks):
+            owner = column ^ (n * blocks + j)
+            pots[pl.ds(pl.multiple_of(owner * 8, 8), 8), :] = source[j, 0:8, :].astype(f32)
     mine = (cols[...] == column).astype(f32)
     left = (pots[...].T * mine).astype(bf16)
     right = pots[...].astype(bf16)
@@ -179,21 +214,20 @@
             jnp.concatenate([jnp.concatenate([h_re, h_im], 1), jnp.concatenate([-h_im, h_re], 1)], 0).astype(bf16)
         )
 
-    prepare(0, coef_even)
-    steps = blocks * LANE // step
-    for m in range(steps):
-        now, later = (coef_even, coef_odd) if m % 2 == 0 else (coef_odd, coef_even)
-        psi = mul(now[...], basis[...])
-        if m + 1 < steps:
-            prepare(m + 1, later)
+    def energy(first, psi):
         e = 0.0
         for h in range(2):
             wave = psi[:, 2 * h * LANE : (2 * h + 2) * LANE]
             v = wave * mul(wave.astype(bf16), forms[h])
             e = e + v[:, :LANE] + v[:, LANE:]
-        for i in range(per):
-            j = m * per + i
-            out[pl.ds(column ^ j, 1), :] = jnp.sum(e[i * LANE : (i + 1) * LANE].T, axis=0, keepdims=True)
+        for i in range(step // LANE):
+            out[pl.ds(column ^ (first + i), 1), :] = jnp.sum(e[i * LANE : (i + 1) * LANE].T, axis=0, keepdims=True)
+
+    def emit(m, psi):
+        energy(blocks + m * step // LANE, psi)
+        energy(m * step // LANE, psi_near[m * step : (m + 1) * step, :])
+
+    waves(far, basis, coef_even, coef_odd, tab, emit)
 
 
 def shards(smatrix, aperture, aberration, beam_k, probe_pos, patches, patch_col):
@@ -204,10 +238,8 @@
     s_own = smatrix.reshape(rows, width)
     s_rem = swap(s_own)
     amp_rem, abr_rem, k_rem = swap(aperture), swap(aberration), swap(beam_k)
-    pos = probe_pos.reshape(1, width)
-    small = jnp.concatenate(
-        [patches, (pos // 32).astype(bf16), (pos % 32).astype(bf16), jnp.zeros((6, width), bf16)], 0
-    )[None]
+    pos = jnp.concatenate([probe_pos // 32, probe_pos % 32], 1).astype(bf16)
+    small = jnp.concatenate([patches, pos, jnp.zeros((6, width), bf16)], 0)[None]
     reach = 1
     while reach < blocks:
         far = lax.ppermute(small, "probe", [(i, i ^ reach) for i in range(blocks)])
@@ -215,29 +247,38 @@
         if reach < blocks:
             small = jnp.concatenate([near, far], 0)
 
-    vmem, anyw = pl.BlockSpec(memory_space=pltpu.VMEM), pl.BlockSpec(memory_space=pl.ANY)
+    vmem = pl.BlockSpec(memory_space=pltpu.VMEM)
     params = pltpu.CompilerParams(vmem_limit_bytes=24 * 1024 * 1024)
-    probes, grid = blocks * LANE, 4 * KMAX * KMAX
+    grid = 4 * KMAX * KMAX
+    lines = rows // LANE
     turning = [
         pltpu.VMEM((4 * LANE, LANE), f32),
         pltpu.VMEM((4 * LANE, LANE), f32),
-        pltpu.VMEM((2, rows // LANE, LANE), f32),
+        pltpu.VMEM((2, lines, LANE), f32),
         pltpu.VMEM((1, rows), jnp.int32),
         pltpu.SMEM((rows,), jnp.int32),
         pltpu.SemaphoreType.DMA,
     ]
-    tile = lambda v: v.reshape(rows // LANE, LANE)
+    tile = lambda v: v.reshape(lines, LANE)
     cost = lambda n: pl.CostEstimate(flops=n, bytes_accessed=4 * 2**20, transcendentals=0)
     held_shape = jax.ShapeDtypeStruct((4 * grid, LANE), f32)
+    hbm = pl.BlockSpec(memory_space=pltpu.HBM)
     held = pl.pallas_call(
         own_kernel,
         out_shape=held_shape,
-        in_specs=[anyw] + [vmem] * 3,
+        in_specs=[hbm] * 4,
         out_specs=vmem,
-        scratch_shapes=[pltpu.VMEM((rows, width), bf16)] + turning + [pltpu.SemaphoreType.DMA],
+        scratch_shapes=[
+            pltpu.VMEM((rows, width), bf16),
+            pltpu.VMEM((lines, LANE), f32),
+            pltpu.VMEM((lines, LANE), f32),
+            pltpu.VMEM((2, rows), jnp.int32),
+        ]
+        + turning
+        + [pltpu.SemaphoreType.DMA((5,))],
         compiler_params=params,
         cost_estimate=cost(3 * 10**9),
-    )(s_own, tile(aperture), tile(aberration), beam_k)
+    )(*(pltpu.with_memory_space_constraint(v, pltpu.HBM) for v in (s_own, tile(aperture), tile(aberration), beam_k)))
     _, basis = pl.pallas_call(
         other_kernel,
         out_shape=(held_shape, jax.ShapeDtypeStruct((grid, width), bf16)),
@@ -248,20 +289,30 @@
         compiler_params=params,
         cost_estimate=cost(4 * 10**9),
     )(held, s_rem, tile(amp_rem), tile(abr_rem), k_rem)
+    probes = blocks // 2 * LANE
+    working = [
+        pltpu.VMEM((2 * LANE, grid), bf16),
+        pltpu.VMEM((2 * LANE, grid), bf16),
+        pltpu.VMEM((6, probes, LANE), f32),
+    ]
+    psi_near = pl.pallas_call(
+        near_kernel,
+        out_shape=jax.ShapeDtypeStruct((probes, width), f32),
+        in_specs=[vmem] * 2,
+        out_specs=vmem,
+        scratch_shapes=working,
+        compiler_params=params,
+        cost_estimate=cost(4 * 10**9),
+    )(basis, near)
     energy = pl.pallas_call(
-        functools.partial(probe_kernel, blocks),
+        far_kernel,
         out_shape=jax.ShapeDtypeStruct((blocks, LANE), f32),
-        in_specs=[vmem] * 5,
+        in_specs=[vmem] * 6,
         out_specs=vmem,
-        scratch_shapes=[
-            pltpu.VMEM((2 * LANE, grid), bf16),
-            pltpu.VMEM((2 * LANE, grid), bf16),
-            pltpu.VMEM((6, probes, LANE), f32),
-            pltpu.VMEM((patch_col.shape[0], width), f32),
-        ],
+        scratch_shapes=working + [pltpu.VMEM((patch_col.shape[0], width), f32)],
         compiler_params=params,
-        cost_estimate=cost(6 * 10**9),
-    )(basis, near, far, patch_col.reshape(1, -1), jnp.asarray(mode_overlap()))
+        cost_estimate=cost(4 * 10**9),
+    )(basis, psi_near, near, far, patch_col.reshape(1, -1), jnp.asarray(mode_overlap()))
     return lax.all_to_all(energy, "probe", 0, 0, tiled=True)
 
 

time: 37.7 us -> 34.1 us (0.905)
  local copies, waits for them, and re-layouts: 5.07 us -> 0.69 us
  Pallas kernels: 11.9 us -> 12.8 us
  blocking collectives: 9.86 us -> 9.15 us
  other arithmetic: 0.81 us -> 1.48 us
    unnamed x14 -> x5, local copies, waits for them, and re-layouts: 4.99 us -> 0.61 us
    pallas_call x2 -> x3, Pallas kernels: 8.2 us -> 9.12 us  [the longest x1 3.25 us: shards(): pl.pallas_call(far_kernel, out_shape=jax.ShapeDtypeStruct((blocks, LANE),...]
    all_to_all x1, blocking collectives: 9.86 us -> 9.15 us  [shards(): return lax.all_to_all(energy, 'probe', 0, 0, tiled=True)]
    another operation x0 -> x1, other arithmetic: none -> 0.69 us
  transfers between devices with their start and end apart: 7 -> 7, of which waited for: 1 -> 1; matrix products, arithmetic and copies ran while one was open for 4% -> 5% of each run, Pallas kernels for 17% -> 28%
where the time goes in v3:
time: 34.1 us; the launch traced here: 33.7 us
  Pallas kernels  12.8 us (38%)
  blocking collectives  9.15 us (27%)
  starting transfers between devices  8.44 us (25%)
  other arithmetic  1.48 us (4%)
  waiting for transfers between devices  1 us (3%)
  local copies, waits for them, and re-layouts  0.69 us (2%)
    all_to_all x1, blocking collectives, shards(): return lax.all_to_all(energy, 'probe', 0, 0, tiled=True)  9.15 us
    ppermute x3, starting transfers between devices, shards(): far = lax.ppermute(small, 'probe', [(i, i ^ reach) for i in range(blocks)])  7.25 us
    pallas_call x1, Pallas kernels, shards(): pl.pallas_call(other_kernel, out_shape=(held_shape, jax.ShapeDtypeStruct(...  3.72 us
    pallas_call x1, Pallas kernels, shards(): pl.pallas_call(far_kernel, out_shape=jax.ShapeDtypeStruct((blocks, LANE),...  3.25 us
    pallas_call x1, Pallas kernels, shards(): pl.pallas_call(own_kernel, out_shape=held_shape, in_specs=[hbm] * 4, out_...  3.23 us
    pallas_call x1, Pallas kernels, shards(): pl.pallas_call(near_kernel, out_shape=jax.ShapeDtypeStruct((probes, width...  2.64 us
    ppermute x4, starting transfers between devices, shards(): swap = lambda v: lax.ppermute(v, 'beam', [(0, 1), (1, 0)])  1.19 us
    ppermute x3, waiting for transfers between devices, shards(): far = lax.ppermute(small, 'probe', [(i, i ^ reach) for i in range(blocks)])  0.99 us
  transfers between devices with their start and end apart: 7, of which 1 were waited for; matrix products, arithmetic and copies ran while one was open for 5% of the time, Pallas kernels for 28%

profile of v3, /device:TPU:0, one launch (start us, length us, event | category | flops | bytes accessed | tf_op | source)
XLA Modules:
  0.0 33.7 jit_solution(9603325269826898899)
XLA Ops:
  0.0 0.5 %collective-permute-start = (bf16[2048,512]{1,0:T(8,128)(2,1)}, bf16[2048,512]{1,0:T(8,128)(2,1)S(1)}, u32[]{:S(2)}, u32[]{:S(2)}) collective-permute-start(bf16[2048,512]{1,0:T(8,128)(2,1)} %bitcast.17), channel_id=1, source_target_pairs={{0,1},{1,0},{2,3},{3,2},{4,5},{5,4},{6,7},{7,6},{8,9},{9,8},{10,11... | collective-permute-start | bytes 6291464 | tf_op jit(solution)/shard_map/ppermute | solution.py:237
  0.5 0.1 pad.8.clone
  0.5 0.7 %fusion.1 = (bf16[2,256]{1,0:T(2,128)(2,1)S(1)}, bf16[2,256]{1,0:T(2,128)(2,1)S(1)}) fusion(s32[2,256]{1,0:T(2,128)} %param.12), kind=kLoop, calls=%fused_computation.9 | loop fusion | flops 10752 | bytes 4096 | tf_op jit(solution)/shard_map/convert
  1.2 0.8 %maximum_bitcast_fusion = bf16[1,16,512]{2,1,0:T(8,128)(2,1)S(1)} fusion(bf16[2,256]{1,0:T(2,128)(2,1)S(1)} %get-tuple-element.8, bf16[2,256]{1,0:T(2,128)(2,1)S(1)} %get-tuple-element.7, bf16[8,512]{1,0:T(8,128)(2,1)} %param.13, bf16[16]{0:T(256)(128)(2,1)S(1)} %pad.8.clone), kind=kLoop, calls=%fused_computation.2 | loop fusion | flops 65536 | bytes 26656 | tf_op jit(solution)/shard_map/broadcast_in_dim | solution.py:242
  2.0 2.5 %collective-permute-start.4 = (bf16[1,16,512]{2,1,0:T(8,128)(2,1)S(1)}, bf16[1,16,512]{2,1,0:T(8,128)(2,1)S(1)}, u32[]{:S(2)}, u32[]{:S(2)}) collective-permute-start(bf16[1,16,512]{2,1,0:T(8,128)(2,1)S(1)} %maximum_bitcast_fusion), channel_id=1, source_target_pairs={{0,2},{2,0},{4,6},{6,4},{8,10},{10,8},{12,14},{14,12},{1,3},{3,1},... | collective-permute-start | bytes 49160 | tf_op jit(solution)/shard_map/ppermute | solution.py:245
  4.5 0.2 collective-permute-start.1
  4.8 0.3 collective-permute-start.2
  5.0 0.2 collective-permute-start.3
  5.3 1.0 %collective-permute-done.4 = bf16[1,16,512]{2,1,0:T(8,128)(2,1)S(1)} collective-permute-done((bf16[1,16,512]{2,1,0:T(8,128)(2,1)S(1)}, bf16[1,16,512]{2,1,0:T(8,128)(2,1)S(1)}, u32[]{:S(2)}, u32[]{:S(2)}) %collective-permute-start.4) | collective-permute-done | bytes 16416 | tf_op jit(solution)/shard_map/ppermute | solution.py:245
  6.3 2.1 %collective-permute-start.5 = (bf16[2,16,512]{2,1,0:T(8,128)(2,1)S(1)}, bf16[2,16,512]{2,1,0:T(8,128)(2,1)S(1)}, u32[]{:S(2)}, u32[]{:S(2)}) collective-permute-start(bf16[2,16,512]{2,1,0:T(8,128)(2,1)S(1)} %pad_maximum_fusion.1), channel_id=1, source_target_pairs={{0,4},{2,6},{4,0},{6,2},{8,12},{10,14},{12,8},{14,10},{1,5},{3,7},... | collective-permute-start | bytes 98312 | tf_op jit(solution)/shard_map/ppermute | solution.py:245
  8.3 3.2 %shard_map.82.held = f32[16384,128]{1,0:T(8,128)S(1)} custom-call(bf16[2048,512]{1,0:T(8,128)(2,1)} %bitcast.18, f32[16,128]{1,0:T(8,128)} %bitcast.19, f32[16,128]{1,0:T(8,128)} %bitcast.20, s32[2,2048]{1,0:T(2,128)} %k_ref.1), custom_call_target="tpu_custom_call" | custom-call | flops 3000000000 | bytes 4194304 | tf_op jit(solution)/shard_map/pallas_call | solution.py:266
  11.6 0.0 collective-permute-done.5
  11.6 2.7 %collective-permute-start.6 = (bf16[4,16,512]{2,1,0:T(8,128)(2,1)S(1)}, bf16[4,16,512]{2,1,0:T(8,128)(2,1)S(1)}, u32[]{:S(2)}, u32[]{:S(2)}) collective-permute-start(bf16[4,16,512]{2,1,0:T(8,128)(2,1)S(1)} %pad_maximum_fusion.near), channel_id=1, source_target_pairs={{0,8},{2,10},{4,12},{6,14},{8,0},{10,2},{12,4},{14,6},{1,9},{3,11}... | collective-permute-start | bytes 196616 | tf_op jit(solution)/shard_map/ppermute | solution.py:245
  14.3 0.0 collective-permute-done.1
  14.3 0.0 collective-permute-done.2
  14.3 0.0 collective-permute-done.3.k_ref
  14.3 0.0 collective-permute-done.s_rem
  14.3 3.7 %shard_map.83 = (f32[16384,128]{1,0:T(8,128)S(1)}, bf16[4096,512]{1,0:T(8,128)(2,1)S(1)}) custom-call(f32[16384,128]{1,0:T(8,128)S(1)} %shard_map.82.held, bf16[2048,512]{1,0:T(8,128)(2,1)S(1)} %collective-permute-done.s_rem, f32[16,128]{1,0:T(8,128)S(1)} %bitcast.13, f32[16,128]{1,0:T(8,128)S(1)} %bitcast.14, ...), custom_call_target="tpu_custom_call", output_to_operand_aliasing={{0}: (0, {})} | custom-call | flops 4000000000 | bytes 4194304 | tf_op jit(solution)/shard_map/pallas_call | solution.py:282
  18.0 0.0 copy-start
  18.0 0.0 copy-start.1
  18.0 2.6 %shard_map.84.psi_near = f32[512,512]{1,0:T(8,128)S(1)} custom-call(bf16[4096,512]{1,0:T(8,128)(2,1)S(1)} %get-tuple-element.6.basis, bf16[4,16,512]{2,1,0:T(8,128)(2,1)S(1)} %pad_maximum_fusion.near), custom_call_target="tpu_custom_call" | custom-call | flops 4000000000 | bytes 4194304 | tf_op jit(solution)/shard_map/pallas_call | solution.py:298
  20.7 0.0 collective-permute-done.6.far
  20.7 0.0 copy-done
  20.7 0.0 copy-done.1
  20.7 3.3 %shard_map.85 = f32[8,128]{1,0:T(8,128)S(1)} custom-call(bf16[4096,512]{1,0:T(8,128)(2,1)S(1)} %get-tuple-element.6.basis, f32[512,512]{1,0:T(8,128)S(1)} %shard_map.84.psi_near, bf16[4,16,512]{2,1,0:T(8,128)(2,1)S(1)} %pad_maximum_fusion.near, bf16[4,16,512]{2,1,0:T(8,128)(2,1)S(1)} %collective-permute-done.6.far, s32[1,64]{1,0:T(1,128)S(1)} %bitcast.15, ...), custom_call_target="tpu_custom_call" | custom-call | flops 4000000000 | bytes 4194304 | tf_op jit(solution)/shard_map/pallas_call | solution.py:307
  24.0 9.2 %all_to_all.12 = f32[8,1,128]{2,1,0:T(1,128)S(1)} all-to-all(f32[8,1,128]{2,1,0:T(1,128)S(1)} %bitcast.12), channel_id=1, replica_groups=mesh['grp'=2,'probe'=8,'beam'=2] {'probe'}, dimensions={0} | all-to-all | bytes 8192 | tf_op jit(solution)/shard_map/all_to_all | solution.py:316
  33.1 0.6 %copy.13 = f32[8,128]{1,0:T(8,128)} copy(f32[8,128]{1,0:T(8,128)S(1)} %bitcast.16) | data formatting | bytes 8192
  (3 shorter events, 0.0 us)
Async XLA Ops:
  0.0 14.3 %collective-permute-start = (bf16[2048,512]{1,0:T(8,128)(2,1)}, bf16[2048,512]{1,0:T(8,128)(2,1)S(1)}, u32[]{:S(2)}, u32[]{:S(2)}) collective-permute-start(bf16[2048,512]{1,0:T(8,128)(2,1)} %bitcast.17), channel_id=1, source_target_pairs={{0,1},{1,0},{2,3},{3,2},{4,5},{5,4},{6,7},{7,6},{8,9},{9,8},{10,11... | collective-permute-start | bytes 6291464 | tf_op jit(solution)/shard_map/ppermute | solution.py:237
  2.0 4.2 %collective-permute-start.4 = (bf16[1,16,512]{2,1,0:T(8,128)(2,1)S(1)}, bf16[1,16,512]{2,1,0:T(8,128)(2,1)S(1)}, u32[]{:S(2)}, u32[]{:S(2)}) collective-permute-start(bf16[1,16,512]{2,1,0:T(8,128)(2,1)S(1)} %maximum_bitcast_fusion), channel_id=1, source_target_pairs={{0,2},{2,0},{4,6},{6,4},{8,10},{10,8},{12,14},{14,12},{1,3},{3,1},... | collective-permute-start | bytes 49160 | tf_op jit(solution)/shard_map/ppermute | solution.py:245
  4.5 9.7 %collective-permute-start.1 = (f32[2048]{0:T(1024)}, f32[2048]{0:T(1024)S(1)}, u32[]{:S(2)}, u32[]{:S(2)}) collective-permute-start(f32[2048]{0:T(1024)} %param.9), channel_id=1, source_target_pairs={{0,1},{1,0},{2,3},{3,2},{4,5},{5,4},{6,7},{7,6},{8,9},{9,8},{10,11... | collective-permute-start | bytes 24584 | tf_op jit(solution)/shard_map/ppermute | solution.py:237
  4.8 9.5 %collective-permute-start.2 = (f32[2048]{0:T(1024)}, f32[2048]{0:T(1024)S(1)}, u32[]{:S(2)}, u32[]{:S(2)}) collective-permute-start(f32[2048]{0:T(1024)} %param.10), channel_id=1, source_target_pairs={{0,1},{1,0},{2,3},{3,2},{4,5},{5,4},{6,7},{7,6},{8,9},{9,8},{10,11... | collective-permute-start | bytes 24584 | tf_op jit(solution)/shard_map/ppermute | solution.py:237
  5.0 9.2 %collective-permute-start.3 = (s32[2,2048]{1,0:T(2,128)}, s32[2,2048]{1,0:T(2,128)S(1)}, u32[]{:S(2)}, u32[]{:S(2)}) collective-permute-start(s32[2,2048]{1,0:T(2,128)} %k_ref.1), channel_id=1, source_target_pairs={{0,1},{1,0},{2,3},{3,2},{4,5},{5,4},{6,7},{7,6},{8,9},{9,8},{10,11... | collective-permute-start | bytes 49160 | tf_op jit(solution)/shard_map/ppermute | solution.py:237
  6.3 5.3 %collective-permute-start.5 = (bf16[2,16,512]{2,1,0:T(8,128)(2,1)S(1)}, bf16[2,16,512]{2,1,0:T(8,128)(2,1)S(1)}, u32[]{:S(2)}, u32[]{:S(2)}) collective-permute-start(bf16[2,16,512]{2,1,0:T(8,128)(2,1)S(1)} %pad_maximum_fusion.1), channel_id=1, source_target_pairs={{0,4},{2,6},{4,0},{6,2},{8,12},{10,14},{12,8},{14,10},{1,5},{3,7},... | collective-permute-start | bytes 98312 | tf_op jit(solution)/shard_map/ppermute | solution.py:245
  11.6 9.1 %collective-permute-start.6 = (bf16[4,16,512]{2,1,0:T(8,128)(2,1)S(1)}, bf16[4,16,512]{2,1,0:T(8,128)(2,1)S(1)}, u32[]{:S(2)}, u32[]{:S(2)}) collective-permute-start(bf16[4,16,512]{2,1,0:T(8,128)(2,1)S(1)} %pad_maximum_fusion.near), channel_id=1, source_target_pairs={{0,8},{2,10},{4,12},{6,14},{8,0},{10,2},{12,4},{14,6},{1,9},{3,11}... | collective-permute-start | bytes 196616 | tf_op jit(solution)/shard_map/ppermute | solution.py:245
  18.0 2.7 %copy-start = (s32[64]{0:T(128)S(1)}, s32[64]{0:T(128)}, u32[]{:S(2)}) copy-start(s32[64]{0:T(128)} %param.14) | copy-start | bytes 772
  18.0 2.7 %copy-start.1 = (f32[2,128,128]{2,1,0:T(8,128)S(1)}, f32[2,128,128]{2,1,0:T(8,128)}, u32[]{:S(2)}) copy-start(f32[2,128,128]{2,1,0:T(8,128)} %constant.32.clone.overlap) | copy-start | bytes 393220

commit v4 on v3

--- a/solution.py
+++ b/solution.py
@@ -39,27 +39,46 @@
     return cos_v, sin_v * u
 
 
-def place_rows(k_ref, place_v):
-    kx, ky = k_ref[0:1, :], k_ref[1:2, :]
+def pack_kernel(amp, abr, k_hbm, pos_hbm, patches, small, param, amp_v, abr_v, k_v, pos_v, pat_v, sems):
+    f32, bf16 = jnp.float32, jnp.bfloat16
+    pairs = [(amp, amp_v), (abr, abr_v), (k_hbm, k_v), (pos_hbm, pos_v), (patches, pat_v)]
+    copies = [pltpu.make_async_copy(src, dst, sems.at[n]) for n, (src, dst) in enumerate(pairs)]
+    for c in copies:
+        c.start()
+    for c in copies:
+        c.wait()
+    half = lax.axis_index("beam")
+    pats = pat_v[...].astype(f32)
+    pos = jnp.where(half == 0, pos_v[:, :LANE], pos_v[:, LANE:])
+    tiles = [pats[:, t * LANE : (t + 1) * LANE] for t in range(pats.shape[1] // LANE)]
+    split = [(pos // 32).astype(f32), (pos % 32).astype(f32), jnp.zeros((12, LANE), f32)]
+    message = jnp.concatenate(tiles + [jnp.concatenate(split, 0)], 0)
+    small[0] = message.astype(bf16)
+    lines = amp_v.shape[0]
+    param[0:lines, :] = amp_v[...] * jnp.cos(abr_v[...])
+    param[lines : 2 * lines, :] = amp_v[...] * jnp.sin(abr_v[...])
+    kx, ky = k_v[0:1, :], k_v[1:2, :]
     qx, qy = kx >= 0, ky >= 0
     mx, my = jnp.where(qx, kx, -1 - kx), jnp.where(qy, ky, -1 - ky)
     quad = 2 * qx.astype(jnp.int32) + qy.astype(jnp.int32)
-    place_v[...] = ((quad * KMAX + mx) * KMAX + my) * 4
-
-
-def spread_rows(s_ref, amp, abr, k_ref, grid_rows, x_even, x_odd, phase, place_v, place_s, sem, ready=(None,)):
+    place = (((quad * KMAX + mx) * KMAX + my) * 4).astype(f32)
+    for r in range(lines):
+        param[2 * lines + r : 2 * lines + r + 1, :] = place[:, r * LANE : (r + 1) * LANE]
+
+
+def spread_rows(s_ref, param, grid_rows, x_even, x_odd, place_v, place_s, sem, ready=()):
     f32 = jnp.float32
-    rows = s_ref.shape[0]
-    place_rows(k_ref, place_v)
+    lines = s_ref.shape[0] // LANE
+    place = param[2 * lines : 3 * lines, :].astype(jnp.int32)
+    for r in range(lines):
+        place_v[0:1, r * LANE : (r + 1) * LANE] = place[r : r + 1, :]
     idx_copy = pltpu.make_async_copy(place_v.at[0], place_s, sem)
     idx_copy.start()
-    phase[0] = amp[...] * jnp.cos(abr[...])
-    phase[1] = amp[...] * jnp.sin(abr[...])
 
     def turned(r, x_ref):
         here = pl.ds(pl.multiple_of(r * LANE, LANE), LANE)
-        ph_c = jnp.broadcast_to(phase[0, pl.ds(r, 1), :], (LANE, LANE)).T
-        ph_s = jnp.broadcast_to(phase[1, pl.ds(r, 1), :], (LANE, LANE)).T
+        ph_c = jnp.broadcast_to(param[pl.ds(r, 1), :], (LANE, LANE)).T
+        ph_s = jnp.broadcast_to(param[pl.ds(lines + r, 1), :], (LANE, LANE)).T
         for h in range(2):
             re = s_ref[here, pl.ds(h * LANE, LANE)].astype(f32)
             im = s_ref[here, pl.ds((2 + h) * LANE, LANE)].astype(f32)
@@ -72,44 +91,39 @@
             to = pl.multiple_of(place_s[base + u], 4)
             grid_rows[pl.ds(to, 4), :] = x_ref[4 * u : 4 * u + 4, :]
 
-    part = rows // LANE // len(ready)
-    for n, wait in enumerate(ready):
-        first, last = n * part, (n + 1) * part - 1
-        if wait is not None:
-            wait()
+    stops = [last for last, _ in ready] + [lines] if ready else [0, lines]
+    waits = [wait for _, wait in ready] if ready else [lambda: None]
+    idx_copy.wait()
+    for first, stop, wait in zip(stops, stops[1:], waits):
+        wait()
         turned(first, x_even)
-        if n == 0:
-            idx_copy.wait()
-
-        @pl.loop(first // 2, (last + 1) // 2)
+
+        @pl.loop(first // 2, stop // 2)
         def _(i):
             r = 2 * i
             turned(r + 1, x_odd)
             scatter(r, x_even)
-            turned(jnp.minimum(r + 2, last), x_even)
+            turned(jnp.minimum(r + 2, stop - 1), x_even)
             scatter(r + 1, x_odd)
 
 
-def own_kernel(
-    s_own, amp, abr, k_ref, grid_rows, s_vmem, amp_v, abr_v, k_v, x_even, x_odd, phase, place_v, place_s, sem, sems
-):
-    rows = s_vmem.shape[0]
-    chunks = [pl.ds(n * (rows // 2), rows // 2) for n in range(2)]
-    pairs = [(k_ref, k_v), (amp, amp_v), (abr, abr_v)] + [(s_own.at[c], s_vmem.at[c]) for c in chunks]
-    copies = [pltpu.make_async_copy(src, dst, sems.at[n]) for n, (src, dst) in enumerate(pairs)]
-    for c in copies:
-        c.start()
-    for c in copies[:3]:
-        c.wait()
-    ready = [c.wait for c in copies[3:]]
-    spread_rows(s_vmem, amp_v, abr_v, k_v, grid_rows, x_even, x_odd, phase, place_v, place_s, sem, ready)
-
-
-def other_kernel(
-    held, s_rem, amp, abr, k_ref, grid_rows, basis, x_even, x_odd, phase, place_v, place_s, sem
-):
+def own_kernel(s_own, param, grid_rows, zero, s_vmem, sems, *scratch):
+    lines = s_vmem.shape[0] // LANE
+    starts = (0, lines // 4)
+    ready = []
+    for n, (first, stop) in enumerate(zip(starts, starts[1:] + (lines,))):
+        part = pl.ds(first * LANE, (stop - first) * LANE)
+        load = pltpu.make_async_copy(s_own.at[part], s_vmem.at[part], sems.at[n])
+        load.start()
+        ready.append((first, load.wait))
+    zero[...] = jnp.zeros_like(zero)
+    spread_rows(s_vmem, param, grid_rows, *scratch, ready=ready)
+
+
+def other_kernel(held, s_rem, param, grid_rows, basis, zero, *scratch):
     bf16 = jnp.bfloat16
-    spread_rows(s_rem, amp, abr, k_ref, grid_rows, x_even, x_odd, phase, place_v, place_s, sem)
+    zero[...] = jnp.zeros_like(zero)
+    spread_rows(s_rem, param, grid_rows, *scratch)
     quarter = KMAX * KMAX * 4
 
     @pl.loop(0, KMAX * KMAX // LANE)
@@ -134,16 +148,12 @@
 
 def waves(source, basis, coef_even, coef_odd, tab, emit):
     f32, bf16 = jnp.float32, jnp.bfloat16
-    half = lax.axis_index("beam")
     blocks, step = source.shape[0], coef_even.shape[0]
     per = step // LANE
 
     def tables(j):
-        pos = source[j, 8:10, :].astype(f32).astype(jnp.int32)
-        width = pos.shape[1] // 2
-        pos = 32 * pos[:, :width] + pos[:, width:]
-        pos = jnp.where(half == 0, pos[:, :LANE], pos[:, LANE:])
-        px, py = pos[0:1], pos[1:2]
+        pos = source[j, 32:48, :].astype(f32).astype(jnp.int32)
+        px, py = 32 * pos[0:1] + pos[2:3], 32 * pos[1:2] + pos[3:4]
         my = lax.broadcasted_iota(jnp.int32, (KMAX, LANE), 0)
         mx = lax.broadcasted_iota(jnp.int32, (8, LANE), 0)
         cy, sy = half_turns((2 * my + 1) * py)
@@ -190,15 +200,17 @@
     waves(near, basis, coef_even, coef_odd, tab, emit)
 
 
-def far_kernel(basis, psi_near, near, far, cols, overlap, out, coef_even, coef_odd, tab, pots):
+def far_kernel(masks, basis, psi_near, near, far, cols, overlap, out, coef_even, coef_odd, tab, pots):
     f32, bf16 = jnp.float32, jnp.bfloat16
     column = lax.axis_index("probe")
     step = coef_even.shape[0]
     blocks = near.shape[0]
     for n, source in enumerate((near, far)):
         for j in range(blocks):
-            owner = column ^ (n * blocks + j)
-            pots[pl.ds(pl.multiple_of(owner * 8, 8), 8), :] = source[j, 0:8, :].astype(f32)
+            owner = column ^ masks[n * blocks + j]
+            pats = source[j, 0:32, :].astype(f32)
+            for t in range(4):
+                pots[pl.ds(pl.multiple_of(owner * 8, 8), 8), t * LANE : (t + 1) * LANE] = pats[8 * t : 8 * t + 8]
     mine = (cols[...] == column).astype(f32)
     left = (pots[...].T * mine).astype(bf16)
     right = pots[...].astype(bf16)
@@ -221,7 +233,7 @@
             v = wave * mul(wave.astype(bf16), forms[h])
             e = e + v[:, :LANE] + v[:, LANE:]
         for i in range(step // LANE):
-            out[pl.ds(column ^ (first + i), 1), :] = jnp.sum(e[i * LANE : (i + 1) * LANE].T, axis=0, keepdims=True)
+            out[pl.ds(column ^ masks[first + i], 1), :] = jnp.sum(e[i * LANE : (i + 1) * LANE].T, axis=0, keepdims=True)
 
     def emit(m, psi):
         energy(blocks + m * step // LANE, psi)
@@ -234,61 +246,67 @@
     f32, bf16 = jnp.float32, jnp.bfloat16
     blocks = lax.axis_size("probe")
     rows, width = smatrix.shape[0], smatrix.shape[2]
+    lines, grid = rows // LANE, 4 * KMAX * KMAX
     swap = lambda v: lax.ppermute(v, "beam", [(0, 1), (1, 0)])
+    sds = jax.ShapeDtypeStruct
+    vmem, hbm = pl.BlockSpec(memory_space=pltpu.VMEM), pl.BlockSpec(memory_space=pltpu.HBM)
+    params = pltpu.CompilerParams(vmem_limit_bytes=24 * 1024 * 1024)
+    cost = lambda n: pl.CostEstimate(flops=n, bytes_accessed=4 * 2**20, transcendentals=0)
+
+    message = sds((1, 48, LANE), bf16)
     s_own = smatrix.reshape(rows, width)
-    s_rem = swap(s_own)
-    amp_rem, abr_rem, k_rem = swap(aperture), swap(aberration), swap(beam_k)
-    pos = jnp.concatenate([probe_pos // 32, probe_pos % 32], 1).astype(bf16)
-    small = jnp.concatenate([patches, pos, jnp.zeros((6, width), bf16)], 0)[None]
-    reach = 1
-    while reach < blocks:
-        far = lax.ppermute(small, "probe", [(i, i ^ reach) for i in range(blocks)])
-        near, reach = small, 2 * reach
-        if reach < blocks:
-            small = jnp.concatenate([near, far], 0)
-
-    vmem = pl.BlockSpec(memory_space=pltpu.VMEM)
-    params = pltpu.CompilerParams(vmem_limit_bytes=24 * 1024 * 1024)
-    grid = 4 * KMAX * KMAX
-    lines = rows // LANE
+    raw = (aperture.reshape(lines, LANE), aberration.reshape(lines, LANE), beam_k, probe_pos, patches)
+    small, param = pl.pallas_call(
+        pack_kernel,
+        out_shape=(message, sds((3 * lines, LANE), f32)),
+        in_specs=[hbm] * len(raw),
+        out_specs=(vmem,) * 2,
+        scratch_shapes=[pltpu.VMEM(v.shape, v.dtype) for v in raw] + [pltpu.SemaphoreType.DMA((len(raw),))],
+        compiler_params=params,
+        cost_estimate=cost(10**9),
+    )(*(pltpu.with_memory_space_constraint(v, pltpu.HBM) for v in raw))
+    param_rem = swap(param)
+    later, _ = lax.optimization_barrier((s_own, small))
+    s_rem = swap(later)
+
     turning = [
         pltpu.VMEM((4 * LANE, LANE), f32),
         pltpu.VMEM((4 * LANE, LANE), f32),
-        pltpu.VMEM((2, lines, LANE), f32),
         pltpu.VMEM((1, rows), jnp.int32),
         pltpu.SMEM((rows,), jnp.int32),
         pltpu.SemaphoreType.DMA,
     ]
-    tile = lambda v: v.reshape(lines, LANE)
-    cost = lambda n: pl.CostEstimate(flops=n, bytes_accessed=4 * 2**20, transcendentals=0)
-    held_shape = jax.ShapeDtypeStruct((4 * grid, LANE), f32)
-    hbm = pl.BlockSpec(memory_space=pltpu.HBM)
-    held = pl.pallas_call(
+    held_shape = sds((4 * grid, LANE), f32)
+    held, zero_own = pl.pallas_call(
         own_kernel,
-        out_shape=held_shape,
-        in_specs=[hbm] * 4,
-        out_specs=vmem,
-        scratch_shapes=[
-            pltpu.VMEM((rows, width), bf16),
-            pltpu.VMEM((lines, LANE), f32),
-            pltpu.VMEM((lines, LANE), f32),
-            pltpu.VMEM((2, rows), jnp.int32),
-        ]
-        + turning
-        + [pltpu.SemaphoreType.DMA((5,))],
+        out_shape=(held_shape, message),
+        in_specs=[hbm, vmem],
+        out_specs=(vmem,) * 2,
+        scratch_shapes=[pltpu.VMEM((rows, width), bf16), pltpu.SemaphoreType.DMA((2,))] + turning,
         compiler_params=params,
         cost_estimate=cost(3 * 10**9),
-    )(*(pltpu.with_memory_space_constraint(v, pltpu.HBM) for v in (s_own, tile(aperture), tile(aberration), beam_k)))
-    _, basis = pl.pallas_call(
+    )(pltpu.with_memory_space_constraint(s_own, pltpu.HBM), param)
+    _, basis, zero_other = pl.pallas_call(
         other_kernel,
-        out_shape=(held_shape, jax.ShapeDtypeStruct((grid, width), bf16)),
-        in_specs=[vmem] * 5,
-        out_specs=(vmem, vmem),
+        out_shape=(held_shape, sds((grid, width), bf16), message),
+        in_specs=[vmem] * 3,
+        out_specs=(vmem,) * 3,
         scratch_shapes=turning,
         input_output_aliases={0: 0},
         compiler_params=params,
         cost_estimate=cost(4 * 10**9),
-    )(held, s_rem, tile(amp_rem), tile(abr_rem), k_rem)
+    )(held, s_rem, param_rem)
+
+    steps = [1 << n for n in range(blocks.bit_length() - 1)]
+    steps = steps[-2:] + steps[:-2][::-1]
+    beside, masks = [zero_own, zero_other], [0]
+    for reach in steps:
+        far = lax.ppermute(small, "probe", [(i, i ^ reach) for i in range(blocks)])
+        masks = masks + [m ^ reach for m in masks]
+        near = small
+        if reach != steps[-1]:
+            small = jnp.concatenate([near, far + beside.pop(0) if beside else far], 0)
+
     probes = blocks // 2 * LANE
     working = [
         pltpu.VMEM((2 * LANE, grid), bf16),
@@ -305,7 +323,7 @@
         cost_estimate=cost(4 * 10**9),
     )(basis, near)
     energy = pl.pallas_call(
-        far_kernel,
+        functools.partial(far_kernel, tuple(masks)),
         out_shape=jax.ShapeDtypeStruct((blocks, LANE), f32),
         in_specs=[vmem] * 6,
         out_specs=vmem,

time: 34.1 us -> 31.8 us (0.933)
  other arithmetic: 1.48 us -> 0.03 us
  Pallas kernels: 12.8 us -> 14.2 us
  waiting for transfers between devices: 1 us -> 0.01 us
  starting transfers between devices: 8.44 us -> 7.57 us
    pallas_call x3 -> x4, Pallas kernels: 10.2 us -> 11.2 us  [the longest x1 3.78 us: shards(): pl.pallas_call(other_kernel, out_shape=(held_shape, sds((grid, width), bf...]
    ppermute x3, waiting for transfers between devices: 0.99 us -> 0.01 us  [shards(): far = lax.ppermute(small, 'probe', [(i, i ^ reach) for i in range(blocks)])]
    broadcast_in_dim x1 -> x0, other arithmetic: 0.77 us -> none  [shards(): jnp.concatenate([patches, pos, jnp.zeros((6, width), bf16)], 0)[None]]
    another operation x1 -> x0, other arithmetic: 0.69 us -> none
    ppermute x4 -> x2, starting transfers between devices: 1.19 us -> 0.68 us  [shards(): swap = lambda v: lax.ppermute(v, 'beam', [(0, 1), (1, 0)])]
    ppermute x3, starting transfers between devices: 7.25 us -> 6.89 us  [shards(): far = lax.ppermute(small, 'probe', [(i, i ^ reach) for i in range(blocks)])]
  transfers between devices with their start and end apart: 7 -> 5, of which waited for: 1 -> 0; matrix products, arithmetic and copies ran while one was open for 5% -> 0% of each run, Pallas kernels for 28% -> 31%
where the time goes in v4:
time: 31.8 us; the launch traced here: 31.5 us
  Pallas kernels  14.2 us (45%)
  blocking collectives  8.95 us (28%)
  starting transfers between devices  7.57 us (24%)
  local copies, waits for them, and re-layouts  0.6 us (2%)
    all_to_all x1, blocking collectives, shards(): return lax.all_to_all(energy, 'probe', 0, 0, tiled=True)  8.95 us
    ppermute x3, starting transfers between devices, shards(): far = lax.ppermute(small, 'probe', [(i, i ^ reach) for i in range(blocks)])  6.89 us
    pallas_call x1, Pallas kernels, shards(): pl.pallas_call(other_kernel, out_shape=(held_shape, sds((grid, width), bf...  3.78 us
    pallas_call x1, Pallas kernels, shards(): pl.pallas_call(functools.partial(far_kernel, tuple(masks)), out_shape=jax...  3.61 us
    pallas_call x1, Pallas kernels, shards(): pl.pallas_call(near_kernel, out_shape=jax.ShapeDtypeStruct((probes, width...  2.98 us
    pallas_call x1, Pallas kernels, shards(): pl.pallas_call(own_kernel, out_shape=(held_shape, message), in_specs=[hbm...  2.96 us
    pallas_call x1, Pallas kernels, shards(): pl.pallas_call(pack_kernel, out_shape=(message, sds((3 * lines, LANE), f3...  0.86 us
    ppermute x2, starting transfers between devices, shards(): swap = lambda v: lax.ppermute(v, 'beam', [(0, 1), (1, 0)])  0.68 us
  transfers between devices with their start and end apart: 5, of which 0 were waited for; matrix products, arithmetic and copies ran while one was open for 0% of the time, Pallas kernels for 31%

profile of v4, /device:TPU:0, one launch (start us, length us, event | category | flops | bytes accessed | tf_op | source)
XLA Modules:
  0.0 31.5 jit_solution(8726108522462584346)
XLA Ops:
  0.0 0.9 %shard_map.82 = (bf16[1,48,128]{2,1,0:T(8,128)(2,1)S(1)}, f32[48,128]{1,0:T(8,128)S(1)}) custom-call(f32[16,128]{1,0:T(8,128)} %bitcast.15, f32[16,128]{1,0:T(8,128)} %bitcast.16, s32[2,2048]{1,0:T(2,128)} %k_hbm.1, s32[2,256]{1,0:T(2,128)} %pos_hbm.1, bf16[8,512]{1,0:T(8,128)(2,1)} %patches.1), custom_call_target="tpu_custom_call" | custom-call | flops 1000000000 | bytes 4194304 | tf_op jit(solution)/shard_map/pallas_call | solution.py:259
  0.9 0.5 %collective-permute-start = (bf16[2048,512]{1,0:T(8,128)(2,1)}, bf16[2048,512]{1,0:T(8,128)(2,1)S(1)}, u32[]{:S(2)}, u32[]{:S(2)}) collective-permute-start(bf16[2048,512]{1,0:T(8,128)(2,1)} %bitcast.13), channel_id=1, source_target_pairs={{0,1},{1,0},{2,3},{3,2},{4,5},{5,4},{6,7},{7,6},{8,9},{9,8},{10,11... | collective-permute-start | bytes 6291464 | tf_op jit(solution)/shard_map/ppermute | solution.py:250
  1.4 2.7 %collective-permute-start.2 = (bf16[1,48,128]{2,1,0:T(8,128)(2,1)S(1)}, bf16[1,48,128]{2,1,0:T(8,128)(2,1)S(1)}, u32[]{:S(2)}, u32[]{:S(2)}) collective-permute-start(bf16[1,48,128]{2,1,0:T(8,128)(2,1)S(1)} %get-tuple-element.14), channel_id=1, source_target_pairs={{0,4},{2,6},{4,0},{6,2},{8,12},{10,14},{12,8},{14,10},{1,5},{3,7},... | collective-permute-start | bytes 36872 | tf_op jit(solution)/shard_map/ppermute | solution.py:304
  4.0 0.2 collective-permute-start.1
  4.2 3.0 %shard_map.83 = (f32[16384,128]{1,0:T(8,128)S(1)}, bf16[1,48,128]{2,1,0:T(8,128)(2,1)S(1)}) custom-call(bf16[2048,512]{1,0:T(8,128)(2,1)} %bitcast.14, f32[48,128]{1,0:T(8,128)S(1)} %get-tuple-element.12.param), custom_call_target="tpu_custom_call" | custom-call | flops 3000000000 | bytes 4194304 | tf_op jit(solution)/shard_map/pallas_call | solution.py:280
  7.2 0.0 collective-permute-done.2
  7.2 2.7 %collective-permute-start.3 = (bf16[2,48,128]{2,1,0:T(8,128)(2,1)S(1)}, bf16[2,48,128]{2,1,0:T(8,128)(2,1)S(1)}, u32[]{:S(2)}, u32[]{:S(2)}) collective-permute-start(bf16[2,48,128]{2,1,0:T(8,128)(2,1)S(1)} %pad_maximum_fusion.1), channel_id=1, source_target_pairs={{0,8},{2,10},{4,12},{6,14},{8,0},{10,2},{12,4},{14,6},{1,9},{3,11}... | collective-permute-start | bytes 73736 | tf_op jit(solution)/shard_map/ppermute | solution.py:304
  9.9 0.0 collective-permute-done.1.param
  9.9 0.0 collective-permute-done.s_rem
  9.9 3.8 %shard_map.84 = (f32[16384,128]{1,0:T(8,128)S(1)}, bf16[4096,512]{1,0:T(8,128)(2,1)S(1)}, bf16[1,48,128]{2,1,0:T(8,128)(2,1)S(1)}) custom-call(f32[16384,128]{1,0:T(8,128)S(1)} %get-tuple-element.13.held, bf16[2048,512]{1,0:T(8,128)(2,1)S(1)} %collective-permute-done.s_rem, f32[48,128]{1,0:T(8,128)S(1)} %collective-permute-done.1.param), custom_call_target="tpu_custom_call", output_to_operand_aliasing={{0}: (0, {})} | custom-call | flops 4000000000 | bytes 4194304 | tf_op jit(solution)/shard_map/pallas_call | solution.py:289
  13.7 0.0 collective-permute-done.3
  13.7 1.6 %collective-permute-start.4 = (bf16[4,48,128]{2,1,0:T(8,128)(2,1)S(1)}, bf16[4,48,128]{2,1,0:T(8,128)(2,1)S(1)}, u32[]{:S(2)}, u32[]{:S(2)}) collective-permute-start(bf16[4,48,128]{2,1,0:T(8,128)(2,1)S(1)} %pad_maximum_fusion.near), channel_id=1, source_target_pairs={{0,2},{2,0},{4,6},{6,4},{8,10},{10,8},{12,14},{14,12},{1,3},{3,1},... | collective-permute-start | bytes 147464 | tf_op jit(solution)/shard_map/ppermute | solution.py:304
  15.3 0.0 copy-start
  15.3 0.0 copy-start.1
  15.3 3.0 %shard_map.85.psi_near = f32[512,512]{1,0:T(8,128)S(1)} custom-call(bf16[4096,512]{1,0:T(8,128)(2,1)S(1)} %get-tuple-element.16.basis, bf16[4,48,128]{2,1,0:T(8,128)(2,1)S(1)} %pad_maximum_fusion.near), custom_call_target="tpu_custom_call" | custom-call | flops 4000000000 | bytes 4194304 | tf_op jit(solution)/shard_map/pallas_call | solution.py:316
  18.3 0.0 collective-permute-done.4.far
  18.3 0.0 copy-done
  18.3 0.0 copy-done.1
  18.3 3.6 %shard_map.86 = f32[8,128]{1,0:T(8,128)S(1)} custom-call(bf16[4096,512]{1,0:T(8,128)(2,1)S(1)} %get-tuple-element.16.basis, f32[512,512]{1,0:T(8,128)S(1)} %shard_map.85.psi_near, bf16[4,48,128]{2,1,0:T(8,128)(2,1)S(1)} %pad_maximum_fusion.near, bf16[4,48,128]{2,1,0:T(8,128)(2,1)S(1)} %collective-permute-done.4.far, s32[1,64]{1,0:T(1,128)S(1)} %bitcast.11, ...), custom_call_target="tpu_custom_call" | custom-call | flops 4000000000 | bytes 4194304 | tf_op jit(solution)/shard_map/pallas_call | solution.py:325
  21.9 9.0 %all_to_all.12 = f32[8,1,128]{2,1,0:T(1,128)S(1)} all-to-all(f32[8,1,128]{2,1,0:T(1,128)S(1)} %bitcast.10), channel_id=1, replica_groups=mesh['grp'=2,'probe'=8,'beam'=2] {'probe'}, dimensions={0} | all-to-all | bytes 8192 | tf_op jit(solution)/shard_map/all_to_all | solution.py:334
  30.9 0.6 %copy.13 = f32[8,128]{1,0:T(8,128)} copy(f32[8,128]{1,0:T(8,128)S(1)} %bitcast.12) | data formatting | bytes 8192
  (4 shorter events, 0.0 us)
Async XLA Ops:
  0.9 9.0 %collective-permute-start = (bf16[2048,512]{1,0:T(8,128)(2,1)}, bf16[2048,512]{1,0:T(8,128)(2,1)S(1)}, u32[]{:S(2)}, u32[]{:S(2)}) collective-permute-start(bf16[2048,512]{1,0:T(8,128)(2,1)} %bitcast.13), channel_id=1, source_target_pairs={{0,1},{1,0},{2,3},{3,2},{4,5},{5,4},{6,7},{7,6},{8,9},{9,8},{10,11... | collective-permute-start | bytes 6291464 | tf_op jit(solution)/shard_map/ppermute | solution.py:250
  1.4 5.8 %collective-permute-start.2 = (bf16[1,48,128]{2,1,0:T(8,128)(2,1)S(1)}, bf16[1,48,128]{2,1,0:T(8,128)(2,1)S(1)}, u32[]{:S(2)}, u32[]{:S(2)}) collective-permute-start(bf16[1,48,128]{2,1,0:T(8,128)(2,1)S(1)} %get-tuple-element.14), channel_id=1, source_target_pairs={{0,4},{2,6},{4,0},{6,2},{8,12},{10,14},{12,8},{14,10},{1,5},{3,7},... | collective-permute-start | bytes 36872 | tf_op jit(solution)/shard_map/ppermute | solution.py:304
  4.0 5.8 %collective-permute-start.1 = (f32[48,128]{1,0:T(8,128)S(1)}, f32[48,128]{1,0:T(8,128)S(1)}, u32[]{:S(2)}, u32[]{:S(2)}) collective-permute-start(f32[48,128]{1,0:T(8,128)S(1)} %get-tuple-element.12.param), channel_id=1, source_target_pairs={{0,1},{1,0},{2,3},{3,2},{4,5},{5,4},{6,7},{7,6},{8,9},{9,8},{10,11... | collective-permute-start | bytes 73736 | tf_op jit(solution)/shard_map/ppermute | solution.py:250
  7.2 6.5 %collective-permute-start.3 = (bf16[2,48,128]{2,1,0:T(8,128)(2,1)S(1)}, bf16[2,48,128]{2,1,0:T(8,128)(2,1)S(1)}, u32[]{:S(2)}, u32[]{:S(2)}) collective-permute-start(bf16[2,48,128]{2,1,0:T(8,128)(2,1)S(1)} %pad_maximum_fusion.1), channel_id=1, source_target_pairs={{0,8},{2,10},{4,12},{6,14},{8,0},{10,2},{12,4},{14,6},{1,9},{3,11}... | collective-permute-start | bytes 73736 | tf_op jit(solution)/shard_map/ppermute | solution.py:304
  13.7 4.6 %collective-permute-start.4 = (bf16[4,48,128]{2,1,0:T(8,128)(2,1)S(1)}, bf16[4,48,128]{2,1,0:T(8,128)(2,1)S(1)}, u32[]{:S(2)}, u32[]{:S(2)}) collective-permute-start(bf16[4,48,128]{2,1,0:T(8,128)(2,1)S(1)} %pad_maximum_fusion.near), channel_id=1, source_target_pairs={{0,2},{2,0},{4,6},{6,4},{8,10},{10,8},{12,14},{14,12},{1,3},{3,1},... | collective-permute-start | bytes 147464 | tf_op jit(solution)/shard_map/ppermute | solution.py:304
  15.3 3.0 %copy-start = (s32[64]{0:T(128)S(1)}, s32[64]{0:T(128)}, u32[]{:S(2)}) copy-start(s32[64]{0:T(128)} %param.14) | copy-start | bytes 772
  15.3 3.0 %copy-start.1 = (f32[2,128,128]{2,1,0:T(8,128)S(1)}, f32[2,128,128]{2,1,0:T(8,128)}, u32[]{:S(2)}) copy-start(f32[2,128,128]{2,1,0:T(8,128)} %constant.2.clone.overlap) | copy-start | bytes 393220

commit v5 on v4

--- a/solution.py
+++ b/solution.py
@@ -47,11 +47,10 @@
         c.start()
     for c in copies:
         c.wait()
-    half = lax.axis_index("beam")
     pats = pat_v[...].astype(f32)
-    pos = jnp.where(half == 0, pos_v[:, :LANE], pos_v[:, LANE:])
+    pos = jnp.concatenate([pos_v[:, :LANE], pos_v[:, LANE:]], 0)
     tiles = [pats[:, t * LANE : (t + 1) * LANE] for t in range(pats.shape[1] // LANE)]
-    split = [(pos // 32).astype(f32), (pos % 32).astype(f32), jnp.zeros((12, LANE), f32)]
+    split = [(pos // 32).astype(f32), (pos % 32).astype(f32), jnp.zeros((8, LANE), f32)]
     message = jnp.concatenate(tiles + [jnp.concatenate(split, 0)], 0)
     small[0] = message.astype(bf16)
     lines = amp_v.shape[0]
@@ -148,12 +147,15 @@
 
 def waves(source, basis, coef_even, coef_odd, tab, emit):
     f32, bf16 = jnp.float32, jnp.bfloat16
+    half = lax.axis_index("beam")
     blocks, step = source.shape[0], coef_even.shape[0]
     per = step // LANE
 
     def tables(j):
         pos = source[j, 32:48, :].astype(f32).astype(jnp.int32)
-        px, py = 32 * pos[0:1] + pos[2:3], 32 * pos[1:2] + pos[3:4]
+        pos = 32 * pos[0:4] + pos[4:8]
+        pos = jnp.where(half == 0, pos[0:2], pos[2:4])
+        px, py = pos[0:1], pos[1:2]
         my = lax.broadcasted_iota(jnp.int32, (KMAX, LANE), 0)
         mx = lax.broadcasted_iota(jnp.int32, (8, LANE), 0)
         cy, sy = half_turns((2 * my + 1) * py)
@@ -276,7 +278,7 @@
         pltpu.SMEM((rows,), jnp.int32),
         pltpu.SemaphoreType.DMA,
     ]
-    held_shape = sds((4 * grid, LANE), f32)
+    held_shape = sds((4 * grid + 24, LANE), f32)
     held, zero_own = pl.pallas_call(
         own_kernel,
         out_shape=(held_shape, message),
@@ -301,7 +303,9 @@
     steps = steps[-2:] + steps[:-2][::-1]
     beside, masks = [zero_own, zero_other], [0]
     for reach in steps:
-        far = lax.ppermute(small, "probe", [(i, i ^ reach) for i in range(blocks)])
+        far = lax.ppermute(
+            small, ("probe", "beam"), [(2 * i + b, 2 * (i ^ reach) + 1 - b) for i in range(blocks) for b in range(2)]
+        )
         masks = masks + [m ^ reach for m in masks]
         near = small
         if reach != steps[-1]:

time: 31.8 us -> 30.8 us (0.969)
  Pallas kernels: 14.2 us -> 13.5 us
  starting transfers between devices: 7.57 us -> 7.24 us
    pallas_call x1, Pallas kernels: 3.61 us -> 3.25 us  [shards(): pl.pallas_call(functools.partial(far_kernel, tuple(masks)), out_shape=jax...]
    pallas_call x1, Pallas kernels: 2.98 us -> 2.63 us  [shards(): pl.pallas_call(near_kernel, out_shape=jax.ShapeDtypeStruct((probes, width...]
where the time goes in v5:
time: 30.8 us; the launch traced here: 30.5 us
  Pallas kernels  13.5 us (44%)
  blocking collectives  8.99 us (29%)
  starting transfers between devices  7.24 us (24%)
  local copies, waits for them, and re-layouts  0.6 us (2%)
    all_to_all x1, blocking collectives, shards(): return lax.all_to_all(energy, 'probe', 0, 0, tiled=True)  8.99 us
    ppermute x3, starting transfers between devices, shards(): lax.ppermute(small, ('probe', 'beam'), [(2 * i + b, 2 * (i ^ reach) + 1 -...  6.66 us
    pallas_call x1, Pallas kernels, shards(): pl.pallas_call(other_kernel, out_shape=(held_shape, sds((grid, width), bf...  3.78 us
    pallas_call x1, Pallas kernels, shards(): pl.pallas_call(functools.partial(far_kernel, tuple(masks)), out_shape=jax...  3.25 us
    pallas_call x1, Pallas kernels, shards(): pl.pallas_call(own_kernel, out_shape=(held_shape, message), in_specs=[hbm...  2.96 us
    pallas_call x1, Pallas kernels, shards(): pl.pallas_call(near_kernel, out_shape=jax.ShapeDtypeStruct((probes, width...  2.63 us
    pallas_call x1, Pallas kernels, shards(): pl.pallas_call(pack_kernel, out_shape=(message, sds((3 * lines, LANE), f3...  0.86 us
  transfers between devices with their start and end apart: 5, of which 0 were waited for; matrix products, arithmetic and copies ran while one was open for 0% of the time, Pallas kernels for 31%

profile of v5, /device:TPU:0, one launch (start us, length us, event | category | flops | bytes accessed | tf_op | source)
XLA Modules:
  0.0 30.5 jit_solution(10999997122376846670)
XLA Ops:
  0.0 0.9 %shard_map.82 = (bf16[1,48,128]{2,1,0:T(8,128)(2,1)S(1)}, f32[48,128]{1,0:T(8,128)S(1)}) custom-call(f32[16,128]{1,0:T(8,128)} %bitcast.15, f32[16,128]{1,0:T(8,128)} %bitcast.16, s32[2,2048]{1,0:T(2,128)} %k_hbm.1, s32[2,256]{1,0:T(2,128)} %pos_hbm.1, bf16[8,512]{1,0:T(8,128)(2,1)} %patches.1), custom_call_target="tpu_custom_call" | custom-call | flops 1000000000 | bytes 4194304 | tf_op jit(solution)/shard_map/pallas_call | solution.py:261
  0.9 0.5 %collective-permute-start = (bf16[2048,512]{1,0:T(8,128)(2,1)}, bf16[2048,512]{1,0:T(8,128)(2,1)S(1)}, u32[]{:S(2)}, u32[]{:S(2)}) collective-permute-start(bf16[2048,512]{1,0:T(8,128)(2,1)} %bitcast.13), channel_id=1, source_target_pairs={{0,1},{1,0},{2,3},{3,2},{4,5},{5,4},{6,7},{7,6},{8,9},{9,8},{10,11... | collective-permute-start | bytes 6291464 | tf_op jit(solution)/shard_map/ppermute | solution.py:252
  1.4 2.7 %collective-permute-start.2 = (bf16[1,48,128]{2,1,0:T(8,128)(2,1)S(1)}, bf16[1,48,128]{2,1,0:T(8,128)(2,1)S(1)}, u32[]{:S(2)}, u32[]{:S(2)}) collective-permute-start(bf16[1,48,128]{2,1,0:T(8,128)(2,1)S(1)} %get-tuple-element.14), channel_id=1, source_target_pairs={{0,5},{1,4},{2,7},{3,6},{4,1},{5,0},{6,3},{7,2},{8,13},{9,12},{10,... | collective-permute-start | bytes 36872 | tf_op jit(solution)/shard_map/ppermute | solution.py:306
  4.1 0.1 collective-permute-start.1
  4.2 3.0 %shard_map.83 = (f32[16408,128]{1,0:T(8,128)S(1)}, bf16[1,48,128]{2,1,0:T(8,128)(2,1)S(1)}) custom-call(bf16[2048,512]{1,0:T(8,128)(2,1)} %bitcast.14, f32[48,128]{1,0:T(8,128)S(1)} %get-tuple-element.12.param), custom_call_target="tpu_custom_call" | custom-call | flops 3000000000 | bytes 4194304 | tf_op jit(solution)/shard_map/pallas_call | solution.py:282
  7.1 0.0 collective-permute-done.2
  7.2 2.7 %collective-permute-start.3 = (bf16[2,48,128]{2,1,0:T(8,128)(2,1)S(1)}, bf16[2,48,128]{2,1,0:T(8,128)(2,1)S(1)}, u32[]{:S(2)}, u32[]{:S(2)}) collective-permute-start(bf16[2,48,128]{2,1,0:T(8,128)(2,1)S(1)} %pad_maximum_fusion.1), channel_id=1, source_target_pairs={{0,9},{1,8},{2,11},{3,10},{4,13},{5,12},{6,15},{7,14},{8,1},{9,0},... | collective-permute-start | bytes 73736 | tf_op jit(solution)/shard_map/ppermute | solution.py:306
  9.9 0.0 collective-permute-done.1.param
  9.9 0.0 collective-permute-done.s_rem
  9.9 3.8 %shard_map.84 = (f32[16408,128]{1,0:T(8,128)S(1)}, bf16[4096,512]{1,0:T(8,128)(2,1)S(1)}, bf16[1,48,128]{2,1,0:T(8,128)(2,1)S(1)}) custom-call(f32[16408,128]{1,0:T(8,128)S(1)} %get-tuple-element.13.held, bf16[2048,512]{1,0:T(8,128)(2,1)S(1)} %collective-permute-done.s_rem, f32[48,128]{1,0:T(8,128)S(1)} %collective-permute-done.1.param), custom_call_target="tpu_custom_call", output_to_operand_aliasing={{0}: (0, {})} | custom-call | flops 4000000000 | bytes 4194304 | tf_op jit(solution)/shard_map/pallas_call | solution.py:291
  13.7 0.0 collective-permute-done.3
  13.7 1.3 %collective-permute-start.4 = (bf16[4,48,128]{2,1,0:T(8,128)(2,1)S(1)}, bf16[4,48,128]{2,1,0:T(8,128)(2,1)S(1)}, u32[]{:S(2)}, u32[]{:S(2)}) collective-permute-start(bf16[4,48,128]{2,1,0:T(8,128)(2,1)S(1)} %pad_maximum_fusion.near), channel_id=1, source_target_pairs={{0,3},{1,2},{2,1},{3,0},{4,7},{5,6},{6,5},{7,4},{8,11},{9,10},{10,... | collective-permute-start | bytes 147464 | tf_op jit(solution)/shard_map/ppermute | solution.py:306
  15.0 0.0 copy-start
  15.0 0.0 copy-start.1
  15.0 2.6 %shard_map.85.psi_near = f32[512,512]{1,0:T(8,128)S(1)} custom-call(bf16[4096,512]{1,0:T(8,128)(2,1)S(1)} %get-tuple-element.16.basis, bf16[4,48,128]{2,1,0:T(8,128)(2,1)S(1)} %pad_maximum_fusion.near), custom_call_target="tpu_custom_call" | custom-call | flops 4000000000 | bytes 4194304 | tf_op jit(solution)/shard_map/pallas_call | solution.py:320
  17.6 0.0 collective-permute-done.4.far
  17.6 0.0 copy-done
  17.6 0.0 copy-done.1
  17.6 3.2 %shard_map.86 = f32[8,128]{1,0:T(8,128)S(1)} custom-call(bf16[4096,512]{1,0:T(8,128)(2,1)S(1)} %get-tuple-element.16.basis, f32[512,512]{1,0:T(8,128)S(1)} %shard_map.85.psi_near, bf16[4,48,128]{2,1,0:T(8,128)(2,1)S(1)} %pad_maximum_fusion.near, bf16[4,48,128]{2,1,0:T(8,128)(2,1)S(1)} %collective-permute-done.4.far, s32[1,64]{1,0:T(1,128)S(1)} %bitcast.11, ...), custom_call_target="tpu_custom_call" | custom-call | flops 4000000000 | bytes 4194304 | tf_op jit(solution)/shard_map/pallas_call | solution.py:329
  20.9 9.0 %all_to_all.12 = f32[8,1,128]{2,1,0:T(1,128)S(1)} all-to-all(f32[8,1,128]{2,1,0:T(1,128)S(1)} %bitcast.10), channel_id=1, replica_groups=mesh['grp'=2,'probe'=8,'beam'=2] {'probe'}, dimensions={0} | all-to-all | bytes 8192 | tf_op jit(solution)/shard_map/all_to_all | solution.py:338
  29.9 0.6 %copy.13 = f32[8,128]{1,0:T(8,128)} copy(f32[8,128]{1,0:T(8,128)S(1)} %bitcast.12) | data formatting | bytes 8192
  (4 shorter events, 0.0 us)
Async XLA Ops:
  0.9 9.0 %collective-permute-start = (bf16[2048,512]{1,0:T(8,128)(2,1)}, bf16[2048,512]{1,0:T(8,128)(2,1)S(1)}, u32[]{:S(2)}, u32[]{:S(2)}) collective-permute-start(bf16[2048,512]{1,0:T(8,128)(2,1)} %bitcast.13), channel_id=1, source_target_pairs={{0,1},{1,0},{2,3},{3,2},{4,5},{5,4},{6,7},{7,6},{8,9},{9,8},{10,11... | collective-permute-start | bytes 6291464 | tf_op jit(solution)/shard_map/ppermute | solution.py:252
  1.4 5.7 %collective-permute-start.2 = (bf16[1,48,128]{2,1,0:T(8,128)(2,1)S(1)}, bf16[1,48,128]{2,1,0:T(8,128)(2,1)S(1)}, u32[]{:S(2)}, u32[]{:S(2)}) collective-permute-start(bf16[1,48,128]{2,1,0:T(8,128)(2,1)S(1)} %get-tuple-element.14), channel_id=1, source_target_pairs={{0,5},{1,4},{2,7},{3,6},{4,1},{5,0},{6,3},{7,2},{8,13},{9,12},{10,... | collective-permute-start | bytes 36872 | tf_op jit(solution)/shard_map/ppermute | solution.py:306
  4.1 5.8 %collective-permute-start.1 = (f32[48,128]{1,0:T(8,128)S(1)}, f32[48,128]{1,0:T(8,128)S(1)}, u32[]{:S(2)}, u32[]{:S(2)}) collective-permute-start(f32[48,128]{1,0:T(8,128)S(1)} %get-tuple-element.12.param), channel_id=1, source_target_pairs={{0,1},{1,0},{2,3},{3,2},{4,5},{5,4},{6,7},{7,6},{8,9},{9,8},{10,11... | collective-permute-start | bytes 73736 | tf_op jit(solution)/shard_map/ppermute | solution.py:252
  7.2 6.5 %collective-permute-start.3 = (bf16[2,48,128]{2,1,0:T(8,128)(2,1)S(1)}, bf16[2,48,128]{2,1,0:T(8,128)(2,1)S(1)}, u32[]{:S(2)}, u32[]{:S(2)}) collective-permute-start(bf16[2,48,128]{2,1,0:T(8,128)(2,1)S(1)} %pad_maximum_fusion.1), channel_id=1, source_target_pairs={{0,9},{1,8},{2,11},{3,10},{4,13},{5,12},{6,15},{7,14},{8,1},{9,0},... | collective-permute-start | bytes 73736 | tf_op jit(solution)/shard_map/ppermute | solution.py:306
  13.7 3.9 %collective-permute-start.4 = (bf16[4,48,128]{2,1,0:T(8,128)(2,1)S(1)}, bf16[4,48,128]{2,1,0:T(8,128)(2,1)S(1)}, u32[]{:S(2)}, u32[]{:S(2)}) collective-permute-start(bf16[4,48,128]{2,1,0:T(8,128)(2,1)S(1)} %pad_maximum_fusion.near), channel_id=1, source_target_pairs={{0,3},{1,2},{2,1},{3,0},{4,7},{5,6},{6,5},{7,4},{8,11},{9,10},{10,... | collective-permute-start | bytes 147464 | tf_op jit(solution)/shard_map/ppermute | solution.py:306
  15.0 2.7 %copy-start = (s32[64]{0:T(128)S(1)}, s32[64]{0:T(128)}, u32[]{:S(2)}) copy-start(s32[64]{0:T(128)} %param.14) | copy-start | bytes 772
  15.0 2.7 %copy-start.1 = (f32[2,128,128]{2,1,0:T(8,128)S(1)}, f32[2,128,128]{2,1,0:T(8,128)}, u32[]{:S(2)}) copy-start(f32[2,128,128]{2,1,0:T(8,128)} %constant.2.clone.overlap) | copy-start | bytes 393220

commit v6 on v5

--- a/solution.py
+++ b/solution.py
@@ -92,10 +92,11 @@
 
     stops = [last for last, _ in ready] + [lines] if ready else [0, lines]
     waits = [wait for _, wait in ready] if ready else [lambda: None]
-    idx_copy.wait()
     for first, stop, wait in zip(stops, stops[1:], waits):
         wait()
         turned(first, x_even)
+        if first == 0:
+            idx_copy.wait()
 
         @pl.loop(first // 2, stop // 2)
         def _(i):
@@ -106,7 +107,7 @@
             scatter(r + 1, x_odd)
 
 
-def own_kernel(s_own, param, grid_rows, zero, s_vmem, sems, *scratch):
+def own_kernel(s_own, param, grid_rows, basis, zero, s_vmem, sems, *scratch):
     lines = s_vmem.shape[0] // LANE
     starts = (0, lines // 4)
     ready = []
@@ -119,40 +120,42 @@
     spread_rows(s_vmem, param, grid_rows, *scratch, ready=ready)
 
 
-def other_kernel(held, s_rem, param, grid_rows, basis, zero, *scratch):
+def basis_rows(grid_rows, g, basis, at):
     bf16 = jnp.bfloat16
+    quarter = KMAX * KMAX * 4
+    for h in range(2):
+        vals = []
+        for part in range(2):
+            mm, mp, pm, pp = (
+                grid_rows[pl.ds(q * quarter + g * 4 * LANE + 2 * part + h, LANE, stride=4), :] for q in range(4)
+            )
+            a, c = pp + mm, pm + mp
+            b, d = (pp - mm, pm - mp) if part else (mm - pp, mp - pm)
+            vals.append((a + c, c - a, b + d, b - d))
+        re, im = vals
+        at_re, at_im = pl.ds(2 * h * LANE, LANE), pl.ds((2 * h + 1) * LANE, LANE)
+        for n in range(4):
+            to = pl.ds(pl.multiple_of((4 * at + n) * LANE, LANE), LANE)
+            one, two = (re[n], im[n]) if n < 2 else (im[n], re[n])
+            basis[to, at_re], basis[to, at_im] = one.astype(bf16), two.astype(bf16)
+
+
+def other_kernel(held, room, s_rem, param, grid_rows, basis, zero, *scratch):
     zero[...] = jnp.zeros_like(zero)
     spread_rows(s_rem, param, grid_rows, *scratch)
-    quarter = KMAX * KMAX * 4
 
     @pl.loop(0, KMAX * KMAX // LANE)
     def _(g):
-        to = lambda n: pl.ds(pl.multiple_of((4 * g + n) * LANE, LANE), LANE)
-        for h in range(2):
-            vals = []
-            for part in range(2):
-                mm, mp, pm, pp = (
-                    grid_rows[pl.ds(q * quarter + g * 4 * LANE + 2 * part + h, LANE, stride=4), :] for q in range(4)
-                )
-                a, b, c, d = pp + mm, pp - mm, pm + mp, pm - mp
-                vals.append((a + c, c - a, b + d, b - d))
-            re, im = vals
-            at_re, at_im = pl.ds(2 * h * LANE, LANE), pl.ds((2 * h + 1) * LANE, LANE)
-            for n in range(4):
-                if n < 2:
-                    basis[to(n), at_re], basis[to(n), at_im] = re[n].astype(bf16), im[n].astype(bf16)
-                else:
-                    basis[to(n), at_re], basis[to(n), at_im] = im[n].astype(bf16), (-re[n]).astype(bf16)
-
-
-def waves(source, basis, coef_even, coef_odd, tab, emit):
+        basis_rows(grid_rows, g, basis, g)
+
+
+def prepare(source, j, coef, tab, sub=32):
     f32, bf16 = jnp.float32, jnp.bfloat16
     half = lax.axis_index("beam")
-    blocks, step = source.shape[0], coef_even.shape[0]
-    per = step // LANE
-
-    def tables(j):
-        pos = source[j, 32:48, :].astype(f32).astype(jnp.int32)
+    step = coef.shape[0]
+
+    def tables(i):
+        pos = source[j + i, 32:48, :].astype(f32).astype(jnp.int32)
         pos = 32 * pos[0:4] + pos[4:8]
         pos = jnp.where(half == 0, pos[0:2], pos[2:4])
         px, py = pos[0:1], pos[1:2]
@@ -167,81 +170,90 @@
             jnp.broadcast_to(cx[4:5], (LANE, LANE)), jnp.broadcast_to(sx[4:5], (LANE, LANE)),
         )
         for n, t in enumerate(made):
-            tab[n, j * LANE : (j + 1) * LANE, :] = t.T
-
-    def coefficients(m, coef, sub=32):
-        for row in range(0, step, sub):
-            cy, sy, cx, sx, c4, s4 = (tab[n, m * step + row : m * step + row + sub, :] for n in range(6))
-            for g in range(KMAX // 4):
-                prods = (cx * cy, sx * sy, sx * cy, cx * sy)
-                for n, v in enumerate(prods):
-                    coef[row : row + sub, (4 * g + n) * LANE : (4 * g + n + 1) * LANE] = v.astype(bf16)
-                cx, sx = cx * c4 - sx * s4, sx * c4 + cx * s4
-
-    def prepare(m, coef):
-        for j in range(m * per, (m + 1) * per):
-            tables(j)
-        coefficients(m, coef)
-
-    prepare(0, coef_even)
-    steps = blocks // per
+            tab[n, i * LANE : (i + 1) * LANE, :] = t.T
+
+    for i in range(step // LANE):
+        tables(i)
+    for row in range(0, step, sub):
+        cy, sy, cx, sx, c4, s4 = (tab[n, row : row + sub, :] for n in range(6))
+        for g in range(KMAX // 4):
+            prods = (cx * cy, sx * sy, sx * cy, cx * sy)
+            for n, v in enumerate(prods):
+                coef[row : row + sub, (4 * g + n) * LANE : (4 * g + n + 1) * LANE] = v.astype(bf16)
+            cx, sx = cx * c4 - sx * s4, sx * c4 + cx * s4
+
+
+def near_kernel(basis, near, psi_near, coef_even, coef_odd, tab_even, tab_odd):
+    step = coef_even.shape[0]
+    turns = [(coef_even, tab_even), (coef_odd, tab_odd)]
+    prepare(near, 0, *turns[0])
+    steps = near.shape[0] * LANE // step
     for m in range(steps):
-        now, later = (coef_even, coef_odd) if m % 2 == 0 else (coef_odd, coef_even)
-        psi = jnp.dot(now[...], basis[...], preferred_element_type=f32)
+        psi = jnp.dot(turns[m % 2][0][...], basis[...], preferred_element_type=jnp.float32)
         if m + 1 < steps:
-            prepare(m + 1, later)
-        emit(m, psi)
-
-
-def near_kernel(basis, near, psi_near, coef_even, coef_odd, tab):
-    step = coef_even.shape[0]
-
-    def emit(m, psi):
+            prepare(near, (m + 1) * step // LANE, *turns[(m + 1) % 2])
         psi_near[m * step : (m + 1) * step, :] = psi
 
-    waves(near, basis, coef_even, coef_odd, tab, emit)
-
-
-def far_kernel(masks, basis, psi_near, near, far, cols, overlap, out, coef_even, coef_odd, tab, pots):
+
+def far_kernel(masks, basis, psi_near, near, far, cols, overlap, out, coef_even, coef_odd, tab_even, tab_odd, pots):
     f32, bf16 = jnp.float32, jnp.bfloat16
     column = lax.axis_index("probe")
     step = coef_even.shape[0]
     blocks = near.shape[0]
-    for n, source in enumerate((near, far)):
-        for j in range(blocks):
-            owner = column ^ masks[n * blocks + j]
-            pats = source[j, 0:32, :].astype(f32)
-            for t in range(4):
-                pots[pl.ds(pl.multiple_of(owner * 8, 8), 8), t * LANE : (t + 1) * LANE] = pats[8 * t : 8 * t + 8]
-    mine = (cols[...] == column).astype(f32)
-    left = (pots[...].T * mine).astype(bf16)
-    right = pots[...].astype(bf16)
-    g_re, g_im = overlap[0], overlap[1]
     mul = lambda a, b: jnp.dot(a, b, preferred_element_type=f32)
     forms = []
-    for h in range(2):
-        lr, li = left[h * LANE : (h + 1) * LANE], left[(2 + h) * LANE : (3 + h) * LANE]
-        rr, ri = right[:, h * LANE : (h + 1) * LANE], right[:, (2 + h) * LANE : (3 + h) * LANE]
-        r_re, r_im = mul(lr, rr) + mul(li, ri), mul(li, rr) - mul(lr, ri)
-        h_re, h_im = g_re * r_re - g_im * r_im, g_re * r_im + g_im * r_re
-        forms.append(
-            jnp.concatenate([jnp.concatenate([h_re, h_im], 1), jnp.concatenate([-h_im, h_re], 1)], 0).astype(bf16)
-        )
-
-    def energy(first, psi):
-        e = 0.0
+
+    def make_forms():
+        for n, source in enumerate((near, far)):
+            for j in range(blocks):
+                owner = column ^ masks[n * blocks + j]
+                pats = source[j, 0:32, :].astype(f32)
+                for t in range(4):
+                    pots[pl.ds(pl.multiple_of(owner * 8, 8), 8), t * LANE : (t + 1) * LANE] = pats[8 * t : 8 * t + 8]
+        mine = (cols[...] == column).astype(f32)
+        left = (pots[...].T * mine).astype(bf16)
+        right = pots[...].astype(bf16)
+        g_re, g_im = overlap[0], overlap[1]
         for h in range(2):
-            wave = psi[:, 2 * h * LANE : (2 * h + 2) * LANE]
-            v = wave * mul(wave.astype(bf16), forms[h])
-            e = e + v[:, :LANE] + v[:, LANE:]
+            lr, li = left[h * LANE : (h + 1) * LANE], left[(2 + h) * LANE : (3 + h) * LANE]
+            rr, ri = right[:, h * LANE : (h + 1) * LANE], right[:, (2 + h) * LANE : (3 + h) * LANE]
+            r_re, r_im = mul(lr, rr) + mul(li, ri), mul(li, rr) - mul(lr, ri)
+            h_re, h_im = g_re * r_re - g_im * r_im, g_re * r_im + g_im * r_re
+            forms.append(
+                jnp.concatenate([jnp.concatenate([h_re, h_im], 1), jnp.concatenate([-h_im, h_re], 1)], 0).astype(bf16)
+            )
+
+    def half_energy(wave, h):
+        v = wave * mul(wave.astype(bf16), forms[h])
+        return v[:, :LANE] + v[:, LANE:]
+
+    def finish(first, e):
         for i in range(step // LANE):
             out[pl.ds(column ^ masks[first + i], 1), :] = jnp.sum(e[i * LANE : (i + 1) * LANE].T, axis=0, keepdims=True)
 
-    def emit(m, psi):
-        energy(blocks + m * step // LANE, psi)
-        energy(m * step // LANE, psi_near[m * step : (m + 1) * step, :])
-
-    waves(far, basis, coef_even, coef_odd, tab, emit)
+    turns = [(coef_even, tab_even), (coef_odd, tab_odd)]
+    prepare(far, 0, *turns[0])
+    cols_of = [slice(2 * h * LANE, (2 * h + 2) * LANE) for h in range(2)]
+    units = [(m, h) for m in range(far.shape[0] * LANE // step) for h in range(2)]
+    waiting, e = None, 0.0
+    for m, h in units + [(None, None)]:
+        if m is not None:
+            wave = mul(turns[m % 2][0][...], basis[:, cols_of[h]])
+            if h == 0 and (m + 1, 0) in units:
+                prepare(far, (m + 1) * step // LANE, *turns[(m + 1) % 2])
+            if (m, h) == (0, 0):
+                make_forms()
+            if (m, h) == (0, 1):
+                for first in range(0, psi_near.shape[0], step):
+                    rows = slice(first, first + step)
+                    finish(first // LANE, sum(half_energy(psi_near[rows, cols_of[k]], k) for k in range(2)))
+        if waiting is not None:
+            old_m, old_h, old = waiting
+            part = half_energy(old, old_h)
+            e = part if old_h == 0 else e + part
+            if old_h == 1:
+                finish(blocks + old_m * step // LANE, e)
+        waiting = (m, h, wave)
 
 
 def shards(smatrix, aperture, aberration, beam_k, probe_pos, patches, patch_col):
@@ -268,8 +280,7 @@
         cost_estimate=cost(10**9),
     )(*(pltpu.with_memory_space_constraint(v, pltpu.HBM) for v in raw))
     param_rem = swap(param)
-    later, _ = lax.optimization_barrier((s_own, small))
-    s_rem = swap(later)
+    s_rem = swap(s_own)
 
     turning = [
         pltpu.VMEM((4 * LANE, LANE), f32),
@@ -278,26 +289,27 @@
         pltpu.SMEM((rows,), jnp.int32),
         pltpu.SemaphoreType.DMA,
     ]
-    held_shape = sds((4 * grid + 24, LANE), f32)
-    held, zero_own = pl.pallas_call(
+    held_shape = sds((4 * grid, LANE), f32)
+    basis_shape = sds((grid, width), bf16)
+    held, room, zero_own = pl.pallas_call(
         own_kernel,
-        out_shape=(held_shape, message),
+        out_shape=(held_shape, basis_shape, message),
         in_specs=[hbm, vmem],
-        out_specs=(vmem,) * 2,
+        out_specs=(vmem,) * 3,
         scratch_shapes=[pltpu.VMEM((rows, width), bf16), pltpu.SemaphoreType.DMA((2,))] + turning,
         compiler_params=params,
         cost_estimate=cost(3 * 10**9),
     )(pltpu.with_memory_space_constraint(s_own, pltpu.HBM), param)
     _, basis, zero_other = pl.pallas_call(
         other_kernel,
-        out_shape=(held_shape, sds((grid, width), bf16), message),
-        in_specs=[vmem] * 3,
+        out_shape=(held_shape, basis_shape, message),
+        in_specs=[vmem] * 4,
         out_specs=(vmem,) * 3,
         scratch_shapes=turning,
-        input_output_aliases={0: 0},
+        input_output_aliases={0: 0, 1: 1},
         compiler_params=params,
         cost_estimate=cost(4 * 10**9),
-    )(held, s_rem, param_rem)
+    )(held, room, s_rem, param_rem)
 
     steps = [1 << n for n in range(blocks.bit_length() - 1)]
     steps = steps[-2:] + steps[:-2][::-1]
@@ -315,11 +327,12 @@
     working = [
         pltpu.VMEM((2 * LANE, grid), bf16),
         pltpu.VMEM((2 * LANE, grid), bf16),
-        pltpu.VMEM((6, probes, LANE), f32),
+        pltpu.VMEM((6, 2 * LANE, LANE), f32),
+        pltpu.VMEM((6, 2 * LANE, LANE), f32),
     ]
     psi_near = pl.pallas_call(
         near_kernel,
-        out_shape=jax.ShapeDtypeStruct((probes, width), f32),
+        out_shape=sds((probes, width), f32),
         in_specs=[vmem] * 2,
         out_specs=vmem,
         scratch_shapes=working,

time: 30.8 us -> 30.7 us (level)
  transfers between devices with their start and end apart: 5 -> 5, of which waited for: 0 -> 1; matrix products, arithmetic and copies ran while one was open for 0% -> 0% of each run, Pallas kernels for 31% -> 33%
where the time goes in v6:
time: 30.7 us; the launch traced here: 30.4 us
  Pallas kernels  13.4 us (44%)
  blocking collectives  9.06 us (30%)
  starting transfers between devices  7.17 us (23%)
  local copies, waits for them, and re-layouts  0.6 us (2%)
    all_to_all x1, blocking collectives, shards(): return lax.all_to_all(energy, 'probe', 0, 0, tiled=True)  9.06 us
    ppermute x3, starting transfers between devices, shards(): lax.ppermute(small, ('probe', 'beam'), [(2 * i + b, 2 * (i ^ reach) + 1 -...  6.71 us
    pallas_call x1, Pallas kernels, shards(): pl.pallas_call(other_kernel, out_shape=(held_shape, basis_shape, message)...  3.67 us
    pallas_call x1, Pallas kernels, shards(): pl.pallas_call(functools.partial(far_kernel, tuple(masks)), out_shape=jax...  3.24 us
    pallas_call x1, Pallas kernels, shards(): pl.pallas_call(own_kernel, out_shape=(held_shape, basis_shape, message),...  2.96 us
    pallas_call x1, Pallas kernels, shards(): pl.pallas_call(near_kernel, out_shape=sds((probes, width), f32), in_specs...  2.63 us
    pallas_call x1, Pallas kernels, shards(): pl.pallas_call(pack_kernel, out_shape=(message, sds((3 * lines, LANE), f3...  0.86 us
  transfers between devices with their start and end apart: 5, of which 1 were waited for; matrix products, arithmetic and copies ran while one was open for 0% of the time, Pallas kernels for 33%

profile of v6, /device:TPU:0, one launch (start us, length us, event | category | flops | bytes accessed | tf_op | source)
XLA Modules:
  0.0 30.4 jit_solution(16592077042562832158)
XLA Ops:
  0.0 0.5 %collective-permute-start = (bf16[2048,512]{1,0:T(8,128)(2,1)}, bf16[2048,512]{1,0:T(8,128)(2,1)S(1)}, u32[]{:S(2)}, u32[]{:S(2)}) collective-permute-start(bf16[2048,512]{1,0:T(8,128)(2,1)} %bitcast.13), channel_id=1, source_target_pairs={{0,1},{1,0},{2,3},{3,2},{4,5},{5,4},{6,7},{7,6},{8,9},{9,8},{10,11... | collective-permute-start | bytes 6291464 | tf_op jit(solution)/shard_map/ppermute | solution.py:264
  0.5 0.9 %shard_map.82 = (bf16[1,48,128]{2,1,0:T(8,128)(2,1)S(1)}, f32[48,128]{1,0:T(8,128)S(1)}) custom-call(f32[16,128]{1,0:T(8,128)} %bitcast.15, f32[16,128]{1,0:T(8,128)} %bitcast.16, s32[2,2048]{1,0:T(2,128)} %k_hbm.1, s32[2,256]{1,0:T(2,128)} %pos_hbm.1, bf16[8,512]{1,0:T(8,128)(2,1)} %patches.1), custom_call_target="tpu_custom_call" | custom-call | flops 1000000000 | bytes 4194304 | tf_op jit(solution)/shard_map/pallas_call | solution.py:273
  1.3 2.8 %collective-permute-start.2 = (bf16[1,48,128]{2,1,0:T(8,128)(2,1)S(1)}, bf16[1,48,128]{2,1,0:T(8,128)(2,1)S(1)}, u32[]{:S(2)}, u32[]{:S(2)}) collective-permute-start(bf16[1,48,128]{2,1,0:T(8,128)(2,1)S(1)} %get-tuple-element.16), channel_id=1, source_target_pairs={{0,5},{1,4},{2,7},{3,6},{4,1},{5,0},{6,3},{7,2},{8,13},{9,12},{10,... | collective-permute-start | bytes 36872 | tf_op jit(solution)/shard_map/ppermute | solution.py:318
  4.1 0.0 collective-permute-start.1
  4.1 3.0 %shard_map.83 = (f32[16384,128]{1,0:T(8,128)S(1)}, bf16[4096,512]{1,0:T(8,128)(2,1)S(1)}, bf16[1,48,128]{2,1,0:T(8,128)(2,1)S(1)}) custom-call(bf16[2048,512]{1,0:T(8,128)(2,1)} %bitcast.14, f32[48,128]{1,0:T(8,128)S(1)} %get-tuple-element.12.param), custom_call_target="tpu_custom_call" | custom-call | flops 3000000000 | bytes 4194304 | tf_op jit(solution)/shard_map/pallas_call | solution.py:294
  7.1 0.0 collective-permute-done.2
  7.1 2.8 %collective-permute-start.3 = (bf16[2,48,128]{2,1,0:T(8,128)(2,1)S(1)}, bf16[2,48,128]{2,1,0:T(8,128)(2,1)S(1)}, u32[]{:S(2)}, u32[]{:S(2)}) collective-permute-start(bf16[2,48,128]{2,1,0:T(8,128)(2,1)S(1)} %pad_maximum_fusion.1), channel_id=1, source_target_pairs={{0,9},{1,8},{2,11},{3,10},{4,13},{5,12},{6,15},{7,14},{8,1},{9,0},... | collective-permute-start | bytes 73736 | tf_op jit(solution)/shard_map/ppermute | solution.py:318
  9.9 0.0 collective-permute-done.1.param
  9.9 0.0 collective-permute-done.s_rem
  9.9 3.7 %shard_map.84 = (f32[16384,128]{1,0:T(8,128)S(1)}, bf16[4096,512]{1,0:T(8,128)(2,1)S(1)}, bf16[1,48,128]{2,1,0:T(8,128)(2,1)S(1)}) custom-call(f32[16384,128]{1,0:T(8,128)S(1)} %get-tuple-element.13.held, bf16[4096,512]{1,0:T(8,128)(2,1)S(1)} %get-tuple-element.14.room, ...), custom_call_target="tpu_custom_call", output_to_operand_aliasing={{0}: (0, {}), {1}: (1, {})} | custom-call | flops 4000000000 | bytes 4194304 | tf_op jit(solution)/shard_map/pallas_call | solution.py:303
  13.5 0.0 collective-permute-done.3
  13.6 1.2 %collective-permute-start.4 = (bf16[4,48,128]{2,1,0:T(8,128)(2,1)S(1)}, bf16[4,48,128]{2,1,0:T(8,128)(2,1)S(1)}, u32[]{:S(2)}, u32[]{:S(2)}) collective-permute-start(bf16[4,48,128]{2,1,0:T(8,128)(2,1)S(1)} %pad_maximum_fusion.near), channel_id=1, source_target_pairs={{0,3},{1,2},{2,1},{3,0},{4,7},{5,6},{6,5},{7,4},{8,11},{9,10},{10,... | collective-permute-start | bytes 147464 | tf_op jit(solution)/shard_map/ppermute | solution.py:318
  14.8 0.0 copy-start
  14.8 0.0 copy-start.1
  14.8 2.6 %shard_map.85.psi_near = f32[512,512]{1,0:T(8,128)S(1)} custom-call(bf16[4096,512]{1,0:T(8,128)(2,1)S(1)} %get-tuple-element.15.basis, bf16[4,48,128]{2,1,0:T(8,128)(2,1)S(1)} %pad_maximum_fusion.near), custom_call_target="tpu_custom_call" | custom-call | flops 4000000000 | bytes 4194304 | tf_op jit(solution)/shard_map/pallas_call | solution.py:333
  17.4 0.1 collective-permute-done.4.far
  17.5 0.0 copy-done
  17.5 0.0 copy-done.1
  17.5 3.2 %shard_map.86 = f32[8,128]{1,0:T(8,128)S(1)} custom-call(bf16[4096,512]{1,0:T(8,128)(2,1)S(1)} %get-tuple-element.15.basis, f32[512,512]{1,0:T(8,128)S(1)} %shard_map.85.psi_near, bf16[4,48,128]{2,1,0:T(8,128)(2,1)S(1)} %pad_maximum_fusion.near, bf16[4,48,128]{2,1,0:T(8,128)(2,1)S(1)} %collective-permute-done.4.far, s32[1,64]{1,0:T(1,128)S(1)} %bitcast.11, ...), custom_call_target="tpu_custom_call" | custom-call | flops 4000000000 | bytes 4194304 | tf_op jit(solution)/shard_map/pallas_call | solution.py:342
  20.7 9.1 %all_to_all.12 = f32[8,1,128]{2,1,0:T(1,128)S(1)} all-to-all(f32[8,1,128]{2,1,0:T(1,128)S(1)} %bitcast.10), channel_id=1, replica_groups=mesh['grp'=2,'probe'=8,'beam'=2] {'probe'}, dimensions={0} | all-to-all | bytes 8192 | tf_op jit(solution)/shard_map/all_to_all | solution.py:351
  29.8 0.6 %copy.15 = f32[8,128]{1,0:T(8,128)} copy(f32[8,128]{1,0:T(8,128)S(1)} %bitcast.12) | data formatting | bytes 8192
  (4 shorter events, 0.0 us)
Async XLA Ops:
  0.0 9.9 %collective-permute-start = (bf16[2048,512]{1,0:T(8,128)(2,1)}, bf16[2048,512]{1,0:T(8,128)(2,1)S(1)}, u32[]{:S(2)}, u32[]{:S(2)}) collective-permute-start(bf16[2048,512]{1,0:T(8,128)(2,1)} %bitcast.13), channel_id=1, source_target_pairs={{0,1},{1,0},{2,3},{3,2},{4,5},{5,4},{6,7},{7,6},{8,9},{9,8},{10,11... | collective-permute-start | bytes 6291464 | tf_op jit(solution)/shard_map/ppermute | solution.py:264
  1.3 5.7 %collective-permute-start.2 = (bf16[1,48,128]{2,1,0:T(8,128)(2,1)S(1)}, bf16[1,48,128]{2,1,0:T(8,128)(2,1)S(1)}, u32[]{:S(2)}, u32[]{:S(2)}) collective-permute-start(bf16[1,48,128]{2,1,0:T(8,128)(2,1)S(1)} %get-tuple-element.16), channel_id=1, source_target_pairs={{0,5},{1,4},{2,7},{3,6},{4,1},{5,0},{6,3},{7,2},{8,13},{9,12},{10,... | collective-permute-start | bytes 36872 | tf_op jit(solution)/shard_map/ppermute | solution.py:318
  4.1 5.8 %collective-permute-start.1 = (f32[48,128]{1,0:T(8,128)S(1)}, f32[48,128]{1,0:T(8,128)S(1)}, u32[]{:S(2)}, u32[]{:S(2)}) collective-permute-start(f32[48,128]{1,0:T(8,128)S(1)} %get-tuple-element.12.param), channel_id=1, source_target_pairs={{0,1},{1,0},{2,3},{3,2},{4,5},{5,4},{6,7},{7,6},{8,9},{9,8},{10,11... | collective-permute-start | bytes 73736 | tf_op jit(solution)/shard_map/ppermute | solution.py:264
  7.1 6.5 %collective-permute-start.3 = (bf16[2,48,128]{2,1,0:T(8,128)(2,1)S(1)}, bf16[2,48,128]{2,1,0:T(8,128)(2,1)S(1)}, u32[]{:S(2)}, u32[]{:S(2)}) collective-permute-start(bf16[2,48,128]{2,1,0:T(8,128)(2,1)S(1)} %pad_maximum_fusion.1), channel_id=1, source_target_pairs={{0,9},{1,8},{2,11},{3,10},{4,13},{5,12},{6,15},{7,14},{8,1},{9,0},... | collective-permute-start | bytes 73736 | tf_op jit(solution)/shard_map/ppermute | solution.py:318
  13.6 3.9 %collective-permute-start.4 = (bf16[4,48,128]{2,1,0:T(8,128)(2,1)S(1)}, bf16[4,48,128]{2,1,0:T(8,128)(2,1)S(1)}, u32[]{:S(2)}, u32[]{:S(2)}) collective-permute-start(bf16[4,48,128]{2,1,0:T(8,128)(2,1)S(1)} %pad_maximum_fusion.near), channel_id=1, source_target_pairs={{0,3},{1,2},{2,1},{3,0},{4,7},{5,6},{6,5},{7,4},{8,11},{9,10},{10,... | collective-permute-start | bytes 147464 | tf_op jit(solution)/shard_map/ppermute | solution.py:318
  14.8 2.7 %copy-start = (s32[64]{0:T(128)S(1)}, s32[64]{0:T(128)}, u32[]{:S(2)}) copy-start(s32[64]{0:T(128)} %param.14) | copy-start | bytes 772
  14.8 2.7 %copy-start.1 = (f32[2,128,128]{2,1,0:T(8,128)S(1)}, f32[2,128,128]{2,1,0:T(8,128)}, u32[]{:S(2)}) copy-start(f32[2,128,128]{2,1,0:T(8,128)} %constant.2.clone.overlap) | copy-start | bytes 393220

commit v7 on v6

--- a/solution.py
+++ b/solution.py
@@ -50,7 +50,7 @@
     pats = pat_v[...].astype(f32)
     pos = jnp.concatenate([pos_v[:, :LANE], pos_v[:, LANE:]], 0)
     tiles = [pats[:, t * LANE : (t + 1) * LANE] for t in range(pats.shape[1] // LANE)]
-    split = [(pos // 32).astype(f32), (pos % 32).astype(f32), jnp.zeros((8, LANE), f32)]
+    split = [(pos // 32).astype(f32), (pos % 32).astype(f32)]
     message = jnp.concatenate(tiles + [jnp.concatenate(split, 0)], 0)
     small[0] = message.astype(bf16)
     lines = amp_v.shape[0]
@@ -144,9 +144,10 @@
     zero[...] = jnp.zeros_like(zero)
     spread_rows(s_rem, param, grid_rows, *scratch)
 
-    @pl.loop(0, KMAX * KMAX // LANE)
+    @pl.loop(0, KMAX * KMAX // LANE // 2)
     def _(g):
-        basis_rows(grid_rows, g, basis, g)
+        basis_rows(grid_rows, 2 * g, basis, 2 * g)
+        basis_rows(grid_rows, 2 * g + 1, basis, 2 * g + 1)
 
 
 def prepare(source, j, coef, tab, sub=32):
@@ -155,7 +156,7 @@
     step = coef.shape[0]
 
     def tables(i):
-        pos = source[j + i, 32:48, :].astype(f32).astype(jnp.int32)
+        pos = source[j + i].astype(f32)[32:40].astype(jnp.int32)
         pos = 32 * pos[0:4] + pos[4:8]
         pos = jnp.where(half == 0, pos[0:2], pos[2:4])
         px, py = pos[0:1], pos[1:2]
@@ -207,7 +208,7 @@
         for n, source in enumerate((near, far)):
             for j in range(blocks):
                 owner = column ^ masks[n * blocks + j]
-                pats = source[j, 0:32, :].astype(f32)
+                pats = source[j].astype(f32)
                 for t in range(4):
                     pots[pl.ds(pl.multiple_of(owner * 8, 8), 8), t * LANE : (t + 1) * LANE] = pats[8 * t : 8 * t + 8]
         mine = (cols[...] == column).astype(f32)
@@ -267,7 +268,7 @@
     params = pltpu.CompilerParams(vmem_limit_bytes=24 * 1024 * 1024)
     cost = lambda n: pl.CostEstimate(flops=n, bytes_accessed=4 * 2**20, transcendentals=0)
 
-    message = sds((1, 48, LANE), bf16)
+    message = sds((1, 40, LANE), bf16)
     s_own = smatrix.reshape(rows, width)
     raw = (aperture.reshape(lines, LANE), aberration.reshape(lines, LANE), beam_k, probe_pos, patches)
     small, param = pl.pallas_call(

time: 30.7 us -> 30.5 us (level)
  transfers between devices with their start and end apart: 5 -> 5, of which waited for: 1 -> 0; matrix products, arithmetic and copies ran while one was open for 0% -> 0% of each run, Pallas kernels for 33% -> 33%
where the time goes in v7:
time: 30.5 us; the launch traced here: 30.2 us
  Pallas kernels  13.4 us (44%)
  blocking collectives  8.94 us (29%)
  starting transfers between devices  7.17 us (24%)
  local copies, waits for them, and re-layouts  0.6 us (2%)
    all_to_all x1, blocking collectives, shards(): return lax.all_to_all(energy, 'probe', 0, 0, tiled=True)  8.94 us
    ppermute x3, starting transfers between devices, shards(): lax.ppermute(small, ('probe', 'beam'), [(2 * i + b, 2 * (i ^ reach) + 1 -...  6.71 us
    pallas_call x1, Pallas kernels, shards(): pl.pallas_call(other_kernel, out_shape=(held_shape, basis_shape, message)...  3.64 us
    pallas_call x1, Pallas kernels, shards(): pl.pallas_call(functools.partial(far_kernel, tuple(masks)), out_shape=jax...  3.29 us
    pallas_call x1, Pallas kernels, shards(): pl.pallas_call(own_kernel, out_shape=(held_shape, basis_shape, message),...  2.96 us
    pallas_call x1, Pallas kernels, shards(): pl.pallas_call(near_kernel, out_shape=sds((probes, width), f32), in_specs...  2.63 us
    pallas_call x1, Pallas kernels, shards(): pl.pallas_call(pack_kernel, out_shape=(message, sds((3 * lines, LANE), f3...  0.86 us
  transfers between devices with their start and end apart: 5, of which 0 were waited for; matrix products, arithmetic and copies ran while one was open for 0% of the time, Pallas kernels for 33%

profile of v7, /device:TPU:0, one launch (start us, length us, event | category | flops | bytes accessed | tf_op | source)
XLA Modules:
  0.0 30.2 jit_solution(1275173468283783490)
XLA Ops:
  0.0 0.5 %collective-permute-start = (bf16[2048,512]{1,0:T(8,128)(2,1)}, bf16[2048,512]{1,0:T(8,128)(2,1)S(1)}, u32[]{:S(2)}, u32[]{:S(2)}) collective-permute-start(bf16[2048,512]{1,0:T(8,128)(2,1)} %bitcast.13), channel_id=1, source_target_pairs={{0,1},{1,0},{2,3},{3,2},{4,5},{5,4},{6,7},{7,6},{8,9},{9,8},{10,11... | collective-permute-start | bytes 6291464 | tf_op jit(solution)/shard_map/ppermute | solution.py:265
  0.5 0.9 %shard_map.82 = (bf16[1,40,128]{2,1,0:T(8,128)(2,1)S(1)}, f32[48,128]{1,0:T(8,128)S(1)}) custom-call(f32[16,128]{1,0:T(8,128)} %bitcast.15, f32[16,128]{1,0:T(8,128)} %bitcast.16, s32[2,2048]{1,0:T(2,128)} %k_hbm.1, s32[2,256]{1,0:T(2,128)} %pos_hbm.1, bf16[8,512]{1,0:T(8,128)(2,1)} %patches.1), custom_call_target="tpu_custom_call" | custom-call | flops 1000000000 | bytes 4194304 | tf_op jit(solution)/shard_map/pallas_call | solution.py:274
  1.3 2.8 %collective-permute-start.2 = (bf16[1,40,128]{2,1,0:T(8,128)(2,1)S(1)}, bf16[1,40,128]{2,1,0:T(8,128)(2,1)S(1)}, u32[]{:S(2)}, u32[]{:S(2)}) collective-permute-start(bf16[1,40,128]{2,1,0:T(8,128)(2,1)S(1)} %get-tuple-element.16), channel_id=1, source_target_pairs={{0,5},{1,4},{2,7},{3,6},{4,1},{5,0},{6,3},{7,2},{8,13},{9,12},{10,... | collective-permute-start | bytes 30728 | tf_op jit(solution)/shard_map/ppermute | solution.py:319
  4.1 0.0 collective-permute-start.1
  4.1 3.0 %shard_map.83 = (f32[16384,128]{1,0:T(8,128)S(1)}, bf16[4096,512]{1,0:T(8,128)(2,1)S(1)}, bf16[1,40,128]{2,1,0:T(8,128)(2,1)S(1)}) custom-call(bf16[2048,512]{1,0:T(8,128)(2,1)} %bitcast.14, f32[48,128]{1,0:T(8,128)S(1)} %get-tuple-element.12.param), custom_call_target="tpu_custom_call" | custom-call | flops 3000000000 | bytes 4194304 | tf_op jit(solution)/shard_map/pallas_call | solution.py:295
  7.1 0.0 collective-permute-done.2
  7.1 2.8 %collective-permute-start.3 = (bf16[2,40,128]{2,1,0:T(8,128)(2,1)S(1)}, bf16[2,40,128]{2,1,0:T(8,128)(2,1)S(1)}, u32[]{:S(2)}, u32[]{:S(2)}) collective-permute-start(bf16[2,40,128]{2,1,0:T(8,128)(2,1)S(1)} %pad_maximum_fusion.1), channel_id=1, source_target_pairs={{0,9},{1,8},{2,11},{3,10},{4,13},{5,12},{6,15},{7,14},{8,1},{9,0},... | collective-permute-start | bytes 61448 | tf_op jit(solution)/shard_map/ppermute | solution.py:319
  9.9 0.0 collective-permute-done.1.param
  9.9 0.0 collective-permute-done.s_rem
  9.9 3.6 %shard_map.84 = (f32[16384,128]{1,0:T(8,128)S(1)}, bf16[4096,512]{1,0:T(8,128)(2,1)S(1)}, bf16[1,40,128]{2,1,0:T(8,128)(2,1)S(1)}) custom-call(f32[16384,128]{1,0:T(8,128)S(1)} %get-tuple-element.13.held, bf16[4096,512]{1,0:T(8,128)(2,1)S(1)} %get-tuple-element.14.room, ...), custom_call_target="tpu_custom_call", output_to_operand_aliasing={{0}: (0, {}), {1}: (1, {})} | custom-call | flops 4000000000 | bytes 4194304 | tf_op jit(solution)/shard_map/pallas_call | solution.py:304
  13.5 0.0 collective-permute-done.3
  13.6 1.2 %collective-permute-start.4 = (bf16[4,40,128]{2,1,0:T(8,128)(2,1)S(1)}, bf16[4,40,128]{2,1,0:T(8,128)(2,1)S(1)}, u32[]{:S(2)}, u32[]{:S(2)}) collective-permute-start(bf16[4,40,128]{2,1,0:T(8,128)(2,1)S(1)} %pad_maximum_fusion.near), channel_id=1, source_target_pairs={{0,3},{1,2},{2,1},{3,0},{4,7},{5,6},{6,5},{7,4},{8,11},{9,10},{10,... | collective-permute-start | bytes 122888 | tf_op jit(solution)/shard_map/ppermute | solution.py:319
  14.7 0.0 copy-start
  14.7 0.0 copy-start.1
  14.7 2.6 %shard_map.85.psi_near = f32[512,512]{1,0:T(8,128)S(1)} custom-call(bf16[4096,512]{1,0:T(8,128)(2,1)S(1)} %get-tuple-element.15.basis, bf16[4,40,128]{2,1,0:T(8,128)(2,1)S(1)} %pad_maximum_fusion.near), custom_call_target="tpu_custom_call" | custom-call | flops 4000000000 | bytes 4194304 | tf_op jit(solution)/shard_map/pallas_call | solution.py:334
  17.4 0.0 collective-permute-done.4.far
  17.4 0.0 copy-done
  17.4 0.0 copy-done.1
  17.4 3.3 %shard_map.86 = f32[8,128]{1,0:T(8,128)S(1)} custom-call(bf16[4096,512]{1,0:T(8,128)(2,1)S(1)} %get-tuple-element.15.basis, f32[512,512]{1,0:T(8,128)S(1)} %shard_map.85.psi_near, bf16[4,40,128]{2,1,0:T(8,128)(2,1)S(1)} %pad_maximum_fusion.near, bf16[4,40,128]{2,1,0:T(8,128)(2,1)S(1)} %collective-permute-done.4.far, s32[1,64]{1,0:T(1,128)S(1)} %bitcast.11, ...), custom_call_target="tpu_custom_call" | custom-call | flops 4000000000 | bytes 4194304 | tf_op jit(solution)/shard_map/pallas_call | solution.py:343
  20.7 8.9 %all_to_all.12 = f32[8,1,128]{2,1,0:T(1,128)S(1)} all-to-all(f32[8,1,128]{2,1,0:T(1,128)S(1)} %bitcast.10), channel_id=1, replica_groups=mesh['grp'=2,'probe'=8,'beam'=2] {'probe'}, dimensions={0} | all-to-all | bytes 8192 | tf_op jit(solution)/shard_map/all_to_all | solution.py:352
  29.7 0.6 %copy.15 = f32[8,128]{1,0:T(8,128)} copy(f32[8,128]{1,0:T(8,128)S(1)} %bitcast.12) | data formatting | bytes 8192
  (4 shorter events, 0.0 us)
Async XLA Ops:
  0.0 9.9 %collective-permute-start = (bf16[2048,512]{1,0:T(8,128)(2,1)}, bf16[2048,512]{1,0:T(8,128)(2,1)S(1)}, u32[]{:S(2)}, u32[]{:S(2)}) collective-permute-start(bf16[2048,512]{1,0:T(8,128)(2,1)} %bitcast.13), channel_id=1, source_target_pairs={{0,1},{1,0},{2,3},{3,2},{4,5},{5,4},{6,7},{7,6},{8,9},{9,8},{10,11... | collective-permute-start | bytes 6291464 | tf_op jit(solution)/shard_map/ppermute | solution.py:265
  1.3 5.7 %collective-permute-start.2 = (bf16[1,40,128]{2,1,0:T(8,128)(2,1)S(1)}, bf16[1,40,128]{2,1,0:T(8,128)(2,1)S(1)}, u32[]{:S(2)}, u32[]{:S(2)}) collective-permute-start(bf16[1,40,128]{2,1,0:T(8,128)(2,1)S(1)} %get-tuple-element.16), channel_id=1, source_target_pairs={{0,5},{1,4},{2,7},{3,6},{4,1},{5,0},{6,3},{7,2},{8,13},{9,12},{10,... | collective-permute-start | bytes 30728 | tf_op jit(solution)/shard_map/ppermute | solution.py:319
  4.1 5.8 %collective-permute-start.1 = (f32[48,128]{1,0:T(8,128)S(1)}, f32[48,128]{1,0:T(8,128)S(1)}, u32[]{:S(2)}, u32[]{:S(2)}) collective-permute-start(f32[48,128]{1,0:T(8,128)S(1)} %get-tuple-element.12.param), channel_id=1, source_target_pairs={{0,1},{1,0},{2,3},{3,2},{4,5},{5,4},{6,7},{7,6},{8,9},{9,8},{10,11... | collective-permute-start | bytes 73736 | tf_op jit(solution)/shard_map/ppermute | solution.py:265
  7.1 6.4 %collective-permute-start.3 = (bf16[2,40,128]{2,1,0:T(8,128)(2,1)S(1)}, bf16[2,40,128]{2,1,0:T(8,128)(2,1)S(1)}, u32[]{:S(2)}, u32[]{:S(2)}) collective-permute-start(bf16[2,40,128]{2,1,0:T(8,128)(2,1)S(1)} %pad_maximum_fusion.1), channel_id=1, source_target_pairs={{0,9},{1,8},{2,11},{3,10},{4,13},{5,12},{6,15},{7,14},{8,1},{9,0},... | collective-permute-start | bytes 61448 | tf_op jit(solution)/shard_map/ppermute | solution.py:319
  13.6 3.8 %collective-permute-start.4 = (bf16[4,40,128]{2,1,0:T(8,128)(2,1)S(1)}, bf16[4,40,128]{2,1,0:T(8,128)(2,1)S(1)}, u32[]{:S(2)}, u32[]{:S(2)}) collective-permute-start(bf16[4,40,128]{2,1,0:T(8,128)(2,1)S(1)} %pad_maximum_fusion.near), channel_id=1, source_target_pairs={{0,3},{1,2},{2,1},{3,0},{4,7},{5,6},{6,5},{7,4},{8,11},{9,10},{10,... | collective-permute-start | bytes 122888 | tf_op jit(solution)/shard_map/ppermute | solution.py:319
  14.7 2.7 %copy-start = (s32[64]{0:T(128)S(1)}, s32[64]{0:T(128)}, u32[]{:S(2)}) copy-start(s32[64]{0:T(128)} %param.14) | copy-start | bytes 772
  14.7 2.7 %copy-start.1 = (f32[2,128,128]{2,1,0:T(8,128)S(1)}, f32[2,128,128]{2,1,0:T(8,128)}, u32[]{:S(2)}) copy-start(f32[2,128,128]{2,1,0:T(8,128)} %constant.2.clone.overlap) | copy-start | bytes 393220

commit v8 on v7

--- a/solution.py
+++ b/solution.py
@@ -281,7 +281,8 @@
         cost_estimate=cost(10**9),
     )(*(pltpu.with_memory_space_constraint(v, pltpu.HBM) for v in raw))
     param_rem = swap(param)
-    s_rem = swap(s_own)
+    later, _ = lax.optimization_barrier((s_own, small))
+    s_rem = swap(later)
 
     turning = [
         pltpu.VMEM((4 * LANE, LANE), f32),

time: 30.5 us -> 30.5 us (level)
  transfers between devices with their start and end apart: 5 -> 5, of which waited for: 0 -> 0; matrix products, arithmetic and copies ran while one was open for 0% -> 0% of each run, Pallas kernels for 33% -> 31%
where the time goes in v8:
time: 30.5 us; the launch traced here: 30.2 us
  Pallas kernels  13.4 us (44%)
  blocking collectives  8.83 us (29%)
  starting transfers between devices  7.24 us (24%)
  local copies, waits for them, and re-layouts  0.6 us (2%)
    all_to_all x1, blocking collectives, shards(): return lax.all_to_all(energy, 'probe', 0, 0, tiled=True)  8.83 us
    ppermute x3, starting transfers between devices, shards(): lax.ppermute(small, ('probe', 'beam'), [(2 * i + b, 2 * (i ^ reach) + 1 -...  6.66 us
    pallas_call x1, Pallas kernels, shards(): pl.pallas_call(other_kernel, out_shape=(held_shape, basis_shape, message)...  3.64 us
    pallas_call x1, Pallas kernels, shards(): pl.pallas_call(functools.partial(far_kernel, tuple(masks)), out_shape=jax...  3.29 us
    pallas_call x1, Pallas kernels, shards(): pl.pallas_call(own_kernel, out_shape=(held_shape, basis_shape, message),...  2.96 us
    pallas_call x1, Pallas kernels, shards(): pl.pallas_call(near_kernel, out_shape=sds((probes, width), f32), in_specs...  2.63 us
    pallas_call x1, Pallas kernels, shards(): pl.pallas_call(pack_kernel, out_shape=(message, sds((3 * lines, LANE), f3...  0.86 us
  transfers between devices with their start and end apart: 5, of which 0 were waited for; matrix products, arithmetic and copies ran while one was open for 0% of the time, Pallas kernels for 31%

profile of v8, /device:TPU:0, one launch (start us, length us, event | category | flops | bytes accessed | tf_op | source)
XLA Modules:
  0.0 30.2 jit_solution(12787849646382116735)
XLA Ops:
  0.0 0.9 %shard_map.82 = (bf16[1,40,128]{2,1,0:T(8,128)(2,1)S(1)}, f32[48,128]{1,0:T(8,128)S(1)}) custom-call(f32[16,128]{1,0:T(8,128)} %bitcast.15, f32[16,128]{1,0:T(8,128)} %bitcast.16, s32[2,2048]{1,0:T(2,128)} %k_hbm.1, s32[2,256]{1,0:T(2,128)} %pos_hbm.1, bf16[8,512]{1,0:T(8,128)(2,1)} %patches.1), custom_call_target="tpu_custom_call" | custom-call | flops 1000000000 | bytes 4194304 | tf_op jit(solution)/shard_map/pallas_call | solution.py:274
  0.9 0.5 %collective-permute-start = (bf16[2048,512]{1,0:T(8,128)(2,1)}, bf16[2048,512]{1,0:T(8,128)(2,1)S(1)}, u32[]{:S(2)}, u32[]{:S(2)}) collective-permute-start(bf16[2048,512]{1,0:T(8,128)(2,1)} %bitcast.13), channel_id=1, source_target_pairs={{0,1},{1,0},{2,3},{3,2},{4,5},{5,4},{6,7},{7,6},{8,9},{9,8},{10,11... | collective-permute-start | bytes 6291464 | tf_op jit(solution)/shard_map/ppermute | solution.py:265
  1.4 2.7 %collective-permute-start.2 = (bf16[1,40,128]{2,1,0:T(8,128)(2,1)S(1)}, bf16[1,40,128]{2,1,0:T(8,128)(2,1)S(1)}, u32[]{:S(2)}, u32[]{:S(2)}) collective-permute-start(bf16[1,40,128]{2,1,0:T(8,128)(2,1)S(1)} %get-tuple-element.16), channel_id=1, source_target_pairs={{0,5},{1,4},{2,7},{3,6},{4,1},{5,0},{6,3},{7,2},{8,13},{9,12},{10,... | collective-permute-start | bytes 30728 | tf_op jit(solution)/shard_map/ppermute | solution.py:320
  4.1 0.1 collective-permute-start.1
  4.2 3.0 %shard_map.83 = (f32[16384,128]{1,0:T(8,128)S(1)}, bf16[4096,512]{1,0:T(8,128)(2,1)S(1)}, bf16[1,40,128]{2,1,0:T(8,128)(2,1)S(1)}) custom-call(bf16[2048,512]{1,0:T(8,128)(2,1)} %bitcast.14, f32[48,128]{1,0:T(8,128)S(1)} %get-tuple-element.13.param), custom_call_target="tpu_custom_call" | custom-call | flops 3000000000 | bytes 4194304 | tf_op jit(solution)/shard_map/pallas_call | solution.py:296
  7.1 0.0 collective-permute-done.2
  7.2 2.7 %collective-permute-start.3 = (bf16[2,40,128]{2,1,0:T(8,128)(2,1)S(1)}, bf16[2,40,128]{2,1,0:T(8,128)(2,1)S(1)}, u32[]{:S(2)}, u32[]{:S(2)}) collective-permute-start(bf16[2,40,128]{2,1,0:T(8,128)(2,1)S(1)} %pad_maximum_fusion.1), channel_id=1, source_target_pairs={{0,9},{1,8},{2,11},{3,10},{4,13},{5,12},{6,15},{7,14},{8,1},{9,0},... | collective-permute-start | bytes 61448 | tf_op jit(solution)/shard_map/ppermute | solution.py:320
  9.9 0.0 collective-permute-done.1.param
  9.9 0.0 collective-permute-done.s_rem
  9.9 3.6 %shard_map.84 = (f32[16384,128]{1,0:T(8,128)S(1)}, bf16[4096,512]{1,0:T(8,128)(2,1)S(1)}, bf16[1,40,128]{2,1,0:T(8,128)(2,1)S(1)}) custom-call(f32[16384,128]{1,0:T(8,128)S(1)} %get-tuple-element.14.held, bf16[4096,512]{1,0:T(8,128)(2,1)S(1)} %get-tuple-element.15.room, ...), custom_call_target="tpu_custom_call", output_to_operand_aliasing={{0}: (0, {}), {1}: (1, {})} | custom-call | flops 4000000000 | bytes 4194304 | tf_op jit(solution)/shard_map/pallas_call | solution.py:305
  13.5 0.0 collective-permute-done.3
  13.6 1.3 %collective-permute-start.4 = (bf16[4,40,128]{2,1,0:T(8,128)(2,1)S(1)}, bf16[4,40,128]{2,1,0:T(8,128)(2,1)S(1)}, u32[]{:S(2)}, u32[]{:S(2)}) collective-permute-start(bf16[4,40,128]{2,1,0:T(8,128)(2,1)S(1)} %pad_maximum_fusion.near), channel_id=1, source_target_pairs={{0,3},{1,2},{2,1},{3,0},{4,7},{5,6},{6,5},{7,4},{8,11},{9,10},{10,... | collective-permute-start | bytes 122888 | tf_op jit(solution)/shard_map/ppermute | solution.py:320
  14.8 0.0 copy-start
  14.8 0.0 copy-start.1
  14.8 2.6 %shard_map.85.psi_near = f32[512,512]{1,0:T(8,128)S(1)} custom-call(bf16[4096,512]{1,0:T(8,128)(2,1)S(1)} %get-tuple-element.18.basis, bf16[4,40,128]{2,1,0:T(8,128)(2,1)S(1)} %pad_maximum_fusion.near), custom_call_target="tpu_custom_call" | custom-call | flops 4000000000 | bytes 4194304 | tf_op jit(solution)/shard_map/pallas_call | solution.py:335
  17.5 0.0 collective-permute-done.4.far
  17.5 0.0 copy-done
  17.5 0.0 copy-done.1
  17.5 3.3 %shard_map.86 = f32[8,128]{1,0:T(8,128)S(1)} custom-call(bf16[4096,512]{1,0:T(8,128)(2,1)S(1)} %get-tuple-element.18.basis, f32[512,512]{1,0:T(8,128)S(1)} %shard_map.85.psi_near, bf16[4,40,128]{2,1,0:T(8,128)(2,1)S(1)} %pad_maximum_fusion.near, bf16[4,40,128]{2,1,0:T(8,128)(2,1)S(1)} %collective-permute-done.4.far, s32[1,64]{1,0:T(1,128)S(1)} %bitcast.11, ...), custom_call_target="tpu_custom_call" | custom-call | flops 4000000000 | bytes 4194304 | tf_op jit(solution)/shard_map/pallas_call | solution.py:344
  20.8 8.8 %all_to_all.12 = f32[8,1,128]{2,1,0:T(1,128)S(1)} all-to-all(f32[8,1,128]{2,1,0:T(1,128)S(1)} %bitcast.10), channel_id=1, replica_groups=mesh['grp'=2,'probe'=8,'beam'=2] {'probe'}, dimensions={0} | all-to-all | bytes 8192 | tf_op jit(solution)/shard_map/all_to_all | solution.py:353
  29.6 0.6 %copy.15 = f32[8,128]{1,0:T(8,128)} copy(f32[8,128]{1,0:T(8,128)S(1)} %bitcast.12) | data formatting | bytes 8192
  (4 shorter events, 0.0 us)
Async XLA Ops:
  0.9 9.0 %collective-permute-start = (bf16[2048,512]{1,0:T(8,128)(2,1)}, bf16[2048,512]{1,0:T(8,128)(2,1)S(1)}, u32[]{:S(2)}, u32[]{:S(2)}) collective-permute-start(bf16[2048,512]{1,0:T(8,128)(2,1)} %bitcast.13), channel_id=1, source_target_pairs={{0,1},{1,0},{2,3},{3,2},{4,5},{5,4},{6,7},{7,6},{8,9},{9,8},{10,11... | collective-permute-start | bytes 6291464 | tf_op jit(solution)/shard_map/ppermute | solution.py:265
  1.4 5.7 %collective-permute-start.2 = (bf16[1,40,128]{2,1,0:T(8,128)(2,1)S(1)}, bf16[1,40,128]{2,1,0:T(8,128)(2,1)S(1)}, u32[]{:S(2)}, u32[]{:S(2)}) collective-permute-start(bf16[1,40,128]{2,1,0:T(8,128)(2,1)S(1)} %get-tuple-element.16), channel_id=1, source_target_pairs={{0,5},{1,4},{2,7},{3,6},{4,1},{5,0},{6,3},{7,2},{8,13},{9,12},{10,... | collective-permute-start | bytes 30728 | tf_op jit(solution)/shard_map/ppermute | solution.py:320
  4.1 5.8 %collective-permute-start.1 = (f32[48,128]{1,0:T(8,128)S(1)}, f32[48,128]{1,0:T(8,128)S(1)}, u32[]{:S(2)}, u32[]{:S(2)}) collective-permute-start(f32[48,128]{1,0:T(8,128)S(1)} %get-tuple-element.13.param), channel_id=1, source_target_pairs={{0,1},{1,0},{2,3},{3,2},{4,5},{5,4},{6,7},{7,6},{8,9},{9,8},{10,11... | collective-permute-start | bytes 73736 | tf_op jit(solution)/shard_map/ppermute | solution.py:265
  7.2 6.4 %collective-permute-start.3 = (bf16[2,40,128]{2,1,0:T(8,128)(2,1)S(1)}, bf16[2,40,128]{2,1,0:T(8,128)(2,1)S(1)}, u32[]{:S(2)}, u32[]{:S(2)}) collective-permute-start(bf16[2,40,128]{2,1,0:T(8,128)(2,1)S(1)} %pad_maximum_fusion.1), channel_id=1, source_target_pairs={{0,9},{1,8},{2,11},{3,10},{4,13},{5,12},{6,15},{7,14},{8,1},{9,0},... | collective-permute-start | bytes 61448 | tf_op jit(solution)/shard_map/ppermute | solution.py:320
  13.6 3.9 %collective-permute-start.4 = (bf16[4,40,128]{2,1,0:T(8,128)(2,1)S(1)}, bf16[4,40,128]{2,1,0:T(8,128)(2,1)S(1)}, u32[]{:S(2)}, u32[]{:S(2)}) collective-permute-start(bf16[4,40,128]{2,1,0:T(8,128)(2,1)S(1)} %pad_maximum_fusion.near), channel_id=1, source_target_pairs={{0,3},{1,2},{2,1},{3,0},{4,7},{5,6},{6,5},{7,4},{8,11},{9,10},{10,... | collective-permute-start | bytes 122888 | tf_op jit(solution)/shard_map/ppermute | solution.py:320
  14.8 2.7 %copy-start = (s32[64]{0:T(128)S(1)}, s32[64]{0:T(128)}, u32[]{:S(2)}) copy-start(s32[64]{0:T(128)} %param.14) | copy-start | bytes 772
  14.8 2.7 %copy-start.1 = (f32[2,128,128]{2,1,0:T(8,128)S(1)}, f32[2,128,128]{2,1,0:T(8,128)}, u32[]{:S(2)}) copy-start(f32[2,128,128]{2,1,0:T(8,128)} %constant.2.clone.overlap) | copy-start | bytes 393220

commit v9 on v8

--- a/solution.py
+++ b/solution.py
@@ -50,7 +50,7 @@
     pats = pat_v[...].astype(f32)
     pos = jnp.concatenate([pos_v[:, :LANE], pos_v[:, LANE:]], 0)
     tiles = [pats[:, t * LANE : (t + 1) * LANE] for t in range(pats.shape[1] // LANE)]
-    split = [(pos // 32).astype(f32), (pos % 32).astype(f32)]
+    split = [(pos // 32).astype(f32), (pos % 32).astype(f32), jnp.zeros((8, LANE), f32)]
     message = jnp.concatenate(tiles + [jnp.concatenate(split, 0)], 0)
     small[0] = message.astype(bf16)
     lines = amp_v.shape[0]
@@ -156,7 +156,7 @@
     step = coef.shape[0]
 
     def tables(i):
-        pos = source[j + i].astype(f32)[32:40].astype(jnp.int32)
+        pos = source[j + i, 32:48, :].astype(f32).astype(jnp.int32)
         pos = 32 * pos[0:4] + pos[4:8]
         pos = jnp.where(half == 0, pos[0:2], pos[2:4])
         px, py = pos[0:1], pos[1:2]
@@ -208,7 +208,7 @@
         for n, source in enumerate((near, far)):
             for j in range(blocks):
                 owner = column ^ masks[n * blocks + j]
-                pats = source[j].astype(f32)
+                pats = source[j, 0:32, :].astype(f32)
                 for t in range(4):
                     pots[pl.ds(pl.multiple_of(owner * 8, 8), 8), t * LANE : (t + 1) * LANE] = pats[8 * t : 8 * t + 8]
         mine = (cols[...] == column).astype(f32)
@@ -268,7 +268,7 @@
     params = pltpu.CompilerParams(vmem_limit_bytes=24 * 1024 * 1024)
     cost = lambda n: pl.CostEstimate(flops=n, bytes_accessed=4 * 2**20, transcendentals=0)
 
-    message = sds((1, 40, LANE), bf16)
+    message = sds((1, 48, LANE), bf16)
     s_own = smatrix.reshape(rows, width)
     raw = (aperture.reshape(lines, LANE), aberration.reshape(lines, LANE), beam_k, probe_pos, patches)
     small, param = pl.pallas_call(

time: 30.5 us -> 30.6 us (level)
  transfers between devices with their start and end apart: 5 -> 5, of which waited for: 0 -> 0; matrix products, arithmetic and copies ran while one was open for 0% -> 0% of each run, Pallas kernels for 31% -> 30%
where the time goes in v9:
time: 30.6 us; the launch traced here: 30.3 us
  Pallas kernels  13.3 us (43%)
  blocking collectives  8.99 us (29%)
  starting transfers between devices  7.24 us (24%)
  local copies, waits for them, and re-layouts  0.6 us (2%)
    all_to_all x1, blocking collectives, shards(): return lax.all_to_all(energy, 'probe', 0, 0, tiled=True)  8.99 us
    ppermute x3, starting transfers between devices, shards(): lax.ppermute(small, ('probe', 'beam'), [(2 * i + b, 2 * (i ^ reach) + 1 -...  6.66 us
    pallas_call x1, Pallas kernels, shards(): pl.pallas_call(other_kernel, out_shape=(held_shape, basis_shape, message)...  3.64 us
    pallas_call x1, Pallas kernels, shards(): pl.pallas_call(functools.partial(far_kernel, tuple(masks)), out_shape=jax...  3.24 us
    pallas_call x1, Pallas kernels, shards(): pl.pallas_call(own_kernel, out_shape=(held_shape, basis_shape, message),...  2.96 us
    pallas_call x1, Pallas kernels, shards(): pl.pallas_call(near_kernel, out_shape=sds((probes, width), f32), in_specs...  2.63 us
    pallas_call x1, Pallas kernels, shards(): pl.pallas_call(pack_kernel, out_shape=(message, sds((3 * lines, LANE), f3...  0.86 us
  transfers between devices with their start and end apart: 5, of which 0 were waited for; matrix products, arithmetic and copies ran while one was open for 0% of the time, Pallas kernels for 30%

profile of v9, /device:TPU:0, one launch (start us, length us, event | category | flops | bytes accessed | tf_op | source)
XLA Modules:
  0.0 30.3 jit_solution(12680050008004584870)
XLA Ops:
  0.0 0.9 %shard_map.82 = (bf16[1,48,128]{2,1,0:T(8,128)(2,1)S(1)}, f32[48,128]{1,0:T(8,128)S(1)}) custom-call(f32[16,128]{1,0:T(8,128)} %bitcast.15, f32[16,128]{1,0:T(8,128)} %bitcast.16, s32[2,2048]{1,0:T(2,128)} %k_hbm.1, s32[2,256]{1,0:T(2,128)} %pos_hbm.1, bf16[8,512]{1,0:T(8,128)(2,1)} %patches.1), custom_call_target="tpu_custom_call" | custom-call | flops 1000000000 | bytes 4194304 | tf_op jit(solution)/shard_map/pallas_call | solution.py:274
  0.9 0.5 %collective-permute-start = (bf16[2048,512]{1,0:T(8,128)(2,1)}, bf16[2048,512]{1,0:T(8,128)(2,1)S(1)}, u32[]{:S(2)}, u32[]{:S(2)}) collective-permute-start(bf16[2048,512]{1,0:T(8,128)(2,1)} %bitcast.13), channel_id=1, source_target_pairs={{0,1},{1,0},{2,3},{3,2},{4,5},{5,4},{6,7},{7,6},{8,9},{9,8},{10,11... | collective-permute-start | bytes 6291464 | tf_op jit(solution)/shard_map/ppermute | solution.py:265
  1.4 2.7 %collective-permute-start.2 = (bf16[1,48,128]{2,1,0:T(8,128)(2,1)S(1)}, bf16[1,48,128]{2,1,0:T(8,128)(2,1)S(1)}, u32[]{:S(2)}, u32[]{:S(2)}) collective-permute-start(bf16[1,48,128]{2,1,0:T(8,128)(2,1)S(1)} %get-tuple-element.16), channel_id=1, source_target_pairs={{0,5},{1,4},{2,7},{3,6},{4,1},{5,0},{6,3},{7,2},{8,13},{9,12},{10,... | collective-permute-start | bytes 36872 | tf_op jit(solution)/shard_map/ppermute | solution.py:320
  4.1 0.1 collective-permute-start.1
  4.2 3.0 %shard_map.83 = (f32[16384,128]{1,0:T(8,128)S(1)}, bf16[4096,512]{1,0:T(8,128)(2,1)S(1)}, bf16[1,48,128]{2,1,0:T(8,128)(2,1)S(1)}) custom-call(bf16[2048,512]{1,0:T(8,128)(2,1)} %bitcast.14, f32[48,128]{1,0:T(8,128)S(1)} %get-tuple-element.13.param), custom_call_target="tpu_custom_call" | custom-call | flops 3000000000 | bytes 4194304 | tf_op jit(solution)/shard_map/pallas_call | solution.py:296
  7.1 0.0 collective-permute-done.2
  7.2 2.7 %collective-permute-start.3 = (bf16[2,48,128]{2,1,0:T(8,128)(2,1)S(1)}, bf16[2,48,128]{2,1,0:T(8,128)(2,1)S(1)}, u32[]{:S(2)}, u32[]{:S(2)}) collective-permute-start(bf16[2,48,128]{2,1,0:T(8,128)(2,1)S(1)} %pad_maximum_fusion.1), channel_id=1, source_target_pairs={{0,9},{1,8},{2,11},{3,10},{4,13},{5,12},{6,15},{7,14},{8,1},{9,0},... | collective-permute-start | bytes 73736 | tf_op jit(solution)/shard_map/ppermute | solution.py:320
  9.9 0.0 collective-permute-done.1.param
  9.9 0.0 collective-permute-done.s_rem
  9.9 3.6 %shard_map.84 = (f32[16384,128]{1,0:T(8,128)S(1)}, bf16[4096,512]{1,0:T(8,128)(2,1)S(1)}, bf16[1,48,128]{2,1,0:T(8,128)(2,1)S(1)}) custom-call(f32[16384,128]{1,0:T(8,128)S(1)} %get-tuple-element.14.held, bf16[4096,512]{1,0:T(8,128)(2,1)S(1)} %get-tuple-element.15.room, ...), custom_call_target="tpu_custom_call", output_to_operand_aliasing={{0}: (0, {}), {1}: (1, {})} | custom-call | flops 4000000000 | bytes 4194304 | tf_op jit(solution)/shard_map/pallas_call | solution.py:305
  13.5 0.0 collective-permute-done.3
  13.6 1.3 %collective-permute-start.4 = (bf16[4,48,128]{2,1,0:T(8,128)(2,1)S(1)}, bf16[4,48,128]{2,1,0:T(8,128)(2,1)S(1)}, u32[]{:S(2)}, u32[]{:S(2)}) collective-permute-start(bf16[4,48,128]{2,1,0:T(8,128)(2,1)S(1)} %pad_maximum_fusion.near), channel_id=1, source_target_pairs={{0,3},{1,2},{2,1},{3,0},{4,7},{5,6},{6,5},{7,4},{8,11},{9,10},{10,... | collective-permute-start | bytes 147464 | tf_op jit(solution)/shard_map/ppermute | solution.py:320
  14.8 0.0 copy-start
  14.8 0.0 copy-start.1
  14.8 2.6 %shard_map.85.psi_near = f32[512,512]{1,0:T(8,128)S(1)} custom-call(bf16[4096,512]{1,0:T(8,128)(2,1)S(1)} %get-tuple-element.18.basis, bf16[4,48,128]{2,1,0:T(8,128)(2,1)S(1)} %pad_maximum_fusion.near), custom_call_target="tpu_custom_call" | custom-call | flops 4000000000 | bytes 4194304 | tf_op jit(solution)/shard_map/pallas_call | solution.py:335
  17.5 0.0 collective-permute-done.4.far
  17.5 0.0 copy-done
  17.5 0.0 copy-done.1
  17.5 3.2 %shard_map.86 = f32[8,128]{1,0:T(8,128)S(1)} custom-call(bf16[4096,512]{1,0:T(8,128)(2,1)S(1)} %get-tuple-element.18.basis, f32[512,512]{1,0:T(8,128)S(1)} %shard_map.85.psi_near, bf16[4,48,128]{2,1,0:T(8,128)(2,1)S(1)} %pad_maximum_fusion.near, bf16[4,48,128]{2,1,0:T(8,128)(2,1)S(1)} %collective-permute-done.4.far, s32[1,64]{1,0:T(1,128)S(1)} %bitcast.11, ...), custom_call_target="tpu_custom_call" | custom-call | flops 4000000000 | bytes 4194304 | tf_op jit(solution)/shard_map/pallas_call | solution.py:344
  20.7 9.0 %all_to_all.12 = f32[8,1,128]{2,1,0:T(1,128)S(1)} all-to-all(f32[8,1,128]{2,1,0:T(1,128)S(1)} %bitcast.10), channel_id=1, replica_groups=mesh['grp'=2,'probe'=8,'beam'=2] {'probe'}, dimensions={0} | all-to-all | bytes 8192 | tf_op jit(solution)/shard_map/all_to_all | solution.py:353
  29.7 0.6 %copy.15 = f32[8,128]{1,0:T(8,128)} copy(f32[8,128]{1,0:T(8,128)S(1)} %bitcast.12) | data formatting | bytes 8192
  (4 shorter events, 0.0 us)
Async XLA Ops:
  0.9 9.0 %collective-permute-start = (bf16[2048,512]{1,0:T(8,128)(2,1)}, bf16[2048,512]{1,0:T(8,128)(2,1)S(1)}, u32[]{:S(2)}, u32[]{:S(2)}) collective-permute-start(bf16[2048,512]{1,0:T(8,128)(2,1)} %bitcast.13), channel_id=1, source_target_pairs={{0,1},{1,0},{2,3},{3,2},{4,5},{5,4},{6,7},{7,6},{8,9},{9,8},{10,11... | collective-permute-start | bytes 6291464 | tf_op jit(solution)/shard_map/ppermute | solution.py:265
  1.4 5.7 %collective-permute-start.2 = (bf16[1,48,128]{2,1,0:T(8,128)(2,1)S(1)}, bf16[1,48,128]{2,1,0:T(8,128)(2,1)S(1)}, u32[]{:S(2)}, u32[]{:S(2)}) collective-permute-start(bf16[1,48,128]{2,1,0:T(8,128)(2,1)S(1)} %get-tuple-element.16), channel_id=1, source_target_pairs={{0,5},{1,4},{2,7},{3,6},{4,1},{5,0},{6,3},{7,2},{8,13},{9,12},{10,... | collective-permute-start | bytes 36872 | tf_op jit(solution)/shard_map/ppermute | solution.py:320
  4.1 5.8 %collective-permute-start.1 = (f32[48,128]{1,0:T(8,128)S(1)}, f32[48,128]{1,0:T(8,128)S(1)}, u32[]{:S(2)}, u32[]{:S(2)}) collective-permute-start(f32[48,128]{1,0:T(8,128)S(1)} %get-tuple-element.13.param), channel_id=1, source_target_pairs={{0,1},{1,0},{2,3},{3,2},{4,5},{5,4},{6,7},{7,6},{8,9},{9,8},{10,11... | collective-permute-start | bytes 73736 | tf_op jit(solution)/shard_map/ppermute | solution.py:265
  7.2 6.4 %collective-permute-start.3 = (bf16[2,48,128]{2,1,0:T(8,128)(2,1)S(1)}, bf16[2,48,128]{2,1,0:T(8,128)(2,1)S(1)}, u32[]{:S(2)}, u32[]{:S(2)}) collective-permute-start(bf16[2,48,128]{2,1,0:T(8,128)(2,1)S(1)} %pad_maximum_fusion.1), channel_id=1, source_target_pairs={{0,9},{1,8},{2,11},{3,10},{4,13},{5,12},{6,15},{7,14},{8,1},{9,0},... | collective-permute-start | bytes 73736 | tf_op jit(solution)/shard_map/ppermute | solution.py:320
  13.6 3.9 %collective-permute-start.4 = (bf16[4,48,128]{2,1,0:T(8,128)(2,1)S(1)}, bf16[4,48,128]{2,1,0:T(8,128)(2,1)S(1)}, u32[]{:S(2)}, u32[]{:S(2)}) collective-permute-start(bf16[4,48,128]{2,1,0:T(8,128)(2,1)S(1)} %pad_maximum_fusion.near), channel_id=1, source_target_pairs={{0,3},{1,2},{2,1},{3,0},{4,7},{5,6},{6,5},{7,4},{8,11},{9,10},{10,... | collective-permute-start | bytes 147464 | tf_op jit(solution)/shard_map/ppermute | solution.py:320
  14.8 2.7 %copy-start = (s32[64]{0:T(128)S(1)}, s32[64]{0:T(128)}, u32[]{:S(2)}) copy-start(s32[64]{0:T(128)} %param.14) | copy-start | bytes 772
  14.8 2.7 %copy-start.1 = (f32[2,128,128]{2,1,0:T(8,128)S(1)}, f32[2,128,128]{2,1,0:T(8,128)}, u32[]{:S(2)}) copy-start(f32[2,128,128]{2,1,0:T(8,128)} %constant.2.clone.overlap) | copy-start | bytes 393220
